TPU v7x, 1024 devices: a whole 8x8x8 slice. The times are simulated.
1024 devices in a mesh: dp: 16 (over z_lo, x), mp: 64 (over z_hi, y, core).
Axes of the slice: x: 8, y: 8, z: 8 (z_hi: 4, z_lo: 2; z = z_hi * 2 + z_lo), core: 2. Of those that a mesh axis runs over, the one named last changes fastest.
Arguments:
- upstream: bfloat16 [2048, 6144], P(('dp', 'mp')), may hold values from -6 to 6
- pre_act: bfloat16 [2048, 12288], P('dp', 'mp'), may hold values from -6 to 6
- w_down: bfloat16 [12288, 6144], P('mp'), may hold values from -0.078125 to 0.078125
- first_moment: float32 [12288, 6144], P(('mp', 'dp')), may hold values from -6 to 6
- second_moment: float32 [12288, 6144], P(('mp', 'dp')), may hold values from 1 to 16
- signs: int32 [6144], replicated, may hold values from 0 to 1
- exponents: int32 [12288, 6], P('mp'), may hold values from -6 to -1
Outputs:
- pre_grad: bfloat16 [2048, 12288], P('dp', 'mp')
- grad_mean: float32 [12288, 6144], P(('mp', 'dp'))
- first_new: float32 [12288, 6144], P(('mp', 'dp'))
- second_new: float32 [12288, 6144], P(('mp', 'dp'))
- weight_new: bfloat16 [12288, 6144], P('mp')
Inputs may be any that keep to these rules, and one draw needn't show every extreme that they name: `signs`: 1 turns a column's sign over. `exponents`: equal for every replica.
All inputs are finite; a program needn't handle non-finite values.
Results may differ from a plain program's by a relative error of at most 0.017.
Values may be sent and summed in bfloat16 or wider, within the bound.
No kernel may reach another device: no remote copies, remote signals or barrier semaphores. Data moves between devices by JAX's collectives and lax.ppermute only.
A program may use at most 64 MiB of HBM per device.

v0:
```python
import jax
import jax.numpy as jnp
from jax import lax
from jax.sharding import PartitionSpec as P

hadamard_norm = 0.03125
clip_limit = 448.0
root_half = 0.7071067811865476
density_norm = 0.3989422804014327


def hadamard_table(table_order):
    indices = jnp.arange(table_order, dtype=jnp.int32)
    common = indices[:, None] & indices[None, :]
    parity = jnp.zeros((table_order, table_order), jnp.int32)
    for position in range(table_order.bit_length() - 1):
        parity = parity + (common >> position & 1)
    return (1 - 2 * (parity % 2)).astype(jnp.float32)


def rotate(values):
    leading = values.shape[:-1]
    shaped = values.reshape(leading + (2, 2, 2, 128))
    for section_axis in (-4, -3, -2):
        first = lax.index_in_dim(shaped, 0, shaped.ndim + section_axis, keepdims=False)
        second = lax.index_in_dim(shaped, 1, shaped.ndim + section_axis, keepdims=False)
        shaped = jnp.stack((first + second, first - second), axis=shaped.ndim + section_axis)
    mixed = jnp.einsum(
        "...q,qp->...p", shaped, hadamard_table(128), precision=lax.Precision.HIGHEST
    )
    return (mixed * hadamard_norm).reshape(values.shape)


def encode(gradient, multiplier, sign_vector):
    row_count = gradient.shape[0]
    blocks = sign_vector.shape[0]
    shaped = gradient.reshape(row_count, blocks, 1024) * sign_vector[None]
    turned = rotate(shaped) * multiplier[:, :, None]
    return jnp.clip(turned, -clip_limit, clip_limit).reshape(gradient.shape)


def transpose_product(left, right):
    return lax.dot_general(
        left, right, (((0,), (0,)), ((), ())), preferred_element_type=jnp.float32
    )


def feature_product(left, right):
    return lax.dot_general(
        left, right, (((1,), (1,)), ((), ())), preferred_element_type=jnp.float32
    )


def body(upstream, pre_act, w_down, first_moment, second_moment, signs, exponents):
    preact = pre_act.astype(jnp.float32)
    normal_cdf = 0.5 * (1.0 + lax.erf(preact * root_half))
    hidden = (preact * normal_cdf).astype(jnp.bfloat16)
    derivative = normal_cdf + preact * jnp.exp(-0.5 * preact * preact) * density_norm
    local_rows = w_down.shape[0]
    columns = w_down.shape[1]
    blocks = columns // 1024
    sign_vector = (1 - 2 * signs).astype(jnp.float32).reshape(blocks, 1024)
    scale_power = exponents.astype(jnp.float32)
    shrink = jnp.exp2(-scale_power)
    replicas = lax.axis_size("dp")
    own_count = local_rows // replicas
    gathered = lax.all_gather(upstream, "mp", axis=0, tiled=True)
    hidden_grad = feature_product(gathered, w_down)
    gradient = transpose_product(hidden, gathered)
    summed = lax.psum_scatter(
        encode(gradient, shrink, sign_vector).astype(jnp.bfloat16),
        "dp",
        scatter_dimension=0,
        tiled=True,
    ).astype(jnp.float32)
    pre_grad = (hidden_grad * derivative).astype(jnp.bfloat16)
    offset = lax.axis_index("dp") * own_count
    own_power = lax.dynamic_slice_in_dim(scale_power, offset, own_count, 0)
    grown = summed.reshape(own_count, blocks, 1024) * jnp.exp2(own_power)[:, :, None]
    grad_mean = (rotate(grown) * sign_vector[None]).reshape(own_count, columns) / replicas
    first_new = 0.9 * first_moment + 0.1 * grad_mean
    second_new = 0.95 * second_moment + 0.05 * grad_mean * grad_mean
    adjusted = first_new / 0.6513215599 / (jnp.sqrt(second_new / 0.4012630608) + 1e-08)
    own_weight = lax.dynamic_slice_in_dim(w_down, offset, own_count, 0).astype(jnp.float32)
    weight_shard = (own_weight * (1.0 - 0.01 * 0.1) - 0.01 * adjusted).astype(jnp.bfloat16)
    weight_new = lax.all_gather(weight_shard, "dp", axis=0, tiled=True)
    return (pre_grad, grad_mean, first_new, second_new, weight_new)


def solution(mesh):
    placed = (
        P(("dp", "mp"), None),
        P("dp", "mp"),
        P("mp", None),
        P(("mp", "dp"), None),
        P(("mp", "dp"), None),
        P(),
        P("mp", None),
    )
    return jax.shard_map(
        body,
        mesh=mesh,
        in_specs=placed,
        out_specs=(
            P("dp", "mp"),
            P(("mp", "dp"), None),
            P(("mp", "dp"), None),
            P(("mp", "dp"), None),
            P("mp", None),
        ),
        check_vma=False,
    )
```

profile of v0, /device:TPU:16, one launch (start us, length us, event | category | flops | bytes accessed | tf_op | source)
XLA Modules:
  0.0 334.2 jit_solution(3871521424702217893)
XLA Ops:
  7.2 0.7 all-gather.5.cloned.1.call-update
  7.9 0.7 multiply_exponential_fusion
  8.8 0.5 mul.162
  9.3 6.2 %copy.28 = f32[24,8,6,1024]{3,1,2,0:T(8,128)} copy(f32[24,8,6,1024]{3,2,1,0:T(8,128)S(1)} %bitcast.18) | data formatting | bytes 9437184
  15.5 99.0 %all-gather.5.cloned.1.call-done = bf16[64,2,6144]{2,1,0:T(2,128)(2,1)} async-done(((bf16[1,2,6144]{2,1,0:T(2,128)(2,1)}), bf16[64,2,6144]{2,1,0:T(2,128)(2,1)}) %all-gather.5.cloned.1.call-update) | async-done | bytes 1572880 | tf_op jit(solution)/shard_map/all_gather | solution.py:67
  114.4 3.6 %reshape.49 = bf16[128,6144]{1,0:T(8,128)(2,1)S(1)} reshape(bf16[64,2,6144]{2,1,0:T(2,128)(2,1)} %all-gather.5.cloned.1.call-done) | data formatting | bytes 3145728
  118.0 3.0 fusion.38
  121.0 7.1 %reshape.41 = f32[192,6,2,2,2,128]{5,4,3,2,1,0:T(2,128)} reshape(f32[192,6144]{1,0:T(8,128)} %fusion.38) | data formatting | bytes 9437184 | tf_op jit(solution)/shard_map/reshape | solution.py:37
  128.1 3.8 %copy_multiply_fusion = f32[192,6,2,2,2,128]{5,0,4,3,2,1:T(8,128)S(1)} fusion(f32[192,6,2,2,2,128]{5,4,3,2,1,0:T(2,128)} %reshape.41, f32[6,2,2,2,128]{4,3,2,1,0:T(2,128)S(1)} %bitcast.20), kind=kLoop, calls=%fused_computation.8 | loop fusion | flops 1179648 | bytes 9461760 | tf_op jit(solution)/shard_map/mul | solution.py:37
  131.9 0.5 slice_add_fusion
  132.4 0.6 fusion.10
  133.0 0.7 fusion.12
  133.7 4.1 %broadcast_multiply_fusion = f32[192,6,2,2,2,128]{5,0,4,3,2,1:T(8,128)S(1)} fusion(f32[192,6,2,2,1,128]{5,0,4,3,2,1:T(8,128)S(1)} %get-tuple-element.10, f32[192,6,2,2,1,128]{5,0,4,3,2,1:T(8,128)S(1)} %get-tuple-element.9), kind=kOutput, calls=%fused_computation.14 | convolution fusion | flops 1814872064 | bytes 9437184 | tf_op jit(solution)/shard_map/...q,qp->...p/dot_general | solution.py:28
  137.8 5.9 %copy.22 = f32[192,6,2,2,2,128]{5,4,3,2,1,0:T(2,128)} copy(f32[192,6,2,2,2,128]{5,0,4,3,2,1:T(8,128)S(1)} %broadcast_multiply_fusion) | data formatting | bytes 9437184 | tf_op jit(solution)/shard_map/mul | solution.py:31
  143.7 7.0 %reshape.42 = f32[192,6144]{1,0:T(8,128)} reshape(f32[192,6,2,2,2,128]{5,4,3,2,1,0:T(2,128)} %copy.22) | data formatting | bytes 9437184 | tf_op jit(solution)/shard_map/reshape | solution.py:31
  150.7 5.9 %clamp_convert_fusion = bf16[192,6144]{1,0:T(8,128)(2,1)} fusion(f32[192,6144]{1,0:T(8,128)} %reshape.42, f32[192,6144]{1,0:T(8,128)} %bitcast.19), kind=kLoop, calls=%fused_computation.9 | loop fusion | flops 3538944 | bytes 11796480 | tf_op jit(solution)/shard_map/convert_element_type | solution.py:71
  156.6 48.0 %fusion = bf16[16,6144]{1,0:T(8,128)(2,1)S(1)} fusion(bf16[192,6144]{1,0:T(8,128)(2,1)} %clamp_convert_fusion), kind=kCustom, calls=%all-reduce-scatter | all-reduce-scatter fusion | flops 1572865 | bytes 2560000
  204.7 1.3 collective-permute-start.2
  206.0 2.6 collective-permute-start.1
  208.6 3.4 %collective-permute-start = (bf16[16,6144]{1,0:T(8,128)(2,1)S(1)}, bf16[16,6144]{1,0:T(8,128)(2,1)}, u32[]{:S(2)}, u32[]{:S(2)}) collective-permute-start(bf16[16,6144]{1,0:T(8,128)(2,1)S(1)} %fusion), channel_id=1, source_target_pairs={{0,64},{64,128},{128,192},{192,256},{256,320},{320,384},{384,448},... | collective-permute-start | bytes 589832
  212.0 6.9 %collective-permute-start.3 = (bf16[12,6144]{1,0:T(8,128)(2,1)S(1)}, bf16[12,6144]{1,0:T(8,128)(2,1)S(1)}, u32[]{:S(2)}, u32[]{:S(2)}) collective-permute-start(bf16[12,6144]{1,0:T(8,128)(2,1)S(1)} %slice.60), channel_id=1, source_target_pairs={{0,256},{64,320},{128,384},{192,448},{256,512},{320,576},{384,640}... | collective-permute-start | bytes 442376
  219.2 1.3 dynamic-slice.4
  221.1 12.0 %collective-permute-done.3 = bf16[12,6144]{1,0:T(8,128)(2,1)S(1)} collective-permute-done((bf16[12,6144]{1,0:T(8,128)(2,1)S(1)}, bf16[12,6144]{1,0:T(8,128)(2,1)S(1)}, u32[]{:S(2)}, u32[]{:S(2)}) %collective-permute-start.3) | collective-permute-done | bytes 147488
  233.1 0.7 copy-done.3
  233.8 5.2 %concatenate = bf16[76,6144]{1,0:T(8,128)(2,1)S(1)} concatenate(bf16[12,6144]{1,0:T(8,128)(2,1)} %copy-done.3, bf16[16,6144]{1,0:T(8,128)(2,1)S(1)} %collective-permute-done.2, bf16[16,6144]{1,0:T(8,128)(2,1)S(1)} %collective-permute-done.1, bf16[16,6144]{1,0:T(8,128)(2,1)} %collective-permute-done, bf16[16,6144]{1,0:T(8,128)(2,1)S(1)} %fusion), dimensions={0} | concatenate | bytes 1867776
  239.1 0.2 reshape.47
  239.6 0.6 convolution_multiply_fusion
  240.4 0.2 reshape.45
  240.7 2.3 fusion.19
  243.0 3.1 fusion.9
  246.0 77.1 %all-gather.7.cloned.1.call-done = bf16[16,12,6144]{2,1,0:T(8,128)(2,1)} async-done(((bf16[1,12,6144]{2,1,0:T(8,128)(2,1)}), bf16[16,12,6144]{2,1,0:T(8,128)(2,1)}) %all-gather.7.cloned.1.call-update) | async-done | bytes 2359312 | tf_op jit(solution)/shard_map/all_gather | solution.py:86
  323.2 4.2 %reshape.51 = bf16[192,6144]{1,0:T(8,128)(2,1)} reshape(bf16[16,12,6144]{2,1,0:T(8,128)(2,1)} %all-gather.7.cloned.1.call-done) | data formatting | bytes 4718592
  (29 shorter events, 0.9 us)
Async XLA Ops:
  7.2 107.3 %all-gather.5.cloned.1.call-start = ((), (), s32[]{:S(2)}) async-start(), calls=%async_computation | async-start | bytes 1597440 | tf_op jit(solution)/shard_map/all_gather | solution.py:67
  7.9 315.3 %all-gather.7.cloned.1.call-start = ((), (), s32[]{:S(2)}) async-start(), calls=%async_computation.1 | async-start | bytes 3342336 | tf_op jit(solution)/shard_map/all_gather | solution.py:86
  9.3 6.2 %copy-start.5 = (s32[6144]{0:T(1024)S(1)}, s32[6144]{0:T(1024)}, u32[]{:S(2)}) copy-start(s32[6144]{0:T(1024)} %param.12) | copy-start | bytes 73732
  15.5 102.5 %copy-start.2 = (bf16[128,192]{0,1:T(8,128)(2,1)S(1)}, bf16[128,192]{0,1:T(8,128)(2,1)}, u32[]{:S(2)}) copy-start(bf16[128,192]{0,1:T(8,128)(2,1)} %param.8) | copy-start | bytes 147460
  156.6 62.3 %copy-start.4 = (s32[192,6]{0,1:T(8,128)S(1)}, s32[192,6]{0,1:T(8,128)}, u32[]{:S(2)}) copy-start(s32[192,6]{0,1:T(8,128)} %param.13) | copy-start | bytes 13828
  204.7 28.4 %collective-permute-start.2 = (bf16[16,6144]{1,0:T(8,128)(2,1)S(1)}, bf16[16,6144]{1,0:T(8,128)(2,1)S(1)}, u32[]{:S(2)}, u32[]{:S(2)}) collective-permute-start(bf16[16,6144]{1,0:T(8,128)(2,1)S(1)} %fusion), channel_id=1, source_target_pairs={{0,192},{64,256},{128,320},{192,384},{256,448},{320,512},{384,576}... | collective-permute-start | bytes 589832
  206.0 27.1 %collective-permute-start.1 = (bf16[16,6144]{1,0:T(8,128)(2,1)S(1)}, bf16[16,6144]{1,0:T(8,128)(2,1)S(1)}, u32[]{:S(2)}, u32[]{:S(2)}) collective-permute-start(bf16[16,6144]{1,0:T(8,128)(2,1)S(1)} %fusion), channel_id=1, source_target_pairs={{0,128},{64,192},{128,256},{192,320},{256,384},{320,448},{384,512}... | collective-permute-start | bytes 589832
  208.6 25.2 %collective-permute-start = (bf16[16,6144]{1,0:T(8,128)(2,1)S(1)}, bf16[16,6144]{1,0:T(8,128)(2,1)}, u32[]{:S(2)}, u32[]{:S(2)}) collective-permute-start(bf16[16,6144]{1,0:T(8,128)(2,1)S(1)} %fusion), channel_id=1, source_target_pairs={{0,64},{64,128},{128,192},{192,256},{256,320},{320,384},{384,448},... | collective-permute-start | bytes 589832
  212.0 21.1 %collective-permute-start.3 = (bf16[12,6144]{1,0:T(8,128)(2,1)S(1)}, bf16[12,6144]{1,0:T(8,128)(2,1)S(1)}, u32[]{:S(2)}, u32[]{:S(2)}) collective-permute-start(bf16[12,6144]{1,0:T(8,128)(2,1)S(1)} %slice.60), channel_id=1, source_target_pairs={{0,256},{64,320},{128,384},{192,448},{256,512},{320,576},{384,640}... | collective-permute-start | bytes 442376
  233.1 0.7 copy-start.3
  239.5 1.2 copy-start
  239.5 1.2 copy-start.1
Sparse Core Ops, SparseCore 0:
  12.5 101.9 all-gather.4
  243.1 80.0 all-gather.6
where the time goes:
time: 335 us; the launch traced here: 334 us
  waiting for transfers between devices  189 us (56%)
  blocking collectives  48 us (14%)
  local copies, waits for them, and re-layouts  42.6 us (13%)
  other arithmetic  14.9 us (4%)
  between operations  14.9 us (4%)
  starting transfers between devices  14.3 us (4%)
  matrix products  10.7 us (3%)
    all_gather x1, waiting for transfers between devices, body(): gathered = lax.all_gather(upstream, 'mp', axis=0, tiled=True)  99 us
    all_gather x1, waiting for transfers between devices, body(): weight_new = lax.all_gather(weight_shard, 'dp', axis=0, tiled=True)  77.1 us
    unnamed x1, blocking collectives  48 us
    unnamed x18, local copies, waits for them, and re-layouts  21.2 us
    unnamed x4, starting transfers between devices  14.2 us
    unnamed x6, waiting for transfers between devices  12.7 us
    reshape x2, local copies, waits for them, and re-layouts, rotate(): return (mixed * hadamard_norm).reshape(values.shape)  7.26 us
    reshape x1, local copies, waits for them, and re-layouts, encode(): shaped = gradient.reshape(row_count, blocks, 1024) * sign_vector[None]  7.1 us
  transfers between devices with their start and end apart: 6, of which 3 were waited for; matrix products, arithmetic and copies ran while one was open for 4% of the time, Pallas kernels for 0%

commit v1 on v0

v1 whole, which is shorter than its diff:
```python
import jax
import jax.numpy as jnp
import numpy as np
from jax import lax
from jax.experimental import pallas as pl
from jax.experimental.pallas import tpu as pltpu
from jax.sharding import Mesh
from jax.sharding import PartitionSpec as P

hadamard_norm = 0.03125
clip_limit = 448.0
root_half = 0.7071067811865476
density_norm = 0.3989422804014327

REPLICAS = 16
ROWS = 192
OWN = 12
COLS = 6144
SEGS = 4
SEG = 1536
BLOCKS = 6
TOK = 128
PEERS = 32
LANES = 128
VMEM = 48 * 1024 * 1024
bf16 = jnp.bfloat16
f32 = jnp.float32


def hadamard(order):
    indices = np.arange(order)
    common = indices[:, None] & indices[None, :]
    parity = np.zeros((order, order), np.int64)
    for position in range(order.bit_length() - 1):
        parity += common >> position & 1
    return (1 - 2 * (parity % 2)).astype(np.float32)


def tables():
    row = np.arange(REPLICAS * SEGS * OWN)
    owner, segment, own = row // (SEGS * OWN), row % (SEGS * OWN) // OWN, row % OWN
    spread = (owner * OWN + own)[:, None] == np.arange(ROWS)[None, :]
    col = np.arange(2 * PEERS * SEGS * 2)
    patch = col // (SEGS * 2) * 2 + col % 2
    col_segment = col % (SEGS * 2) // 2
    widen = np.arange(TOK)[:, None] == patch[None, :]
    same = segment[:, None] == col_segment[None, :]
    return (
        spread.astype(np.float32),
        widen.astype(np.float32),
        same.astype(np.float32),
        col_segment,
    )


def butterfly(parts):
    parts = list(parts)
    span = 1
    while span < len(parts):
        for start in range(0, len(parts), 2 * span):
            for k in range(start, start + span):
                first, second = parts[k], parts[k + span]
                parts[k], parts[k + span] = first + second, first - second
        span *= 2
    return parts


def whole(shape):
    return pl.BlockSpec(shape, lambda *_: (0,) * len(shape))


def params():
    return pltpu.CompilerParams(vmem_limit_bytes=VMEM)


def rotate_upstream_kernel(u_ref, sign_ref, had_ref, out_ref, x_ref, z_ref):
    turned = u_ref[...].astype(f32) * sign_ref[...]
    for t in range(COLS // LANES):
        x_ref[2 * t : 2 * t + 2, :] = turned[:, LANES * t : LANES * (t + 1)]
    x_ref[...] = jnp.dot(
        x_ref[...].astype(bf16), had_ref[...], preferred_element_type=f32
    )
    for b in range(BLOCKS):
        mixed = butterfly([x_ref[2 * t : 2 * t + 2, :] for t in range(8 * b, 8 * b + 8)])
        for k, part in enumerate(mixed):
            s, lane = divmod(8 * b + k, SEG // LANES)
            z_ref[2 * s : 2 * s + 2, LANES * lane : LANES * (lane + 1)] = (
                part * hadamard_norm
            )
    out_ref[...] = z_ref[...].astype(bf16)


def rotate_upstream(upstream, sign_row, had):
    return pl.pallas_call(
        rotate_upstream_kernel,
        out_shape=jax.ShapeDtypeStruct((2 * SEGS, SEG), bf16),
        scratch_shapes=[
            pltpu.VMEM((2 * COLS // LANES, LANES), f32),
            pltpu.VMEM((2 * SEGS, SEG), f32),
        ],
        compiler_params=params(),
        name="rotate_upstream",
    )(upstream, sign_row, had)


def expand_hidden_kernel(hidden_ref, spread_ref, widen_ref, same_ref, out_ref):
    rows = lax.dot_general(
        spread_ref[...],
        hidden_ref[...],
        (((1,), (1,)), ((), ())),
        preferred_element_type=f32,
    ).astype(bf16)
    wide = jnp.dot(rows, widen_ref[...], preferred_element_type=f32)
    out_ref[...] = (wide * same_ref[...].astype(f32)).astype(bf16)


def expand_hidden(hidden, spread, widen, same):
    return pl.pallas_call(
        expand_hidden_kernel,
        out_shape=jax.ShapeDtypeStruct(same.shape, bf16),
        compiler_params=params(),
        cost_estimate=pl.CostEstimate(
            flops=2 * 768 * 128 * 700, bytes_accessed=4 << 20, transcendentals=0
        ),
        name="expand_hidden",
    )(hidden, spread, widen, same)


TILE = 256


def encode_kernel(left_ref, own_ref, other_ref, scale_ref, out_ref):
    half = own_ref.shape[0]
    total = jnp.dot(left_ref[:, :half], own_ref[...], preferred_element_type=f32)
    total += jnp.dot(left_ref[:, half:], other_ref[...], preferred_element_type=f32)
    total = jnp.clip(total * scale_ref[0], -clip_limit, clip_limit)
    out_ref[...] = total.astype(bf16)


def encode(left, own, other, scale):
    rows = left.shape[0]
    half = own.shape[0]
    return pl.pallas_call(
        encode_kernel,
        out_shape=jax.ShapeDtypeStruct((rows, SEG), bf16),
        grid=(SEG // TILE,),
        in_specs=[
            whole(left.shape),
            pl.BlockSpec((half, TILE), lambda n: (0, n)),
            pl.BlockSpec((half, TILE), lambda n: (0, n)),
            pl.BlockSpec((1, rows, 1), lambda n: (n // 2, 0, 0)),
        ],
        out_specs=pl.BlockSpec((rows, TILE), lambda n: (0, n)),
        compiler_params=params(),
        cost_estimate=pl.CostEstimate(
            flops=2 * rows * 2 * half * SEG, bytes_accessed=6 << 20, transcendentals=0
        ),
        name="encode",
    )(left, own, other, scale)


def update_kernel(
    received_ref, power_ref, sign_ref, had_ref, first_ref, second_ref, weight_ref,
    mean_ref, first_out, second_out, sent_ref, sum_ref, x_ref, y_ref,
):
    total = received_ref[0].astype(f32)
    for source in range(1, received_ref.shape[0]):
        total += received_ref[source].astype(f32)
    sum_ref[...] = total
    x_ref[...] = jnp.zeros_like(x_ref)
    for t in range(COLS // LANES):
        s, lane = divmod(t, SEG // LANES)
        x_ref[16 * t : 16 * t + OWN, :] = (
            sum_ref[OWN * s : OWN * (s + 1), LANES * lane : LANES * (lane + 1)]
            * power_ref[:, t // 8 : t // 8 + 1]
        )
    x = x_ref[...]
    high = x.astype(bf16)
    low = (x - high.astype(f32)).astype(bf16)
    y_ref[...] = jnp.dot(high, had_ref[...], preferred_element_type=f32) + jnp.dot(
        low, had_ref[...], preferred_element_type=f32
    )
    for b in range(BLOCKS):
        mixed = butterfly(
            [y_ref[16 * t : 16 * t + OWN, :] for t in range(8 * b, 8 * b + 8)]
        )
        for k, part in enumerate(mixed):
            t = 8 * b + k
            s, lane = divmod(t, SEG // LANES)
            lanes = slice(LANES * t, LANES * (t + 1))
            mean = part * (hadamard_norm / REPLICAS) * sign_ref[:, lanes]
            mean_ref[:, lanes] = mean
            first = 0.9 * first_ref[:, lanes] + 0.1 * mean
            second = 0.95 * second_ref[:, lanes] + 0.05 * mean * mean
            first_out[:, lanes] = first
            second_out[:, lanes] = second
            adjusted = first / 0.6513215599 / (jnp.sqrt(second / 0.4012630608) + 1e-08)
            sum_ref[OWN * s : OWN * (s + 1), LANES * lane : LANES * (lane + 1)] = (
                weight_ref[:, lanes].astype(f32) * (1.0 - 0.01 * 0.1) - 0.01 * adjusted
            )
    sent_ref[...] = sum_ref[...].astype(bf16)


def update(received, power, sign_row, had, first, second, weight):
    own = jax.ShapeDtypeStruct((OWN, COLS), f32)
    return pl.pallas_call(
        update_kernel,
        out_shape=(own, own, own, jax.ShapeDtypeStruct((SEGS * OWN, SEG), bf16)),
        scratch_shapes=[
            pltpu.VMEM((SEGS * OWN, SEG), f32),
            pltpu.VMEM((16 * COLS // LANES, LANES), f32),
            pltpu.VMEM((16 * COLS // LANES, LANES), f32),
        ],
        compiler_params=params(),
        name="update",
    )(received, power, sign_row, had, first, second, weight)


def place_kernel(gathered_ref, out_ref, rows_ref):
    for d in range(REPLICAS):
        chunk = gathered_ref[d].astype(f32)
        for s in range(SEGS):
            rows_ref[OWN * d : OWN * (d + 1), SEG * s : SEG * (s + 1)] = chunk[
                OWN * s : OWN * (s + 1), :
            ]
    out_ref[...] = rows_ref[...].astype(bf16)


def place(gathered):
    return pl.pallas_call(
        place_kernel,
        out_shape=jax.ShapeDtypeStruct((ROWS, COLS), bf16),
        scratch_shapes=[pltpu.VMEM((ROWS, COLS), f32)],
        compiler_params=params(),
        name="place",
    )(gathered)


def rotate_weight_kernel(w_ref, sign_ref, had_ref, out_ref):
    turned = w_ref[...].astype(f32) * sign_ref[...]
    parts = [
        jnp.dot(
            turned[:, LANES * k : LANES * (k + 1)].astype(bf16),
            had_ref[...],
            preferred_element_type=f32,
        )
        for k in range(8)
    ]
    for k, part in enumerate(butterfly(parts)):
        out_ref[:, LANES * k : LANES * (k + 1)] = (part * hadamard_norm).astype(bf16)


def rotate_weight(weight, sign_row, had):
    return pl.pallas_call(
        rotate_weight_kernel,
        out_shape=jax.ShapeDtypeStruct((ROWS, COLS), bf16),
        grid=(BLOCKS,),
        in_specs=[
            pl.BlockSpec((ROWS, 1024), lambda b: (0, b)),
            pl.BlockSpec((1, 1024), lambda b: (0, b)),
            whole((LANES, LANES)),
        ],
        out_specs=pl.BlockSpec((ROWS, 1024), lambda b: (0, b)),
        compiler_params=params(),
        cost_estimate=pl.CostEstimate(
            flops=2 * ROWS * COLS * 1024, bytes_accessed=5 << 20, transcendentals=0
        ),
        name="rotate_weight",
    )(weight, sign_row, had)


def pre_grad_kernel(own_ref, other_ref, w_ref, slope_ref, collect_ref, out_ref, acc_ref):
    half = own_ref.shape[0]
    place_in_pair = lax.broadcasted_iota(jnp.int32, (half, 1), 0) & (2 * SEGS - 1)
    for index, rows_ref in enumerate((own_ref, other_ref)):
        rows = rows_ref[...]
        total = jnp.zeros((half, ROWS), f32)
        for s in range(SEGS):
            part = lax.dot_general(
                rows,
                w_ref[:, SEG * s : SEG * (s + 1)],
                (((1,), (1,)), ((), ())),
                preferred_element_type=f32,
            )
            total = jnp.where(place_in_pair >> 1 == s, part, total)
        acc_ref[half * index : half * (index + 1), :] = total
    hidden_grad = jnp.dot(
        collect_ref[...].astype(f32),
        acc_ref[...],
        precision=lax.Precision.HIGHEST,
        preferred_element_type=f32,
    )
    out_ref[...] = (hidden_grad * slope_ref[...]).astype(bf16)


def pre_grad_product(own, other, weight, slope, collect):
    return pl.pallas_call(
        pre_grad_kernel,
        out_shape=jax.ShapeDtypeStruct((TOK, ROWS), bf16),
        scratch_shapes=[pltpu.VMEM((2 * own.shape[0], ROWS), f32)],
        compiler_params=params(),
        cost_estimate=pl.CostEstimate(
            flops=8 * 512 * SEG * ROWS, bytes_accessed=6 << 20, transcendentals=0
        ),
        name="pre_grad",
    )(own, other, weight, slope, collect)


def swap_core(values):
    return lax.ppermute(values, "core", [(0, 1), (1, 0)])


def body(upstream, pre_act, w_down, first_moment, second_moment, signs, exponents):
    spread_np, widen_np, same_np, _ = tables()
    had = jnp.asarray(hadamard(LANES), bf16)
    spread = jnp.asarray(spread_np, bf16)
    widen = jnp.asarray(widen_np, bf16)
    same = jnp.asarray(same_np, bf16)
    sign_row = (1 - 2 * signs).astype(f32).reshape(1, COLS)
    core = lax.axis_index("core")

    rotated = rotate_upstream(upstream, sign_row, had)
    own = lax.all_to_all(
        jnp.broadcast_to(rotated[None], (PEERS, 2 * SEGS, SEG)),
        ("z_hi", "y"),
        0,
        0,
        tiled=True,
    ).reshape(PEERS * 2 * SEGS, SEG)
    other = swap_core(own)

    pairs = pre_act.reshape(PEERS, 2, 2, ROWS)
    mine = jnp.where(core == 0, pairs[:, 0], pairs[:, 1]).reshape(TOK // 2, ROWS)
    yours = jnp.where(core == 0, pairs[:, 1], pairs[:, 0]).reshape(TOK // 2, ROWS)
    preact = jnp.concatenate([mine, yours], axis=0).astype(f32)
    normal_cdf = 0.5 * (1.0 + lax.erf(preact * root_half))
    hidden = (preact * normal_cdf).astype(bf16)
    slope = normal_cdf + preact * jnp.exp(-0.5 * preact * preact) * density_norm

    scale_power = exponents.astype(f32)
    shrink = jnp.exp2(-scale_power)
    picked = jnp.stack(
        [
            jnp.stack([shrink[:, (3 * s + u) // 2] for s in range(SEGS)], axis=0)
            for u in range(3)
        ],
        axis=0,
    )
    scale = (
        picked.reshape(3, SEGS, REPLICAS, OWN)
        .transpose(0, 2, 1, 3)
        .reshape(3, REPLICAS * SEGS * OWN, 1)
    )
    left = expand_hidden(hidden, spread, widen, same)
    encoded = encode(left, own, other, scale)
    received = lax.all_to_all(
        encoded.reshape(REPLICAS, SEGS * OWN, SEG), ("z_lo", "x"), 0, 0, tiled=True
    )

    turned_weight = rotate_weight(w_down, sign_row, had)
    mixed = pre_grad_product(own, other, turned_weight, slope, widen)
    halves = mixed.reshape(2, PEERS, 2, ROWS)
    zero = jnp.where(core == 0, halves[0], halves[1])
    one = jnp.where(core == 0, halves[1], halves[0])
    pre_grad = jnp.stack([zero, one], axis=1).reshape(TOK, ROWS)

    offset = lax.axis_index(("z_lo", "x")) * OWN
    own_power = jnp.exp2(lax.dynamic_slice_in_dim(scale_power, offset, OWN, 0))
    own_weight = lax.dynamic_slice_in_dim(w_down, offset, OWN, 0)
    grad_mean, first_new, second_new, sent = update(
        received, own_power, sign_row, had, first_moment, second_moment, own_weight
    )
    gathered = lax.all_to_all(
        jnp.broadcast_to(sent[None], (REPLICAS, SEGS * OWN, SEG)),
        ("z_lo", "x"),
        0,
        0,
        tiled=True,
    )
    weight_new = place(gathered)
    return (pre_grad, grad_mean, first_new, second_new, weight_new)


def solution(mesh):
    fine = Mesh(
        mesh.devices.reshape(2, 8, 4, 8, 2), ("z_lo", "x", "z_hi", "y", "core")
    )
    dp = ("z_lo", "x")
    mp = ("z_hi", "y", "core")
    placed = (
        P(dp + mp, None),
        P(dp, mp),
        P(mp, None),
        P(mp + dp, None),
        P(mp + dp, None),
        P(),
        P(mp, None),
    )
    return jax.shard_map(
        body,
        mesh=fine,
        in_specs=placed,
        out_specs=(
            P(dp, mp),
            P(mp + dp, None),
            P(mp + dp, None),
            P(mp + dp, None),
            P(mp, None),
        ),
        check_vma=False,
    )
```

time: 335 us -> 199 us (0.59)
  waiting for transfers between devices: 189 us -> 125 us
  blocking collectives: 48 us -> 0 us
  local copies, waits for them, and re-layouts: 42.6 us -> 13.8 us
  starting transfers between devices: 14.3 us -> 41.6 us
  Pallas kernels: 0 us -> 15.2 us
  between operations: 14.9 us -> 0.94 us
  other arithmetic: 14.9 us -> 1.72 us
  matrix products: 10.7 us -> 0 us
    all_gather x2 -> x0, waiting for transfers between devices: 176 us -> none  [the longest x1 99 us: body(): gathered = lax.all_gather(upstream, 'mp', axis=0, tiled=True)]
    all_to_all x0 -> x3, waiting for transfers between devices: none -> 125 us  [the longest x1 53.3 us: body(): lax.all_to_all(encoded.reshape(REPLICAS, SEGS * OWN, SEG), ('z_lo', 'x'),...]
    unnamed x1 -> x0, blocking collectives: 48 us -> none
    all_to_all x0 -> x3, starting transfers between devices: none -> 39.7 us  [the longest x1 22.1 us: body(): lax.all_to_all(jnp.broadcast_to(rotated[None], (PEERS, 2 * SEGS, SEG)), (...]
    pallas_call x0 -> x7, Pallas kernels: none -> 15.2 us  [the longest x1 4.42 us: encode(): pl.pallas_call(encode_kernel, out_shape=jax.ShapeDtypeStruct((rows, SEG),...]
    unnamed x4 -> x0, starting transfers between devices: 14.2 us -> none
    reshape x4 -> x3, local copies, waits for them, and re-layouts: 14.6 us -> 0.47 us  [the longest x1 0.36 us: body(): scale = picked.reshape(3, SEGS, REPLICAS, OWN).transpose(0, 2, 1, 3).resh...]
    unnamed x6 -> x0, waiting for transfers between devices: 12.7 us -> none
  transfers between devices with their start and end apart: 6 -> 4, of which waited for: 3 -> 3; matrix products, arithmetic and copies ran while one was open for 4% -> 2% of each run, Pallas kernels for 0% -> 3%
where the time goes in v1:
time: 199 us; the launch traced here: 198 us
  waiting for transfers between devices  125 us (63%)
  starting transfers between devices  41.6 us (21%)
  Pallas kernels  15.2 us (8%)
  local copies, waits for them, and re-layouts  13.8 us (7%)
    all_to_all x1, waiting for transfers between devices, body(): lax.all_to_all(encoded.reshape(REPLICAS, SEGS * OWN, SEG), ('z_lo', 'x'),...  53.3 us
    all_to_all x1, waiting for transfers between devices, body(): lax.all_to_all(jnp.broadcast_to(sent[None], (REPLICAS, SEGS * OWN, SEG)),...  46.2 us
    all_to_all x1, waiting for transfers between devices, body(): lax.all_to_all(jnp.broadcast_to(rotated[None], (PEERS, 2 * SEGS, SEG)), (...  25.6 us
    all_to_all x1, starting transfers between devices, body(): lax.all_to_all(jnp.broadcast_to(rotated[None], (PEERS, 2 * SEGS, SEG)), (...  22.1 us
    all_to_all x1, starting transfers between devices, body(): lax.all_to_all(jnp.broadcast_to(sent[None], (REPLICAS, SEGS * OWN, SEG)),...  8.87 us
    all_to_all x1, starting transfers between devices, body(): lax.all_to_all(encoded.reshape(REPLICAS, SEGS * OWN, SEG), ('z_lo', 'x'),...  8.7 us
    unnamed x29, local copies, waits for them, and re-layouts  8.65 us
    pallas_call x1, Pallas kernels, encode(): pl.pallas_call(encode_kernel, out_shape=jax.ShapeDtypeStruct((rows, SEG),...  4.42 us
  transfers between devices with their start and end apart: 4, of which 3 were waited for; matrix products, arithmetic and copies ran while one was open for 2% of the time, Pallas kernels for 3%

profile of v1, /device:TPU:16, one launch (start us, length us, event | category | flops | bytes accessed | tf_op | source)
XLA Modules:
  0.0 198.3 jit_solution(16346966865554481270)
XLA Ops:
  0.6 0.8 subtract_convert_fusion
  1.4 0.8 copy-done.7
  2.2 0.7 copy-done.9
  2.9 0.2 rotate_upstream.1
  3.1 0.9 broadcast_in_dim.4
  4.0 22.1 %all-to-all-start = ((bf16[32,8,1536]{2,1,0:T(8,128)(2,1)}), bf16[32,8,1536]{2,1,0:T(8,128)(2,1)S(1)}, u32[]{:S(2)}, u32[]{:S(2)}) async-start(bf16[32,8,1536]{2,1,0:T(8,128)(2,1)} %broadcast_in_dim.4), calls=%async_computation | async-start | bytes 1572864 | tf_op jit(solution)/shard_map/all_to_all | solution.py:323
  26.1 0.1 copy.21
  26.3 25.6 %all-to-all-done = bf16[32,8,1536]{2,1,0:T(8,128)(2,1)S(1)} async-done(((bf16[32,8,1536]{2,1,0:T(8,128)(2,1)}), bf16[32,8,1536]{2,1,0:T(8,128)(2,1)S(1)}, u32[]{:S(2)}, u32[]{:S(2)}) %all-to-all-start) | async-done | bytes 786464 | tf_op jit(solution)/shard_map/all_to_all | solution.py:323
  51.9 1.9 collective-permute-start
  53.9 0.1 copy.24
  54.1 0.4 slice_reduce_fusion.5
  55.1 0.4 reshape.120.scale_ref
  55.5 0.7 fusion.6
  56.2 1.1 copy-done.1
  57.4 0.7 expand_hidden.1.left_ref
  58.1 4.4 %encode.1 = bf16[768,1536]{1,0:T(8,128)(2,1)S(1)} custom-call(bf16[768,512]{1,0:T(8,128)(2,1)S(1)} %expand_hidden.1.left_ref, bf16[256,1536]{1,0:T(8,128)(2,1)S(1)} %bitcast.9, bf16[256,1536]{1,0:T(8,128)(2,1)} %collective-permute-done.other_ref, f32[3,768,1]{2,1,0:T(8,128)S(1)} %reshape.120.scale_ref), custom_call_target="tpu_custom_call" | custom-call | flops 1207959552 | bytes 6291456 | tf_op jit(solution)/shard_map/encode/pallas_call | solution.py:143
  62.5 1.4 copy-done
  63.9 8.7 %all-to-all-start.1 = ((bf16[16,48,1536]{2,1,0:T(8,128)(2,1)}), bf16[16,48,1536]{2,1,0:T(8,128)(2,1)S(1)}, u32[]{:S(2)}, u32[]{:S(2)}) async-start(bf16[16,48,1536]{2,1,0:T(8,128)(2,1)} %bitcast.7), calls=%async_computation.1 | async-start | bytes 4718592 | tf_op jit(solution)/shard_map/all_to_all | solution.py:356
  72.7 1.0 constant_dynamic-slice_fusion.weight_ref
  73.7 53.3 %all-to-all-done.1.received_ref = bf16[16,48,1536]{2,1,0:T(8,128)(2,1)S(1)} async-done(((bf16[16,48,1536]{2,1,0:T(8,128)(2,1)}), bf16[16,48,1536]{2,1,0:T(8,128)(2,1)S(1)}, u32[]{:S(2)}, u32[]{:S(2)}) %all-to-all-start.1) | async-done | bytes 2359328 | tf_op jit(solution)/shard_map/all_to_all | solution.py:356
  127.0 1.0 copy-done.2
  128.0 1.0 copy-done.3
  129.0 1.9 update.1
  130.9 1.6 broadcast_in_dim.5
  132.5 8.9 %all-to-all-start.2 = ((bf16[16,48,1536]{2,1,0:T(8,128)(2,1)}), bf16[16,48,1536]{2,1,0:T(8,128)(2,1)S(1)}, u32[]{:S(2)}, u32[]{:S(2)}) async-start(bf16[16,48,1536]{2,1,0:T(8,128)(2,1)} %broadcast_in_dim.5), calls=%async_computation.2 | async-start | bytes 4718592 | tf_op jit(solution)/shard_map/all_to_all | solution.py:373
  141.4 1.7 copy-done.10
  143.1 2.4 %rotate_weight.1.w_ref = bf16[192,6144]{1,0:T(8,128)(2,1)S(1)} custom-call(bf16[192,6144]{1,0:T(8,128)(2,1)S(1)} %copy-done.10, f32[1,6144]{1,0:T(1,128)S(1)} %bitcast.13, bf16[128,128]{1,0:T(8,128)(2,1)S(1)} %copy-done.8), custom_call_target="tpu_custom_call" | custom-call | flops 2415919104 | bytes 5242880 | tf_op jit(solution)/shard_map/rotate_weight/pallas_call | solution.py:254
  145.5 3.6 %pre_grad.1 = bf16[128,192]{1,0:T(8,128)(2,1)S(1)} custom-call(bf16[256,1536]{1,0:T(8,128)(2,1)S(1)} %bitcast.10, bf16[256,1536]{1,0:T(8,128)(2,1)} %collective-permute-done.other_ref, bf16[192,6144]{1,0:T(8,128)(2,1)S(1)} %rotate_weight.1.w_ref, f32[128,192]{1,0:T(8,128)S(1)} %copy-done.6, bf16[128,512]{1,0:T(8,128)(2,1)S(1)} %copy-done.5), custom_call_target="tpu_custom_call" | custom-call | flops 1207959552 | bytes 6291456 | tf_op jit(solution)/shard_map/pre_grad/pallas_call | solution.py:297
  149.2 0.1 pad_maximum_fusion.1
  149.4 0.7 copy.27
  150.1 46.2 %all-to-all-done.2.gathered_ref = bf16[16,48,1536]{2,1,0:T(8,128)(2,1)S(1)} async-done(((bf16[16,48,1536]{2,1,0:T(8,128)(2,1)}), bf16[16,48,1536]{2,1,0:T(8,128)(2,1)S(1)}, u32[]{:S(2)}, u32[]{:S(2)}) %all-to-all-start.2) | async-done | bytes 2359328 | tf_op jit(solution)/shard_map/all_to_all | solution.py:373
  196.3 2.0 %place.1 = bf16[192,6144]{1,0:T(8,128)(2,1)} custom-call(bf16[16,48,1536]{2,1,0:T(8,128)(2,1)S(1)} %all-to-all-done.2.gathered_ref), custom_call_target="tpu_custom_call" | custom-call | tf_op jit(solution)/shard_map/place/pallas_call | solution.py:230
  (39 shorter events, 0.9 us)
Async XLA Ops:
  0.6 25.5 %copy-start.11 = (bf16[128,192]{0,1:T(8,128)(2,1)S(1)}, bf16[128,192]{0,1:T(8,128)(2,1)}, u32[]{:S(2)}) copy-start(bf16[128,192]{0,1:T(8,128)(2,1)} %param.12) | copy-start | bytes 147460
  1.4 0.8 copy-start.7
  2.2 0.7 copy-start.9
  2.9 51.0 %copy-start.12 = (s32[192,6]{0,1:T(8,128)S(1)}, s32[192,6]{0,1:T(8,128)}, u32[]{:S(2)}) copy-start(s32[192,6]{0,1:T(8,128)} %param.17) | copy-start | bytes 13828
  4.0 52.2 %copy-start.4 = (bf16[768,192]{1,0:T(8,128)(2,1)S(1)}, bf16[768,192]{1,0:T(8,128)(2,1)}, u32[]{:S(2)}) copy-start(bf16[768,192]{1,0:T(8,128)(2,1)} %constant.48.clone.spread_ref) | copy-start | bytes 884740
  4.0 52.2 %copy-start.5 = (bf16[128,512]{1,0:T(8,128)(2,1)S(1)}, bf16[128,512]{1,0:T(8,128)(2,1)}, u32[]{:S(2)}) copy-start(bf16[128,512]{1,0:T(8,128)(2,1)} %constant.49.clone.collect_ref.widen_ref) | copy-start | bytes 393220
  4.0 47.8 %all-to-all-start = ((bf16[32,8,1536]{2,1,0:T(8,128)(2,1)}), bf16[32,8,1536]{2,1,0:T(8,128)(2,1)S(1)}, u32[]{:S(2)}, u32[]{:S(2)}) async-start(bf16[32,8,1536]{2,1,0:T(8,128)(2,1)} %broadcast_in_dim.4), calls=%async_computation | async-start | bytes 1572864 | tf_op jit(solution)/shard_map/all_to_all | solution.py:323
  51.9 6.2 %collective-permute-start = (bf16[256,1536]{1,0:T(8,128)(2,1)S(1)}, bf16[256,1536]{1,0:T(8,128)(2,1)}, u32[]{:S(2)}, u32[]{:S(2)}) collective-permute-start(bf16[256,1536]{1,0:T(8,128)(2,1)S(1)} %bitcast.8), channel_id=1, source_target_pairs={{0,1},{1,0},{2,3},{3,2},{4,5},{5,4},{6,7},{7,6},{8,9},{9,8},{10,11... | collective-permute-start | bytes 2359304 | tf_op jit(solution)/shard_map/ppermute | solution.py:310
  56.2 1.1 copy-start.1
  62.5 1.4 copy-start
  63.9 63.1 %copy-start.8 = (bf16[128,128]{1,0:T(8,128)(2,1)S(1)}, bf16[128,128]{1,0:T(8,128)(2,1)}, u32[]{:S(2)}) copy-start(bf16[128,128]{1,0:T(8,128)(2,1)} %constant.47.clone.had_ref) | copy-start | bytes 98308
  63.9 63.1 %all-to-all-start.1 = ((bf16[16,48,1536]{2,1,0:T(8,128)(2,1)}), bf16[16,48,1536]{2,1,0:T(8,128)(2,1)S(1)}, u32[]{:S(2)}, u32[]{:S(2)}) async-start(bf16[16,48,1536]{2,1,0:T(8,128)(2,1)} %bitcast.7), calls=%async_computation.1 | async-start | bytes 4718592 | tf_op jit(solution)/shard_map/all_to_all | solution.py:356
  127.0 1.0 copy-start.2
  128.0 1.0 copy-start.3
  132.5 63.8 %all-to-all-start.2 = ((bf16[16,48,1536]{2,1,0:T(8,128)(2,1)}), bf16[16,48,1536]{2,1,0:T(8,128)(2,1)S(1)}, u32[]{:S(2)}, u32[]{:S(2)}) async-start(bf16[16,48,1536]{2,1,0:T(8,128)(2,1)} %broadcast_in_dim.5), calls=%async_computation.2 | async-start | bytes 4718592 | tf_op jit(solution)/shard_map/all_to_all | solution.py:373
  141.4 1.7 copy-start.10
  143.1 2.5 %copy-start.6 = (f32[128,192]{1,0:T(8,128)S(1)}, f32[128,192]{1,0:T(8,128)}, u32[]{:S(2)}) copy-start(f32[128,192]{1,0:T(8,128)} %get-tuple-element.25.slope_ref) | copy-start | bytes 294916

commit v2 on v1

v2 whole, which is shorter than its diff:
```python
import functools

import jax
import jax.numpy as jnp
import numpy as np
from jax import lax
from jax.experimental import pallas as pl
from jax.experimental.pallas import tpu as pltpu
from jax.sharding import Mesh
from jax.sharding import PartitionSpec as P

hadamard_norm = 0.03125
clip_limit = 448.0
root_half = 0.7071067811865476
density_norm = 0.3989422804014327

REPLICAS = 16
ROWS = 192
OWN = 12
COLS = 6144
HALF = 3072
SEGS = 4
SEG = 768
BLOCKS = 3
TOK = 128
LINE = 8
SHARE = LINE * OWN
PEERS = 32
LANES = 128
TILE = 256
bf16 = jnp.bfloat16
f32 = jnp.float32


def hadamard(order):
    indices = np.arange(order)
    common = indices[:, None] & indices[None, :]
    parity = np.zeros((order, order), np.int64)
    for position in range(order.bit_length() - 1):
        parity += common >> position & 1
    return (1 - 2 * (parity % 2)).astype(np.float32)


def tables():
    row = np.arange(LINE * SEGS * OWN)
    owner, segment, own = row // (SEGS * OWN), row % (SEGS * OWN) // OWN, row % OWN
    spread = (owner * OWN + own)[:, None] == np.arange(SHARE)[None, :]
    col = np.arange(2 * PEERS * SEGS * 2)
    patch = col // (SEGS * 2) * 2 + col % 2
    col_segment = col % (SEGS * 2) // 2
    widen = np.arange(TOK)[:, None] == patch[None, :]
    same = segment[:, None] == col_segment[None, :]
    return [jnp.asarray(table, bf16) for table in (spread, widen, same)]


def butterfly(parts):
    parts = list(parts)
    span = 1
    while span < len(parts):
        for start in range(0, len(parts), 2 * span):
            for k in range(start, start + span):
                first, second = parts[k], parts[k + span]
                parts[k], parts[k + span] = first + second, first - second
        span *= 2
    return parts


def whole(shape):
    return pl.BlockSpec(shape, lambda *_: (0,) * len(shape))


def params(mebibytes=8):
    return pltpu.CompilerParams(vmem_limit_bytes=mebibytes << 20)


def rotate_upstream_kernel(u_ref, sign_ref, had_ref, low_ref, high_ref, x_ref, z_ref):
    turned = u_ref[...].astype(f32) * sign_ref[...]
    for t in range(COLS // LANES):
        x_ref[2 * t : 2 * t + 2, :] = turned[:, LANES * t : LANES * (t + 1)]
    x_ref[...] = jnp.dot(
        x_ref[...].astype(bf16), had_ref[...], preferred_element_type=f32
    )
    for half, out_ref in enumerate((low_ref, high_ref)):
        for b in range(BLOCKS):
            base = half * HALF // LANES + 8 * b
            mixed = butterfly([x_ref[2 * t : 2 * t + 2, :] for t in range(base, base + 8)])
            for k, part in enumerate(mixed):
                s, lane = divmod(8 * b + k, SEG // LANES)
                z_ref[2 * s : 2 * s + 2, LANES * lane : LANES * (lane + 1)] = (
                    part * hadamard_norm
                )
        out_ref[...] = z_ref[...].astype(bf16)


def rotate_upstream(upstream, sign_row, had):
    part = jax.ShapeDtypeStruct((2 * SEGS, SEG), bf16)
    return pl.pallas_call(
        rotate_upstream_kernel,
        out_shape=(part, part),
        scratch_shapes=[
            pltpu.VMEM((2 * COLS // LANES, LANES), f32),
            pltpu.VMEM((2 * SEGS, SEG), f32),
        ],
        compiler_params=params(),
        name="rotate_upstream",
    )(upstream, sign_row, had)


def expand_hidden_kernel(hidden_ref, spread_ref, widen_ref, same_ref, out_ref):
    rows = lax.dot_general(
        spread_ref[...],
        hidden_ref[...],
        (((1,), (1,)), ((), ())),
        preferred_element_type=f32,
    ).astype(bf16)
    wide = jnp.dot(rows, widen_ref[...], preferred_element_type=f32)
    out_ref[...] = (wide * same_ref[...].astype(f32)).astype(bf16)


def expand_hidden(hidden, spread, widen, same):
    return pl.pallas_call(
        expand_hidden_kernel,
        out_shape=jax.ShapeDtypeStruct(same.shape, bf16),
        compiler_params=params(),
        cost_estimate=pl.CostEstimate(
            flops=2 * 768 * 128 * 700, bytes_accessed=4 << 20, transcendentals=0
        ),
        name="expand_hidden",
    )(hidden, spread, widen, same)


def encode_kernel(
    mine_ref, theirs_ref, own0_ref, other0_ref, own1_ref, other1_ref, scale_ref, out_ref
):
    total = None
    for left_ref, own_ref, other_ref in (
        (mine_ref, own0_ref, other0_ref),
        (theirs_ref, own1_ref, other1_ref),
    ):
        half = own_ref.shape[0]
        term = jnp.dot(left_ref[:, :half], own_ref[...], preferred_element_type=f32)
        term += jnp.dot(left_ref[:, half:], other_ref[...], preferred_element_type=f32)
        term = jnp.clip(term * scale_ref[0], -clip_limit, clip_limit)
        term = term.astype(bf16).astype(f32)
        total = term if total is None else total + term
    out_ref[...] = total.astype(bf16)


def encode(mine, theirs, parts, scale):
    rows = mine.shape[0]
    depth = parts[0].shape[0]
    return pl.pallas_call(
        encode_kernel,
        out_shape=jax.ShapeDtypeStruct((rows, SEG), bf16),
        grid=(SEG // TILE,),
        in_specs=[whole(mine.shape), whole(theirs.shape)]
        + [pl.BlockSpec((depth, TILE), lambda n: (0, n))] * 4
        + [pl.BlockSpec((1, rows, 1), lambda n: (n, 0, 0))],
        out_specs=pl.BlockSpec((rows, TILE), lambda n: (0, n)),
        compiler_params=params(12),
        cost_estimate=pl.CostEstimate(
            flops=8 * rows * depth * SEG, bytes_accessed=4 << 20, transcendentals=0
        ),
        name="encode",
    )(mine, theirs, *parts, scale)


def update_kernel(
    half, received_ref, power_ref, sign_ref, had_ref, first_ref, second_ref,
    weight_ref, *refs,
):
    mean_ref, first_out, second_out, sent_ref, sum_ref, x_ref, y_ref = refs[-7:]
    total = received_ref[0].astype(f32)
    for source in range(1, received_ref.shape[0]):
        total += received_ref[source].astype(f32)
    sum_ref[...] = total
    x_ref[...] = jnp.zeros_like(x_ref)
    for t in range(HALF // LANES):
        s, lane = divmod(t, SEG // LANES)
        block = BLOCKS * half + t // 8
        x_ref[16 * t : 16 * t + OWN, :] = (
            sum_ref[OWN * s : OWN * (s + 1), LANES * lane : LANES * (lane + 1)]
            * power_ref[:, block : block + 1]
        )
    x = x_ref[...]
    high = x.astype(bf16)
    low = (x - high.astype(f32)).astype(bf16)
    y_ref[...] = jnp.dot(high, had_ref[...], preferred_element_type=f32) + jnp.dot(
        low, had_ref[...], preferred_element_type=f32
    )
    for b in range(BLOCKS):
        mixed = butterfly(
            [y_ref[16 * t : 16 * t + OWN, :] for t in range(8 * b, 8 * b + 8)]
        )
        for k, part in enumerate(mixed):
            t = 8 * b + k
            s, lane = divmod(t, SEG // LANES)
            lanes = slice(LANES * t, LANES * (t + 1))
            mean = part * (hadamard_norm / REPLICAS) * sign_ref[:, lanes]
            mean_ref[:, lanes] = mean
            first = 0.9 * first_ref[:, lanes] + 0.1 * mean
            second = 0.95 * second_ref[:, lanes] + 0.05 * mean * mean
            first_out[:, lanes] = first
            second_out[:, lanes] = second
            adjusted = first / 0.6513215599 / (jnp.sqrt(second / 0.4012630608) + 1e-08)
            sum_ref[OWN * s : OWN * (s + 1), LANES * lane : LANES * (lane + 1)] = (
                weight_ref[:, lanes].astype(f32) * (1.0 - 0.01 * 0.1) - 0.01 * adjusted
            )
    sent_ref[...] = sum_ref[...].astype(bf16)


def update(half, received, power, sign_row, had, first, second, weight, earlier):
    own = jax.ShapeDtypeStruct((OWN, COLS), f32)
    sent = jax.ShapeDtypeStruct((SEGS * OWN, SEG), bf16)

    def part(rows):
        return pl.BlockSpec((rows, HALF), lambda _: (0, half))

    kept = [pl.BlockSpec(memory_space=pl.ANY)] * len(earlier)
    return pl.pallas_call(
        functools.partial(update_kernel, half),
        out_shape=(own, own, own, sent),
        grid=(1,),
        in_specs=[
            whole(received.shape),
            whole(power.shape),
            part(1),
            whole(had.shape),
            part(OWN),
            part(OWN),
            part(OWN),
        ]
        + kept,
        out_specs=(part(OWN), part(OWN), part(OWN), whole(sent.shape)),
        scratch_shapes=[
            pltpu.VMEM((SEGS * OWN, SEG), f32),
            pltpu.VMEM((16 * HALF // LANES, LANES), f32),
            pltpu.VMEM((16 * HALF // LANES, LANES), f32),
        ],
        input_output_aliases={7 + k: k for k in range(len(earlier))},
        compiler_params=params(),
        name=f"update_{half}",
    )(received, power, sign_row, had, first, second, weight, *earlier)


def place_kernel(plane_ref, own_ref, other_ref, direct_ref, out_ref, rows_ref):
    plane = plane_ref[0]
    for d in range(REPLICAS):
        here = plane == d // LINE
        near = jnp.where(here, own_ref[d % LINE], other_ref[d % LINE]).astype(f32)
        far = direct_ref[d].astype(f32)
        for half, chunk in enumerate((near, far)):
            for s in range(SEGS):
                start = half * HALF + SEG * s
                rows_ref[OWN * d : OWN * (d + 1), start : start + SEG] = chunk[
                    OWN * s : OWN * (s + 1), :
                ]
    out_ref[...] = rows_ref[...].astype(bf16)


def place(plane, own, other, direct):
    return pl.pallas_call(
        place_kernel,
        out_shape=jax.ShapeDtypeStruct((ROWS, COLS), bf16),
        in_specs=[pl.BlockSpec(memory_space=pltpu.SMEM)]
        + [pl.BlockSpec(memory_space=pltpu.VMEM)] * 3,
        scratch_shapes=[pltpu.VMEM((ROWS, COLS), f32)],
        compiler_params=params(20),
        name="place",
    )(plane, own, other, direct)


def rotate_weight_kernel(w_ref, sign_ref, had_ref, out_ref):
    turned = w_ref[...].astype(f32) * sign_ref[...]
    parts = [
        jnp.dot(
            turned[:, LANES * k : LANES * (k + 1)].astype(bf16),
            had_ref[...],
            preferred_element_type=f32,
        )
        for k in range(8)
    ]
    for k, part in enumerate(butterfly(parts)):
        out_ref[:, LANES * k : LANES * (k + 1)] = (part * hadamard_norm).astype(bf16)


def rotate_weight(weight, sign_row, had):
    return pl.pallas_call(
        rotate_weight_kernel,
        out_shape=jax.ShapeDtypeStruct((ROWS, COLS), bf16),
        grid=(COLS // 1024,),
        in_specs=[
            pl.BlockSpec((ROWS, 1024), lambda b: (0, b)),
            pl.BlockSpec((1, 1024), lambda b: (0, b)),
            whole((LANES, LANES)),
        ],
        out_specs=pl.BlockSpec((ROWS, 1024), lambda b: (0, b)),
        compiler_params=params(),
        cost_estimate=pl.CostEstimate(
            flops=2 * ROWS * COLS * 1024, bytes_accessed=5 << 20, transcendentals=0
        ),
        name="rotate_weight",
    )(weight, sign_row, had)


def pre_grad_kernel(
    own0_ref, other0_ref, own1_ref, other1_ref, w_ref, slope_ref, collect_ref,
    out_ref, acc_ref,
):
    rows = own0_ref.shape[0]
    place_in_pair = lax.broadcasted_iota(jnp.int32, (rows, 1), 0) & (2 * SEGS - 1)
    for index, refs in enumerate(((own0_ref, own1_ref), (other0_ref, other1_ref))):
        total = None
        for half, rows_ref in enumerate(refs):
            left = rows_ref[...]
            chosen = jnp.zeros((rows, ROWS), f32)
            for s in range(SEGS):
                column = half * HALF + SEG * s
                part = lax.dot_general(
                    left,
                    w_ref[:, column : column + SEG],
                    (((1,), (1,)), ((), ())),
                    preferred_element_type=f32,
                )
                chosen = jnp.where(place_in_pair >> 1 == s, part, chosen)
            total = chosen if total is None else total + chosen
        acc_ref[rows * index : rows * (index + 1), :] = total
    hidden_grad = jnp.dot(
        collect_ref[...].astype(f32),
        acc_ref[...],
        precision=lax.Precision.HIGHEST,
        preferred_element_type=f32,
    )
    out_ref[...] = (hidden_grad * slope_ref[...]).astype(bf16)


def pre_grad_product(own0, other0, own1, other1, weight, slope, collect):
    return pl.pallas_call(
        pre_grad_kernel,
        out_shape=jax.ShapeDtypeStruct((TOK, ROWS), bf16),
        scratch_shapes=[pltpu.VMEM((2 * own0.shape[0], ROWS), f32)],
        compiler_params=params(16),
        cost_estimate=pl.CostEstimate(
            flops=8 * 512 * 1536 * ROWS, bytes_accessed=6 << 20, transcendentals=0
        ),
        name="pre_grad",
    )(own0, other0, own1, other1, weight, slope, collect)


def swap(values, axis):
    return lax.ppermute(values, axis, [(0, 1), (1, 0)])


def to_all(values, axes, count):
    return lax.all_to_all(
        jnp.broadcast_to(values[None], (count,) + values.shape), axes, 0, 0, tiled=True
    )


def body(upstream, pre_act, w_down, first_moment, second_moment, signs, exponents):
    spread, widen, same = tables()
    had = jnp.asarray(hadamard(LANES), bf16)
    sign_row = (1 - 2 * signs).astype(f32).reshape(1, COLS)
    core = lax.axis_index("core")
    plane = lax.axis_index("z_lo")
    plane_array = plane.astype(jnp.int32).reshape(1)

    pairs = pre_act.reshape(PEERS, 2, 2, ROWS)
    mine = jnp.where(core == 0, pairs[:, 0], pairs[:, 1]).reshape(TOK // 2, ROWS)
    yours = jnp.where(core == 0, pairs[:, 1], pairs[:, 0]).reshape(TOK // 2, ROWS)
    ordered = jnp.concatenate([mine, yours], axis=0)
    kept = jnp.where(plane == 0, ordered[:, :SHARE], ordered[:, SHARE:])
    given = jnp.where(plane == 0, ordered[:, SHARE:], ordered[:, :SHARE])
    taken = swap(given, "z_lo")

    rotated = rotate_upstream(upstream, sign_row, had)
    own = [to_all(part, ("z_hi", "y"), PEERS).reshape(-1, SEG) for part in rotated]
    other = [swap(part, "core") for part in own]
    partner = [swap(part, "z_lo") for part in own]
    partner_other = [swap(part, "core") for part in partner]

    preact = ordered.astype(f32)
    normal_cdf = 0.5 * (1.0 + lax.erf(preact * root_half))
    slope = normal_cdf + preact * jnp.exp(-0.5 * preact * preact) * density_norm

    def activate(values):
        values = values.astype(f32)
        return (values * (0.5 * (1.0 + lax.erf(values * root_half)))).astype(bf16)

    left = [
        expand_hidden(activate(values), spread, widen, same)
        for values in (kept, taken)
    ]

    scale_power = exponents.astype(f32)
    shrink = jnp.exp2(-jnp.where(plane == 0, scale_power[:SHARE], scale_power[SHARE:]))
    offset = lax.axis_index(("z_lo", "x")) * OWN
    own_power = jnp.exp2(lax.dynamic_slice_in_dim(scale_power, offset, OWN, 0))
    own_weight = lax.dynamic_slice_in_dim(w_down, offset, OWN, 0)

    received = []
    for half in range(2):
        picked = jnp.stack(
            [
                shrink[:, BLOCKS * half + (3 * s + n) // 4]
                for n in range(SEG // TILE)
                for s in range(SEGS)
            ],
            axis=0,
        )
        scale = (
            picked.reshape(SEG // TILE, SEGS, LINE, OWN)
            .transpose(0, 2, 1, 3)
            .reshape(SEG // TILE, LINE * SEGS * OWN, 1)
        )
        parts = (own[half], other[half], partner[half], partner_other[half])
        encoded = encode(left[0], left[1], parts, scale)
        received.append(
            lax.all_to_all(
                encoded.reshape(LINE, SEGS * OWN, SEG), "x", 0, 0, tiled=True
            )
        )

    states = (sign_row, had, first_moment, second_moment, own_weight)
    *earlier, sent0 = update(0, received[0], own_power, *states, ())
    near = to_all(sent0, "x", LINE)
    across = swap(near, "z_lo")
    *updated, sent1 = update(1, received[1], own_power, *states, earlier)
    direct = to_all(sent1, ("z_lo", "x"), REPLICAS)

    turned_weight = rotate_weight(w_down, sign_row, had)
    mixed = pre_grad_product(
        own[0], other[0], own[1], other[1], turned_weight, slope, widen
    )
    halves = mixed.reshape(2, PEERS, 2, ROWS)
    zero = jnp.where(core == 0, halves[0], halves[1])
    one = jnp.where(core == 0, halves[1], halves[0])
    pre_grad = jnp.stack([zero, one], axis=1).reshape(TOK, ROWS)

    weight_new = place(plane_array, near, across, direct)
    return (pre_grad, *updated, weight_new)


def solution(mesh):
    fine = Mesh(
        mesh.devices.reshape(2, 8, 4, 8, 2), ("z_lo", "x", "z_hi", "y", "core")
    )
    dp = ("z_lo", "x")
    mp = ("z_hi", "y", "core")
    placed = (
        P(dp + mp, None),
        P(dp, mp),
        P(mp, None),
        P(mp + dp, None),
        P(mp + dp, None),
        P(),
        P(mp, None),
    )
    return jax.shard_map(
        body,
        mesh=fine,
        in_specs=placed,
        out_specs=(
            P(dp, mp),
            P(mp + dp, None),
            P(mp + dp, None),
            P(mp + dp, None),
            P(mp, None),
        ),
        check_vma=False,
    )
```

time: 199 us -> 193 us (0.970)
  the two profiles are of different devices: /device:TPU:16 before, /device:TPU:32 now
where the time goes in v2:
time: 193 us; the launch traced here: 191 us
  waiting for transfers between devices  88.8 us (46%)
  starting transfers between devices  67.8 us (35%)
  Pallas kernels  18.6 us (10%)
  local copies, waits for them, and re-layouts  13.1 us (7%)
    ppermute x8, waiting for transfers between devices, swap(): return lax.ppermute(values, axis, [(0, 1), (1, 0)])  37.6 us
    all_to_all x4, waiting for transfers between devices, to_all(): lax.all_to_all(jnp.broadcast_to(values[None], (count,) + values.shape), a...  36.5 us
    all_to_all x4, starting transfers between devices, to_all(): lax.all_to_all(jnp.broadcast_to(values[None], (count,) + values.shape), a...  34.2 us
    ppermute x8, starting transfers between devices, swap(): return lax.ppermute(values, axis, [(0, 1), (1, 0)])  19.8 us
    all_to_all x2, waiting for transfers between devices, body(): lax.all_to_all(encoded.reshape(LINE, SEGS * OWN, SEG), 'x', 0, 0, tiled=T...  14.7 us
    all_to_all x2, starting transfers between devices, body(): lax.all_to_all(encoded.reshape(LINE, SEGS * OWN, SEG), 'x', 0, 0, tiled=T...  13.8 us
    unnamed x44, local copies, waits for them, and re-layouts  7.36 us
    pallas_call x2, Pallas kernels, encode(): pl.pallas_call(encode_kernel, out_shape=jax.ShapeDtypeStruct((rows, SEG),...  7.14 us
  transfers between devices with their start and end apart: 14, of which 8 were waited for; matrix products, arithmetic and copies ran while one was open for 3% of the time, Pallas kernels for 9%

profile of v2, /device:TPU:32, one launch (start us, length us, event | category | flops | bytes accessed | tf_op | source)
XLA Modules:
  0.0 191.4 jit_solution(9185972484056859127)
XLA Ops:
  3.9 21.7 %all-to-all-start = ((bf16[32,8,768]{2,1,0:T(8,128)(2,1)}), bf16[32,8,768]{2,1,0:T(8,128)(2,1)S(1)}, u32[]{:S(2)}, u32[]{:S(2)}) async-start(bf16[32,8,768]{2,1,0:T(8,128)(2,1)} %broadcast_in_dim.8), calls=%async_computation | async-start | bytes 786432 | tf_op jit(solution)/shard_map/all_to_all | solution.py:355
  26.8 15.5 %all-to-all-done = bf16[32,8,768]{2,1,0:T(8,128)(2,1)S(1)} async-done(((bf16[32,8,768]{2,1,0:T(8,128)(2,1)}), bf16[32,8,768]{2,1,0:T(8,128)(2,1)S(1)}, u32[]{:S(2)}, u32[]{:S(2)}) %all-to-all-start) | async-done | bytes 393248 | tf_op jit(solution)/shard_map/all_to_all | solution.py:355
  43.1 5.3 %all-to-all-start.1 = ((bf16[32,8,768]{2,1,0:T(8,128)(2,1)}), bf16[32,8,768]{2,1,0:T(8,128)(2,1)S(1)}, u32[]{:S(2)}, u32[]{:S(2)}) async-start(bf16[32,8,768]{2,1,0:T(8,128)(2,1)} %broadcast_in_dim.9), calls=%async_computation.1 | async-start | bytes 786432 | tf_op jit(solution)/shard_map/all_to_all | solution.py:355
  48.3 3.9 %collective-permute-start.5 = (bf16[256,768]{1,0:T(8,128)(2,1)S(1)}, bf16[256,768]{1,0:T(8,128)(2,1)S(1)}, u32[]{:S(2)}, u32[]{:S(2)}) collective-permute-start(bf16[256,768]{1,0:T(8,128)(2,1)S(1)} %bitcast.20), channel_id=1, source_target_pairs={{0,512},{512,0},{1,513},{513,1},{2,514},{514,2},{3,515},{515,3},{4... | collective-permute-start | bytes 1179656 | tf_op jit(solution)/shard_map/ppermute | solution.py:351
  52.3 1.9 %collective-permute-start.2 = (bf16[128,96]{1,0:T(8,128)(2,1)S(1)}, bf16[128,96]{1,0:T(8,128)(2,1)S(1)}, u32[]{:S(2)}, u32[]{:S(2)}) collective-permute-start(bf16[128,96]{1,0:T(8,128)(2,1)S(1)} %broadcast_select_fusion.2), channel_id=1, source_target_pairs={{0,512},{512,0},{1,513},{513,1},{2,514},{514,2},{3,515},{515,3},{4... | collective-permute-start | bytes 73736 | tf_op jit(solution)/shard_map/ppermute | solution.py:351
  54.5 1.9 %collective-permute-start = (bf16[256,768]{1,0:T(8,128)(2,1)S(1)}, bf16[256,768]{1,0:T(8,128)(2,1)S(1)}, u32[]{:S(2)}, u32[]{:S(2)}) collective-permute-start(bf16[256,768]{1,0:T(8,128)(2,1)S(1)} %bitcast.21), channel_id=1, source_target_pairs={{0,1},{1,0},{2,3},{3,2},{4,5},{5,4},{6,7},{7,6},{8,9},{9,8},{10,11... | collective-permute-start | bytes 1179656 | tf_op jit(solution)/shard_map/ppermute | solution.py:351
  56.4 12.2 %collective-permute-done.5.own1_ref = bf16[256,768]{1,0:T(8,128)(2,1)S(1)} collective-permute-done((bf16[256,768]{1,0:T(8,128)(2,1)S(1)}, bf16[256,768]{1,0:T(8,128)(2,1)S(1)}, u32[]{:S(2)}, u32[]{:S(2)}) %collective-permute-start.5) | collective-permute-done | bytes 393248 | tf_op jit(solution)/shard_map/ppermute | solution.py:351
  68.6 1.9 collective-permute-start.6
  73.2 3.5 %encode.3 = bf16[384,768]{1,0:T(8,128)(2,1)} custom-call(bf16[384,512]{1,0:T(8,128)(2,1)S(1)} %expand_hidden.2.mine_ref, bf16[384,512]{1,0:T(8,128)(2,1)S(1)} %expand_hidden.3.theirs_ref, bf16[256,768]{1,0:T(8,128)(2,1)S(1)} %bitcast.22, bf16[256,768]{1,0:T(8,128)(2,1)S(1)} %collective-permute-done.other0_ref, ...), custom_call_target="tpu_custom_call" | custom-call | flops 603979776 | bytes 4194304 | tf_op jit(solution)/shard_map/encode/pallas_call | solution.py:152
  76.7 6.8 %all-to-all-start.3 = ((bf16[8,48,768]{2,1,0:T(8,128)(2,1)}), bf16[8,48,768]{2,1,0:T(8,128)(2,1)S(1)}, u32[]{:S(2)}, u32[]{:S(2)}) async-start(bf16[8,48,768]{2,1,0:T(8,128)(2,1)} %bitcast.8), calls=%async_computation.3 | async-start | bytes 1179648 | tf_op jit(solution)/shard_map/all_to_all | solution.py:419
  83.5 2.4 %collective-permute-start.3 = (bf16[256,768]{1,0:T(8,128)(2,1)S(1)}, bf16[256,768]{1,0:T(8,128)(2,1)}, u32[]{:S(2)}, u32[]{:S(2)}) collective-permute-start(bf16[256,768]{1,0:T(8,128)(2,1)S(1)} %bitcast.24), channel_id=1, source_target_pairs={{0,512},{512,0},{1,513},{513,1},{2,514},{514,2},{3,515},{515,3},{4... | collective-permute-start | bytes 1179656 | tf_op jit(solution)/shard_map/ppermute | solution.py:351
  85.8 1.9 %collective-permute-start.1 = (bf16[256,768]{1,0:T(8,128)(2,1)S(1)}, bf16[256,768]{1,0:T(8,128)(2,1)}, u32[]{:S(2)}, u32[]{:S(2)}) collective-permute-start(bf16[256,768]{1,0:T(8,128)(2,1)S(1)} %bitcast.25), channel_id=1, source_target_pairs={{0,1},{1,0},{2,3},{3,2},{4,5},{5,4},{6,7},{7,6},{8,9},{9,8},{10,11... | collective-permute-start | bytes 1179656 | tf_op jit(solution)/shard_map/ppermute | solution.py:351
  87.8 8.9 %collective-permute-done.3.own1_ref = bf16[256,768]{1,0:T(8,128)(2,1)} collective-permute-done((bf16[256,768]{1,0:T(8,128)(2,1)S(1)}, bf16[256,768]{1,0:T(8,128)(2,1)}, u32[]{:S(2)}, u32[]{:S(2)}) %collective-permute-start.3) | collective-permute-done | bytes 393248 | tf_op jit(solution)/shard_map/ppermute | solution.py:351
  96.7 1.9 collective-permute-start.4
  99.0 1.6 collective-permute-done.4.other1_ref
  100.7 3.6 %encode.2 = bf16[384,768]{1,0:T(8,128)(2,1)} custom-call(bf16[384,512]{1,0:T(8,128)(2,1)S(1)} %expand_hidden.2.mine_ref, bf16[384,512]{1,0:T(8,128)(2,1)S(1)} %expand_hidden.3.theirs_ref, bf16[256,768]{1,0:T(8,128)(2,1)S(1)} %bitcast.26, bf16[256,768]{1,0:T(8,128)(2,1)} %collective-permute-done.1.other1_ref.other0_ref, ...), custom_call_target="tpu_custom_call" | custom-call | flops 603979776 | bytes 4194304 | tf_op jit(solution)/shard_map/encode/pallas_call | solution.py:152
  104.3 7.1 %all-to-all-start.2 = ((bf16[8,48,768]{2,1,0:T(8,128)(2,1)}), bf16[8,48,768]{2,1,0:T(8,128)(2,1)S(1)}, u32[]{:S(2)}, u32[]{:S(2)}) async-start(bf16[8,48,768]{2,1,0:T(8,128)(2,1)} %bitcast.6), calls=%async_computation.2 | async-start | bytes 1179648 | tf_op jit(solution)/shard_map/all_to_all | solution.py:419
  112.1 1.0 constant_dynamic-slice_fusion.weight_ref
  114.6 1.2 update_0.1
  115.9 14.7 %all-to-all-done.2.received_ref = bf16[8,48,768]{2,1,0:T(8,128)(2,1)S(1)} async-done(((bf16[8,48,768]{2,1,0:T(8,128)(2,1)}), bf16[8,48,768]{2,1,0:T(8,128)(2,1)S(1)}, u32[]{:S(2)}, u32[]{:S(2)}) %all-to-all-start.2) | async-done | bytes 589856 | tf_op jit(solution)/shard_map/all_to_all | solution.py:419
  131.4 3.5 %all-to-all-start.4 = ((bf16[8,48,768]{2,1,0:T(8,128)(2,1)}), bf16[8,48,768]{2,1,0:T(8,128)(2,1)S(1)}, u32[]{:S(2)}, u32[]{:S(2)}) async-start(bf16[8,48,768]{2,1,0:T(8,128)(2,1)} %broadcast_in_dim.10), calls=%async_computation.4 | async-start | bytes 1179648 | tf_op jit(solution)/shard_map/all_to_all | solution.py:355
  135.0 1.3 update_1.1
  136.2 18.0 %all-to-all-done.4.own_ref = bf16[8,48,768]{2,1,0:T(8,128)(2,1)S(1)} async-done(((bf16[8,48,768]{2,1,0:T(8,128)(2,1)}), bf16[8,48,768]{2,1,0:T(8,128)(2,1)S(1)}, u32[]{:S(2)}, u32[]{:S(2)}) %all-to-all-start.4) | async-done | bytes 589856 | tf_op jit(solution)/shard_map/all_to_all | solution.py:355
  154.3 1.1 broadcast_in_dim.11
  155.3 3.7 %all-to-all-start.5 = ((bf16[16,48,768]{2,1,0:T(8,128)(2,1)}), bf16[16,48,768]{2,1,0:T(8,128)(2,1)S(1)}, u32[]{:S(2)}, u32[]{:S(2)}) async-start(bf16[16,48,768]{2,1,0:T(8,128)(2,1)} %broadcast_in_dim.11), calls=%async_computation.5 | async-start | bytes 2359296 | tf_op jit(solution)/shard_map/all_to_all | solution.py:355
  159.2 3.9 %collective-permute-start.7 = (bf16[8,48,768]{2,1,0:T(8,128)(2,1)S(1)}, bf16[8,48,768]{2,1,0:T(8,128)(2,1)S(1)}, u32[]{:S(2)}, u32[]{:S(2)}) collective-permute-start(bf16[8,48,768]{2,1,0:T(8,128)(2,1)S(1)} %all-to-all-done.4.own_ref), channel_id=1, source_target_pairs={{0,512},{512,0},{1,513},{513,1},{2,514},{514,2},{3,515},{515,3},{4... | collective-permute-start | bytes 1769480 | tf_op jit(solution)/shard_map/ppermute | solution.py:351
  163.1 1.7 copy-done.15
  164.7 2.4 %rotate_weight.1.w_ref = bf16[192,6144]{1,0:T(8,128)(2,1)S(1)} custom-call(bf16[192,6144]{1,0:T(8,128)(2,1)S(1)} %copy-done.15, f32[1,6144]{1,0:T(1,128)S(1)} %bitcast.31, bf16[128,128]{1,0:T(8,128)(2,1)S(1)} %copy-done.13), custom_call_target="tpu_custom_call" | custom-call | flops 2415919104 | bytes 5242880 | tf_op jit(solution)/shard_map/rotate_weight/pallas_call | solution.py:288
  167.2 3.4 %pre_grad.1 = bf16[128,192]{1,0:T(8,128)(2,1)S(1)} custom-call(bf16[256,768]{1,0:T(8,128)(2,1)S(1)} %bitcast.23, bf16[256,768]{1,0:T(8,128)(2,1)S(1)} %copy-done.9, bf16[256,768]{1,0:T(8,128)(2,1)S(1)} %bitcast.27, bf16[256,768]{1,0:T(8,128)(2,1)} %collective-permute-done.1.other1_ref.other0_ref, bf16[192,6144]{1,0:T(8,128)(2,1)S(1)} %rotate_weight.1.w_ref, ...), custom_call_target="tpu_custom_call" | custom-call | flops 1207959552 | bytes 6291456 | tf_op jit(solution)/shard_map/pre_grad/pallas_call | solution.py:338
  171.6 14.8 %collective-permute-done.7.other_ref = bf16[8,48,768]{2,1,0:T(8,128)(2,1)S(1)} collective-permute-done((bf16[8,48,768]{2,1,0:T(8,128)(2,1)S(1)}, bf16[8,48,768]{2,1,0:T(8,128)(2,1)S(1)}, u32[]{:S(2)}, u32[]{:S(2)}) %collective-permute-start.7) | collective-permute-done | bytes 589856 | tf_op jit(solution)/shard_map/ppermute | solution.py:351
  186.4 2.9 %all-to-all-done.5.direct_ref = bf16[16,48,768]{2,1,0:T(8,128)(2,1)S(1)} async-done(((bf16[16,48,768]{2,1,0:T(8,128)(2,1)}), bf16[16,48,768]{2,1,0:T(8,128)(2,1)S(1)}, u32[]{:S(2)}, u32[]{:S(2)}) %all-to-all-start.5) | async-done | bytes 1179680 | tf_op jit(solution)/shard_map/all_to_all | solution.py:355
  189.4 2.0 %place.1 = bf16[192,6144]{1,0:T(8,128)(2,1)} custom-call(s32[1]{0:T(128)} %bitcast.9.plane_ref, bf16[8,48,768]{2,1,0:T(8,128)(2,1)S(1)} %all-to-all-done.4.own_ref, bf16[8,48,768]{2,1,0:T(8,128)(2,1)S(1)} %collective-permute-done.7.other_ref, bf16[16,48,768]{2,1,0:T(8,128)(2,1)S(1)} %all-to-all-done.5.direct_ref), custom_call_target="tpu_custom_call" | custom-call | tf_op jit(solution)/shard_map/place/pallas_call | solution.py:262
  (82 shorter events, 12.3 us)
Async XLA Ops:
  0.6 53.7 %copy-start.19 = (s32[192,6]{0,1:T(8,128)S(1)}, s32[192,6]{0,1:T(8,128)}, u32[]{:S(2)}) copy-start(s32[192,6]{0,1:T(8,128)} %param.17) | copy-start | bytes 13828
  1.4 1.7 copy-start.5
  1.4 0.8 copy-start.12
  3.1 68.3 %copy-start = (bf16[384,512]{1,0:T(8,128)(2,1)S(1)}, bf16[384,512]{1,0:T(8,128)(2,1)}, u32[]{:S(2)}) copy-start(bf16[384,512]{1,0:T(8,128)(2,1)} %constant.52.clone.same_ref) | copy-start | bytes 1179652
  3.1 68.2 %copy-start.3 = (bf16[128,512]{1,0:T(8,128)(2,1)S(1)}, bf16[128,512]{1,0:T(8,128)(2,1)}, u32[]{:S(2)}) copy-start(bf16[128,512]{1,0:T(8,128)(2,1)} %constant.51.clone.collect_ref.widen_ref) | copy-start | bytes 393220
  3.1 68.2 %copy-start.10 = (bf16[384,96]{1,0:T(8,128)(2,1)S(1)}, bf16[384,96]{1,0:T(8,128)(2,1)}, u32[]{:S(2)}) copy-start(bf16[384,96]{1,0:T(8,128)(2,1)} %constant.50.clone.spread_ref) | copy-start | bytes 221188
  3.9 38.4 %all-to-all-start = ((bf16[32,8,768]{2,1,0:T(8,128)(2,1)}), bf16[32,8,768]{2,1,0:T(8,128)(2,1)S(1)}, u32[]{:S(2)}, u32[]{:S(2)}) async-start(bf16[32,8,768]{2,1,0:T(8,128)(2,1)} %broadcast_in_dim.8), calls=%async_computation | async-start | bytes 786432 | tf_op jit(solution)/shard_map/all_to_all | solution.py:355
  26.8 44.3 %copy-start.16 = (bf16[128,192]{1,0:T(8,128)(2,1)}, bf16[128,192]{1,0:T(8,128)(2,1)S(1)}, u32[]{:S(2)}) copy-start(bf16[128,192]{1,0:T(8,128)(2,1)S(1)} %constant_dynamic-update-slice_fusion) | copy-start | bytes 147460
  43.1 33.6 %all-to-all-start.1 = ((bf16[32,8,768]{2,1,0:T(8,128)(2,1)}), bf16[32,8,768]{2,1,0:T(8,128)(2,1)S(1)}, u32[]{:S(2)}, u32[]{:S(2)}) async-start(bf16[32,8,768]{2,1,0:T(8,128)(2,1)} %broadcast_in_dim.9), calls=%async_computation.1 | async-start | bytes 786432 | tf_op jit(solution)/shard_map/all_to_all | solution.py:355
  48.3 20.3 %collective-permute-start.5 = (bf16[256,768]{1,0:T(8,128)(2,1)S(1)}, bf16[256,768]{1,0:T(8,128)(2,1)S(1)}, u32[]{:S(2)}, u32[]{:S(2)}) collective-permute-start(bf16[256,768]{1,0:T(8,128)(2,1)S(1)} %bitcast.20), channel_id=1, source_target_pairs={{0,512},{512,0},{1,513},{513,1},{2,514},{514,2},{3,515},{515,3},{4... | collective-permute-start | bytes 1179656 | tf_op jit(solution)/shard_map/ppermute | solution.py:351
  52.3 19.5 %collective-permute-start.2 = (bf16[128,96]{1,0:T(8,128)(2,1)S(1)}, bf16[128,96]{1,0:T(8,128)(2,1)S(1)}, u32[]{:S(2)}, u32[]{:S(2)}) collective-permute-start(bf16[128,96]{1,0:T(8,128)(2,1)S(1)} %broadcast_select_fusion.2), channel_id=1, source_target_pairs={{0,512},{512,0},{1,513},{513,1},{2,514},{514,2},{3,515},{515,3},{4... | collective-permute-start | bytes 73736 | tf_op jit(solution)/shard_map/ppermute | solution.py:351
  54.4 16.7 %copy-start.18 = (f32[192,6]{1,0:T(8,128)}, f32[192,6]{1,0:T(8,128)S(1)}, u32[]{:S(2)}) copy-start(f32[192,6]{1,0:T(8,128)S(1)} %convert_element_type.27) | copy-start | bytes 13828
  54.5 18.7 %collective-permute-start = (bf16[256,768]{1,0:T(8,128)(2,1)S(1)}, bf16[256,768]{1,0:T(8,128)(2,1)S(1)}, u32[]{:S(2)}, u32[]{:S(2)}) collective-permute-start(bf16[256,768]{1,0:T(8,128)(2,1)S(1)} %bitcast.21), channel_id=1, source_target_pairs={{0,1},{1,0},{2,3},{3,2},{4,5},{5,4},{6,7},{7,6},{8,9},{9,8},{10,11... | collective-permute-start | bytes 1179656 | tf_op jit(solution)/shard_map/ppermute | solution.py:351
  68.6 4.5 %collective-permute-start.6 = (bf16[256,768]{1,0:T(8,128)(2,1)S(1)}, bf16[256,768]{1,0:T(8,128)(2,1)}, u32[]{:S(2)}, u32[]{:S(2)}) collective-permute-start(bf16[256,768]{1,0:T(8,128)(2,1)S(1)} %collective-permute-done.5.own1_ref), channel_id=1, source_target_pairs={{0,1},{1,0},{2,3},{3,2},{4,5},{5,4},{6,7},{7,6},{8,9},{9,8},{10,11... | collective-permute-start | bytes 1179656 | tf_op jit(solution)/shard_map/ppermute | solution.py:351
  71.8 0.9 copy-start.11
  73.2 3.5 %copy-start.8 = (bf16[256,768]{1,0:T(8,128)(2,1)}, bf16[256,768]{1,0:T(8,128)(2,1)S(1)}, u32[]{:S(2)}) copy-start(bf16[256,768]{1,0:T(8,128)(2,1)S(1)} %collective-permute-done.other0_ref) | copy-start | bytes 1179652
  76.7 27.6 %all-to-all-start.3 = ((bf16[8,48,768]{2,1,0:T(8,128)(2,1)}), bf16[8,48,768]{2,1,0:T(8,128)(2,1)S(1)}, u32[]{:S(2)}, u32[]{:S(2)}) async-start(bf16[8,48,768]{2,1,0:T(8,128)(2,1)} %bitcast.8), calls=%async_computation.3 | async-start | bytes 1179648 | tf_op jit(solution)/shard_map/all_to_all | solution.py:419
  83.5 13.2 %collective-permute-start.3 = (bf16[256,768]{1,0:T(8,128)(2,1)S(1)}, bf16[256,768]{1,0:T(8,128)(2,1)}, u32[]{:S(2)}, u32[]{:S(2)}) collective-permute-start(bf16[256,768]{1,0:T(8,128)(2,1)S(1)} %bitcast.24), channel_id=1, source_target_pairs={{0,512},{512,0},{1,513},{513,1},{2,514},{514,2},{3,515},{515,3},{4... | collective-permute-start | bytes 1179656 | tf_op jit(solution)/shard_map/ppermute | solution.py:351
  85.8 13.2 %collective-permute-start.1 = (bf16[256,768]{1,0:T(8,128)(2,1)S(1)}, bf16[256,768]{1,0:T(8,128)(2,1)}, u32[]{:S(2)}, u32[]{:S(2)}) collective-permute-start(bf16[256,768]{1,0:T(8,128)(2,1)S(1)} %bitcast.25), channel_id=1, source_target_pairs={{0,1},{1,0},{2,3},{3,2},{4,5},{5,4},{6,7},{7,6},{8,9},{9,8},{10,11... | collective-permute-start | bytes 1179656 | tf_op jit(solution)/shard_map/ppermute | solution.py:351
  96.7 3.9 %collective-permute-start.4 = (bf16[256,768]{1,0:T(8,128)(2,1)}, bf16[256,768]{1,0:T(8,128)(2,1)}, u32[]{:S(2)}, u32[]{:S(2)}) collective-permute-start(bf16[256,768]{1,0:T(8,128)(2,1)} %collective-permute-done.3.own1_ref), channel_id=1, source_target_pairs={{0,1},{1,0},{2,3},{3,2},{4,5},{5,4},{6,7},{7,6},{8,9},{9,8},{10,11... | collective-permute-start | bytes 1179656 | tf_op jit(solution)/shard_map/ppermute | solution.py:351
  99.0 14.1 %copy-start.1 = (f32[12,6144]{1,0:T(8,128)S(1)}, f32[12,6144]{1,0:T(8,128)}, u32[]{:S(2)}) copy-start(f32[12,6144]{1,0:T(8,128)} %first_ref.3) | copy-start | bytes 884740
  99.0 14.1 %copy-start.2 = (f32[12,6144]{1,0:T(8,128)S(1)}, f32[12,6144]{1,0:T(8,128)}, u32[]{:S(2)}) copy-start(f32[12,6144]{1,0:T(8,128)} %second_ref.3) | copy-start | bytes 884740
  104.3 30.7 %copy-start.7 = (f32[6144]{0:T(1024)S(1)}, f32[6144]{0:T(1024)}, u32[]{:S(2)}) copy-start(f32[6144]{0:T(1024)} %copy-done.5) | copy-start | bytes 73732
  104.3 26.3 %all-to-all-start.2 = ((bf16[8,48,768]{2,1,0:T(8,128)(2,1)}), bf16[8,48,768]{2,1,0:T(8,128)(2,1)S(1)}, u32[]{:S(2)}, u32[]{:S(2)}) async-start(bf16[8,48,768]{2,1,0:T(8,128)(2,1)} %bitcast.6), calls=%async_computation.2 | async-start | bytes 1179648 | tf_op jit(solution)/shard_map/all_to_all | solution.py:419
  113.8 0.8 copy-start.13
  131.4 22.8 %all-to-all-start.4 = ((bf16[8,48,768]{2,1,0:T(8,128)(2,1)}), bf16[8,48,768]{2,1,0:T(8,128)(2,1)S(1)}, u32[]{:S(2)}, u32[]{:S(2)}) async-start(bf16[8,48,768]{2,1,0:T(8,128)(2,1)} %broadcast_in_dim.10), calls=%async_computation.4 | async-start | bytes 1179648 | tf_op jit(solution)/shard_map/all_to_all | solution.py:355
  136.2 22.8 %copy-start.17 = (bf16[128,192]{1,0:T(8,128)(2,1)S(1)}, bf16[128,192]{1,0:T(8,128)(2,1)}, u32[]{:S(2)}) copy-start(bf16[128,192]{1,0:T(8,128)(2,1)} %copy-done.16) | copy-start | bytes 147460
  155.3 34.0 %all-to-all-start.5 = ((bf16[16,48,768]{2,1,0:T(8,128)(2,1)}), bf16[16,48,768]{2,1,0:T(8,128)(2,1)S(1)}, u32[]{:S(2)}, u32[]{:S(2)}) async-start(bf16[16,48,768]{2,1,0:T(8,128)(2,1)} %broadcast_in_dim.11), calls=%async_computation.5 | async-start | bytes 2359296 | tf_op jit(solution)/shard_map/all_to_all | solution.py:355
  159.1 8.0 %copy-start.4 = (bf16[128,512]{1,0:T(8,128)(2,1)S(1)}, bf16[128,512]{1,0:T(8,128)(2,1)}, u32[]{:S(2)}) copy-start(bf16[128,512]{1,0:T(8,128)(2,1)} %constant.51.clone.collect_ref.widen_ref) | copy-start | bytes 393220
  159.1 8.0 %copy-start.9 = (bf16[256,768]{1,0:T(8,128)(2,1)S(1)}, bf16[256,768]{1,0:T(8,128)(2,1)}, u32[]{:S(2)}) copy-start(bf16[256,768]{1,0:T(8,128)(2,1)} %copy-done.8) | copy-start | bytes 1179652
  159.2 27.3 %collective-permute-start.7 = (bf16[8,48,768]{2,1,0:T(8,128)(2,1)S(1)}, bf16[8,48,768]{2,1,0:T(8,128)(2,1)S(1)}, u32[]{:S(2)}, u32[]{:S(2)}) collective-permute-start(bf16[8,48,768]{2,1,0:T(8,128)(2,1)S(1)} %all-to-all-done.4.own_ref), channel_id=1, source_target_pairs={{0,512},{512,0},{1,513},{513,1},{2,514},{514,2},{3,515},{515,3},{4... | collective-permute-start | bytes 1769480 | tf_op jit(solution)/shard_map/ppermute | solution.py:351
  163.0 1.7 copy-start.15
  (2 other events, 1.5 us)

commit v3 on v2

--- a/solution.py
+++ b/solution.py
@@ -24,7 +24,6 @@
 BLOCKS = 3
 TOK = 128
 LINE = 8
-SHARE = LINE * OWN
 PEERS = 32
 LANES = 128
 TILE = 256
@@ -42,9 +41,9 @@
 
 
 def tables():
-    row = np.arange(LINE * SEGS * OWN)
+    row = np.arange(REPLICAS * SEGS * OWN)
     owner, segment, own = row // (SEGS * OWN), row % (SEGS * OWN) // OWN, row % OWN
-    spread = (owner * OWN + own)[:, None] == np.arange(SHARE)[None, :]
+    spread = (owner * OWN + own)[:, None] == np.arange(ROWS)[None, :]
     col = np.arange(2 * PEERS * SEGS * 2)
     patch = col // (SEGS * 2) * 2 + col % 2
     col_segment = col % (SEGS * 2) // 2
@@ -73,33 +72,31 @@
     return pltpu.CompilerParams(vmem_limit_bytes=mebibytes << 20)
 
 
-def rotate_upstream_kernel(u_ref, sign_ref, had_ref, low_ref, high_ref, x_ref, z_ref):
+def rotate_upstream_kernel(u_ref, sign_ref, had_ref, out_ref, x_ref, z_ref):
     turned = u_ref[...].astype(f32) * sign_ref[...]
     for t in range(COLS // LANES):
         x_ref[2 * t : 2 * t + 2, :] = turned[:, LANES * t : LANES * (t + 1)]
     x_ref[...] = jnp.dot(
         x_ref[...].astype(bf16), had_ref[...], preferred_element_type=f32
     )
-    for half, out_ref in enumerate((low_ref, high_ref)):
+    for half in range(2):
         for b in range(BLOCKS):
             base = half * HALF // LANES + 8 * b
             mixed = butterfly([x_ref[2 * t : 2 * t + 2, :] for t in range(base, base + 8)])
             for k, part in enumerate(mixed):
                 s, lane = divmod(8 * b + k, SEG // LANES)
-                z_ref[2 * s : 2 * s + 2, LANES * lane : LANES * (lane + 1)] = (
-                    part * hadamard_norm
-                )
-        out_ref[...] = z_ref[...].astype(bf16)
+                start = half * SEG + LANES * lane
+                z_ref[2 * s : 2 * s + 2, start : start + LANES] = part * hadamard_norm
+    out_ref[...] = z_ref[...].astype(bf16)
 
 
 def rotate_upstream(upstream, sign_row, had):
-    part = jax.ShapeDtypeStruct((2 * SEGS, SEG), bf16)
     return pl.pallas_call(
         rotate_upstream_kernel,
-        out_shape=(part, part),
+        out_shape=jax.ShapeDtypeStruct((2 * SEGS, 2 * SEG), bf16),
         scratch_shapes=[
             pltpu.VMEM((2 * COLS // LANES, LANES), f32),
-            pltpu.VMEM((2 * SEGS, SEG), f32),
+            pltpu.VMEM((2 * SEGS, 2 * SEG), f32),
         ],
         compiler_params=params(),
         name="rotate_upstream",
@@ -129,50 +126,49 @@
     )(hidden, spread, widen, same)
 
 
-def encode_kernel(
-    mine_ref, theirs_ref, own0_ref, other0_ref, own1_ref, other1_ref, scale_ref, out_ref
-):
-    total = None
-    for left_ref, own_ref, other_ref in (
-        (mine_ref, own0_ref, other0_ref),
-        (theirs_ref, own1_ref, other1_ref),
-    ):
-        half = own_ref.shape[0]
-        term = jnp.dot(left_ref[:, :half], own_ref[...], preferred_element_type=f32)
-        term += jnp.dot(left_ref[:, half:], other_ref[...], preferred_element_type=f32)
-        term = jnp.clip(term * scale_ref[0], -clip_limit, clip_limit)
-        term = term.astype(bf16).astype(f32)
-        total = term if total is None else total + term
-    out_ref[...] = total.astype(bf16)
-
-
-def encode(mine, theirs, parts, scale):
-    rows = mine.shape[0]
-    depth = parts[0].shape[0]
-    return pl.pallas_call(
-        encode_kernel,
+def encode_kernel(by_line, left_ref, own_ref, other_ref, scale_ref, out_ref):
+    half = own_ref.shape[0]
+    total = jnp.dot(left_ref[:, :half], own_ref[...], preferred_element_type=f32)
+    total += jnp.dot(left_ref[:, half:], other_ref[...], preferred_element_type=f32)
+    total = jnp.clip(total * scale_ref[0], -clip_limit, clip_limit).astype(bf16)
+    step = SEGS * OWN
+    for d in range(REPLICAS):
+        to = d % LINE * 2 + d // LINE if by_line else d
+        out_ref[step * to : step * (to + 1), :] = total[step * d : step * (d + 1), :]
+
+
+def encode(half, by_line, left, own, other, scale):
+    rows = left.shape[0]
+    depth = own.shape[0]
+    tiles = SEG // TILE
+    return pl.pallas_call(
+        functools.partial(encode_kernel, by_line),
         out_shape=jax.ShapeDtypeStruct((rows, SEG), bf16),
-        grid=(SEG // TILE,),
-        in_specs=[whole(mine.shape), whole(theirs.shape)]
-        + [pl.BlockSpec((depth, TILE), lambda n: (0, n))] * 4
-        + [pl.BlockSpec((1, rows, 1), lambda n: (n, 0, 0))],
+        grid=(tiles,),
+        in_specs=[
+            whole(left.shape),
+            pl.BlockSpec((depth, TILE), lambda n: (0, half * tiles + n)),
+            pl.BlockSpec((depth, TILE), lambda n: (0, half * tiles + n)),
+            pl.BlockSpec((1, rows, 1), lambda n: (n, 0, 0)),
+        ],
         out_specs=pl.BlockSpec((rows, TILE), lambda n: (0, n)),
         compiler_params=params(12),
         cost_estimate=pl.CostEstimate(
-            flops=8 * rows * depth * SEG, bytes_accessed=4 << 20, transcendentals=0
-        ),
-        name="encode",
-    )(mine, theirs, *parts, scale)
+            flops=4 * rows * depth * SEG, bytes_accessed=4 << 20, transcendentals=0
+        ),
+        name=f"encode_{half}",
+    )(left, own, other, scale)
 
 
 def update_kernel(
-    half, received_ref, power_ref, sign_ref, had_ref, first_ref, second_ref,
-    weight_ref, *refs,
+    half, count, power_ref, sign_ref, had_ref, first_ref, second_ref, weight_ref, *refs
 ):
     mean_ref, first_out, second_out, sent_ref, sum_ref, x_ref, y_ref = refs[-7:]
-    total = received_ref[0].astype(f32)
-    for source in range(1, received_ref.shape[0]):
-        total += received_ref[source].astype(f32)
+    total = None
+    for received_ref in refs[:count]:
+        for source in range(received_ref.shape[0]):
+            term = received_ref[source].astype(f32)
+            total = term if total is None else total + term
     sum_ref[...] = total
     x_ref[...] = jnp.zeros_like(x_ref)
     for t in range(HALF // LANES):
@@ -218,11 +214,10 @@
 
     kept = [pl.BlockSpec(memory_space=pl.ANY)] * len(earlier)
     return pl.pallas_call(
-        functools.partial(update_kernel, half),
+        functools.partial(update_kernel, half, len(received)),
         out_shape=(own, own, own, sent),
         grid=(1,),
         in_specs=[
-            whole(received.shape),
             whole(power.shape),
             part(1),
             whole(had.shape),
@@ -230,6 +225,7 @@
             part(OWN),
             part(OWN),
         ]
+        + [whole(array.shape) for array in received]
         + kept,
         out_specs=(part(OWN), part(OWN), part(OWN), whole(sent.shape)),
         scratch_shapes=[
@@ -237,37 +233,40 @@
             pltpu.VMEM((16 * HALF // LANES, LANES), f32),
             pltpu.VMEM((16 * HALF // LANES, LANES), f32),
         ],
-        input_output_aliases={7 + k: k for k in range(len(earlier))},
+        input_output_aliases={6 + len(received) + k: k for k in range(len(earlier))},
         compiler_params=params(),
         name=f"update_{half}",
-    )(received, power, sign_row, had, first, second, weight, *earlier)
-
-
-def place_kernel(plane_ref, own_ref, other_ref, direct_ref, out_ref, rows_ref):
-    plane = plane_ref[0]
+    )(power, sign_row, had, first, second, weight, *received, *earlier)
+
+
+def place_kernel(by_line, chunks_ref, *refs):
+    out_ref, rows_ref = refs[-2:]
     for d in range(REPLICAS):
-        here = plane == d // LINE
-        near = jnp.where(here, own_ref[d % LINE], other_ref[d % LINE]).astype(f32)
-        far = direct_ref[d].astype(f32)
-        for half, chunk in enumerate((near, far)):
-            for s in range(SEGS):
-                start = half * HALF + SEG * s
-                rows_ref[OWN * d : OWN * (d + 1), start : start + SEG] = chunk[
-                    OWN * s : OWN * (s + 1), :
-                ]
+        source = d % LINE * 2 + d // LINE if by_line else d
+        chunk = chunks_ref[source].astype(f32)
+        for s in range(SEGS):
+            rows_ref[OWN * d : OWN * (d + 1), SEG * s : SEG * (s + 1)] = chunk[
+                OWN * s : OWN * (s + 1), :
+            ]
     out_ref[...] = rows_ref[...].astype(bf16)
 
 
-def place(plane, own, other, direct):
-    return pl.pallas_call(
-        place_kernel,
+def place(half, by_line, chunks, earlier, flops):
+    return pl.pallas_call(
+        functools.partial(place_kernel, by_line),
         out_shape=jax.ShapeDtypeStruct((ROWS, COLS), bf16),
-        in_specs=[pl.BlockSpec(memory_space=pltpu.SMEM)]
-        + [pl.BlockSpec(memory_space=pltpu.VMEM)] * 3,
-        scratch_shapes=[pltpu.VMEM((ROWS, COLS), f32)],
-        compiler_params=params(20),
-        name="place",
-    )(plane, own, other, direct)
+        grid=(1,),
+        in_specs=[whole(chunks.shape)]
+        + [pl.BlockSpec(memory_space=pl.ANY)] * len(earlier),
+        out_specs=pl.BlockSpec((ROWS, HALF), lambda _: (0, half)),
+        scratch_shapes=[pltpu.VMEM((ROWS, HALF), f32)],
+        input_output_aliases={1 + k: k for k in range(len(earlier))},
+        compiler_params=params(12),
+        cost_estimate=pl.CostEstimate(
+            flops=flops, bytes_accessed=3 << 20, transcendentals=0
+        ),
+        name=f"place_{half}",
+    )(chunks, *earlier)
 
 
 def rotate_weight_kernel(w_ref, sign_ref, had_ref, out_ref):
@@ -303,16 +302,13 @@
     )(weight, sign_row, had)
 
 
-def pre_grad_kernel(
-    own0_ref, other0_ref, own1_ref, other1_ref, w_ref, slope_ref, collect_ref,
-    out_ref, acc_ref,
-):
-    rows = own0_ref.shape[0]
+def pre_grad_kernel(own_ref, other_ref, w_ref, slope_ref, collect_ref, out_ref, acc_ref):
+    rows = own_ref.shape[0]
     place_in_pair = lax.broadcasted_iota(jnp.int32, (rows, 1), 0) & (2 * SEGS - 1)
-    for index, refs in enumerate(((own0_ref, own1_ref), (other0_ref, other1_ref))):
+    for index, rows_ref in enumerate((own_ref, other_ref)):
         total = None
-        for half, rows_ref in enumerate(refs):
-            left = rows_ref[...]
+        for half in range(2):
+            left = rows_ref[:, SEG * half : SEG * (half + 1)]
             chosen = jnp.zeros((rows, ROWS), f32)
             for s in range(SEGS):
                 column = half * HALF + SEG * s
@@ -334,17 +330,17 @@
     out_ref[...] = (hidden_grad * slope_ref[...]).astype(bf16)
 
 
-def pre_grad_product(own0, other0, own1, other1, weight, slope, collect):
+def pre_grad_product(own, other, weight, slope, collect):
     return pl.pallas_call(
         pre_grad_kernel,
         out_shape=jax.ShapeDtypeStruct((TOK, ROWS), bf16),
-        scratch_shapes=[pltpu.VMEM((2 * own0.shape[0], ROWS), f32)],
+        scratch_shapes=[pltpu.VMEM((2 * own.shape[0], ROWS), f32)],
         compiler_params=params(16),
         cost_estimate=pl.CostEstimate(
             flops=8 * 512 * 1536 * ROWS, bytes_accessed=6 << 20, transcendentals=0
         ),
         name="pre_grad",
-    )(own0, other0, own1, other1, weight, slope, collect)
+    )(own, other, weight, slope, collect)
 
 
 def swap(values, axis):
@@ -363,42 +359,27 @@
     sign_row = (1 - 2 * signs).astype(f32).reshape(1, COLS)
     core = lax.axis_index("core")
     plane = lax.axis_index("z_lo")
-    plane_array = plane.astype(jnp.int32).reshape(1)
+
+    rotated = rotate_upstream(upstream, sign_row, had)
+    own = to_all(rotated, ("z_hi", "y"), PEERS).reshape(-1, 2 * SEG)
+    other = swap(own, "core")
 
     pairs = pre_act.reshape(PEERS, 2, 2, ROWS)
     mine = jnp.where(core == 0, pairs[:, 0], pairs[:, 1]).reshape(TOK // 2, ROWS)
     yours = jnp.where(core == 0, pairs[:, 1], pairs[:, 0]).reshape(TOK // 2, ROWS)
-    ordered = jnp.concatenate([mine, yours], axis=0)
-    kept = jnp.where(plane == 0, ordered[:, :SHARE], ordered[:, SHARE:])
-    given = jnp.where(plane == 0, ordered[:, SHARE:], ordered[:, :SHARE])
-    taken = swap(given, "z_lo")
-
-    rotated = rotate_upstream(upstream, sign_row, had)
-    own = [to_all(part, ("z_hi", "y"), PEERS).reshape(-1, SEG) for part in rotated]
-    other = [swap(part, "core") for part in own]
-    partner = [swap(part, "z_lo") for part in own]
-    partner_other = [swap(part, "core") for part in partner]
-
-    preact = ordered.astype(f32)
+    preact = jnp.concatenate([mine, yours], axis=0).astype(f32)
     normal_cdf = 0.5 * (1.0 + lax.erf(preact * root_half))
+    hidden = (preact * normal_cdf).astype(bf16)
     slope = normal_cdf + preact * jnp.exp(-0.5 * preact * preact) * density_norm
-
-    def activate(values):
-        values = values.astype(f32)
-        return (values * (0.5 * (1.0 + lax.erf(values * root_half)))).astype(bf16)
-
-    left = [
-        expand_hidden(activate(values), spread, widen, same)
-        for values in (kept, taken)
-    ]
+    left = expand_hidden(hidden, spread, widen, same)
 
     scale_power = exponents.astype(f32)
-    shrink = jnp.exp2(-jnp.where(plane == 0, scale_power[:SHARE], scale_power[SHARE:]))
+    shrink = jnp.exp2(-scale_power)
     offset = lax.axis_index(("z_lo", "x")) * OWN
     own_power = jnp.exp2(lax.dynamic_slice_in_dim(scale_power, offset, OWN, 0))
     own_weight = lax.dynamic_slice_in_dim(w_down, offset, OWN, 0)
 
-    received = []
+    encoded = []
     for half in range(2):
         picked = jnp.stack(
             [
@@ -409,35 +390,41 @@
             axis=0,
         )
         scale = (
-            picked.reshape(SEG // TILE, SEGS, LINE, OWN)
+            picked.reshape(SEG // TILE, SEGS, REPLICAS, OWN)
             .transpose(0, 2, 1, 3)
-            .reshape(SEG // TILE, LINE * SEGS * OWN, 1)
+            .reshape(SEG // TILE, REPLICAS * SEGS * OWN, 1)
         )
-        parts = (own[half], other[half], partner[half], partner_other[half])
-        encoded = encode(left[0], left[1], parts, scale)
-        received.append(
-            lax.all_to_all(
-                encoded.reshape(LINE, SEGS * OWN, SEG), "x", 0, 0, tiled=True
-            )
-        )
-
+        encoded.append(encode(half, half == 0, left, own, other, scale))
+
+    along = lax.psum_scatter(encoded[0], "x", scatter_dimension=0, tiled=True)
+    terms = lax.all_to_all(
+        encoded[1].reshape(REPLICAS, SEGS * OWN, SEG), ("z_lo", "x"), 0, 0, tiled=True
+    )
     states = (sign_row, had, first_moment, second_moment, own_weight)
-    *earlier, sent0 = update(0, received[0], own_power, *states, ())
-    near = to_all(sent0, "x", LINE)
-    across = swap(near, "z_lo")
-    *updated, sent1 = update(1, received[1], own_power, *states, earlier)
-    direct = to_all(sent1, ("z_lo", "x"), REPLICAS)
-
+    *earlier, sent1 = update(1, [terms], own_power, *states, ())
+    across = swap(sent1, "z_lo")
+    both = jnp.where(
+        plane == 0,
+        jnp.concatenate([sent1, across], axis=0),
+        jnp.concatenate([across, sent1], axis=0),
+    )
     turned_weight = rotate_weight(w_down, sign_row, had)
-    mixed = pre_grad_product(
-        own[0], other[0], own[1], other[1], turned_weight, slope, widen
-    )
+    mixed = pre_grad_product(own, other, turned_weight, slope, widen)
     halves = mixed.reshape(2, PEERS, 2, ROWS)
     zero = jnp.where(core == 0, halves[0], halves[1])
     one = jnp.where(core == 0, halves[1], halves[0])
     pre_grad = jnp.stack([zero, one], axis=1).reshape(TOK, ROWS)
 
-    weight_new = place(plane_array, near, across, direct)
+    both, along, pre_grad = lax.optimization_barrier((both, along, pre_grad))
+    line = lax.all_gather(both, "x", axis=0, tiled=True)
+    upper, lower = along[: SEGS * OWN], along[SEGS * OWN :]
+    kept = jnp.where(plane == 0, upper, lower)
+    taken = swap(jnp.where(plane == 0, lower, upper), "z_lo")
+    *updated, sent0 = update(0, [kept[None], taken[None]], own_power, *states, earlier)
+    direct = to_all(sent0, ("z_lo", "x"), REPLICAS)
+
+    placed = place(1, True, line.reshape(REPLICAS, SEGS * OWN, SEG), (), 10**11)
+    weight_new = place(0, False, direct, (placed,), 10**9)
     return (pre_grad, *updated, weight_new)
 
 

time: 193 us -> 194 us (level)
  the two profiles are of different devices: /device:TPU:32 before, /device:TPU:1 now
where the time goes in v3:
time: 194 us; the launch traced here: 193 us
  waiting for transfers between devices  67 us (35%)
  blocking collectives  43.7 us (23%)
  starting transfers between devices  27.1 us (14%)
  local copies, waits for them, and re-layouts  23.6 us (12%)
  between operations  14.4 us (7%)
  Pallas kernels  13.5 us (7%)
  other arithmetic  3.31 us (2%)
    all_to_all x1, blocking collectives, to_all(): lax.all_to_all(jnp.broadcast_to(values[None], (count,) + values.shape), a...  43.7 us
    all_gather x1, waiting for transfers between devices, body(): line = lax.all_gather(both, 'x', axis=0, tiled=True)  42.6 us
    unnamed x45, local copies, waits for them, and re-layouts  13.6 us
    ppermute x3, starting transfers between devices, swap(): return lax.ppermute(values, axis, [(0, 1), (1, 0)])  12.1 us
    reduce_scatter x1, waiting for transfers between devices, body(): along = lax.psum_scatter(encoded[0], 'x', scatter_dimension=0, tiled=True)  10.7 us
    all_to_all x1, waiting for transfers between devices, body(): lax.all_to_all(encoded[1].reshape(REPLICAS, SEGS * OWN, SEG), ('z_lo', 'x...  10.3 us
    all_to_all x1, starting transfers between devices, body(): lax.all_to_all(encoded[1].reshape(REPLICAS, SEGS * OWN, SEG), ('z_lo', 'x...  8.4 us
    all_to_all x1, starting transfers between devices, to_all(): lax.all_to_all(jnp.broadcast_to(values[None], (count,) + values.shape), a...  6.52 us
  transfers between devices with their start and end apart: 7, of which 5 were waited for; matrix products, arithmetic and copies ran while one was open for 7% of the time, Pallas kernels for 6%

profile of v3, /device:TPU:1, one launch (start us, length us, event | category | flops | bytes accessed | tf_op | source)
XLA Modules:
  0.0 192.5 jit_solution(13936608568812390457)
XLA Ops:
  9.7 43.7 %all_to_all.15 = bf16[32,8,1536]{2,1,0:T(8,128)(2,1)S(1)} all-to-all(bf16[32,8,1536]{2,1,0:T(8,128)(2,1)S(1)} %broadcast_in_dim.8), channel_id=1, replica_groups=mesh['z_lo'=2,'x'=8,'z_hi'=4,'y'=8,'core'=2] {'z_hi','y'}, dimensions={0} | all-to-all | bytes 1572864 | tf_op jit(solution)/shard_map/all_to_all | solution.py:351
  53.4 5.7 %collective-permute-start = (bf16[256,1536]{1,0:T(8,128)(2,1)S(1)}, bf16[256,1536]{1,0:T(8,128)(2,1)S(1)}, u32[]{:S(2)}, u32[]{:S(2)}) collective-permute-start(bf16[256,1536]{1,0:T(8,128)(2,1)S(1)} %bitcast.17), channel_id=1, source_target_pairs={{0,1},{1,0},{2,3},{3,2},{4,5},{5,4},{6,7},{7,6},{8,9},{9,8},{10,11... | collective-permute-start | bytes 2359304 | tf_op jit(solution)/shard_map/ppermute | solution.py:347
  61.8 1.1 copy-done.5
  62.9 1.0 copy-done.8
  65.5 1.3 encode_1.1
  66.9 1.0 copy-done.1
  67.9 8.4 %all-to-all-start.1 = ((bf16[16,48,768]{2,1,0:T(8,128)(2,1)}), bf16[16,48,768]{2,1,0:T(8,128)(2,1)S(1)}, u32[]{:S(2)}, u32[]{:S(2)}) async-start(bf16[16,48,768]{2,1,0:T(8,128)(2,1)} %bitcast.21), calls=%async_computation.1 | async-start | bytes 2359296 | tf_op jit(solution)/shard_map/all_to_all | solution.py:400
  76.4 1.6 stack.12
  78.7 1.6 copy.28
  80.3 2.3 %reshape.106.scale_ref = f32[3,768,1]{2,1,0:T(8,128)} reshape(f32[3,16,4,12]{3,2,1,0:T(4,128)} %copy.28) | data formatting | bytes 18432 | tf_op jit(solution)/shard_map/reshape | solution.py:395
  82.5 1.3 copy-done.2
  83.8 1.3 encode_0.1
  85.1 1.0 copy-done
  87.1 1.7 copy-done.15
  88.7 2.5 %rotate_weight.1.w_ref = bf16[192,6144]{1,0:T(8,128)(2,1)S(1)} custom-call(bf16[192,6144]{1,0:T(8,128)(2,1)S(1)} %copy-done.15, f32[1,6144]{1,0:T(1,128)S(1)} %bitcast.23, bf16[128,128]{1,0:T(8,128)(2,1)S(1)} %copy-done.10), custom_call_target="tpu_custom_call" | custom-call | flops 2415919104 | bytes 5242880 | tf_op jit(solution)/shard_map/rotate_weight/pallas_call | solution.py:287
  91.2 1.0 constant_dynamic-slice_fusion.weight_ref
  92.3 2.4 %pre_grad.1 = bf16[128,192]{1,0:T(8,128)(2,1)S(1)} custom-call(bf16[256,1536]{1,0:T(8,128)(2,1)S(1)} %bitcast.20, bf16[256,1536]{1,0:T(8,128)(2,1)S(1)} %collective-permute-done.other_ref, bf16[192,6144]{1,0:T(8,128)(2,1)S(1)} %rotate_weight.1.w_ref, f32[128,192]{1,0:T(8,128)S(1)} %copy-done.13, bf16[128,512]{1,0:T(8,128)(2,1)S(1)} %copy-done.12), custom_call_target="tpu_custom_call" | custom-call | flops 1207959552 | bytes 6291456 | tf_op jit(solution)/shard_map/pre_grad/pallas_call | solution.py:334
  94.8 10.3 %all-to-all-done.1.refs_0_ = bf16[16,48,768]{2,1,0:T(8,128)(2,1)S(1)} async-done(((bf16[16,48,768]{2,1,0:T(8,128)(2,1)}), bf16[16,48,768]{2,1,0:T(8,128)(2,1)S(1)}, u32[]{:S(2)}, u32[]{:S(2)}) %all-to-all-start.1) | async-done | bytes 1179680 | tf_op jit(solution)/shard_map/all_to_all | solution.py:400
  105.1 1.0 copy-done.4
  106.1 1.3 update_1.1
  107.4 3.0 %collective-permute-start.1 = (bf16[48,768]{1,0:T(8,128)(2,1)S(1)}, bf16[48,768]{1,0:T(8,128)(2,1)S(1)}, u32[]{:S(2)}, u32[]{:S(2)}) collective-permute-start(bf16[48,768]{1,0:T(8,128)(2,1)S(1)} %get-tuple-element.16), channel_id=1, source_target_pairs={{0,512},{512,0},{1,513},{513,1},{2,514},{514,2},{3,515},{515,3},{4... | collective-permute-start | bytes 221192 | tf_op jit(solution)/shard_map/ppermute | solution.py:347
  110.6 2.3 %collective-permute-done.1 = bf16[48,768]{1,0:T(8,128)(2,1)S(1)} collective-permute-done((bf16[48,768]{1,0:T(8,128)(2,1)S(1)}, bf16[48,768]{1,0:T(8,128)(2,1)S(1)}, u32[]{:S(2)}, u32[]{:S(2)}) %collective-permute-start.1) | collective-permute-done | bytes 73760 | tf_op jit(solution)/shard_map/ppermute | solution.py:347
  113.5 10.7 %reduce-scatter.2.cloned.1.call-done = bf16[96,768]{1,0:T(8,128)(2,1)} async-done(((bf16[768,768]{1,0:T(8,128)(2,1)}), bf16[96,768]{1,0:T(8,128)(2,1)}) %reduce-scatter.2.cloned.1.call-update) | async-done | bytes 147472 | tf_op jit(solution)/shard_map/reduce_scatter | solution.py:399
  125.2 3.4 %collective-permute-start.2 = (bf16[48,768]{1,0:T(8,128)(2,1)S(1)}, bf16[48,768]{1,0:T(8,128)(2,1)S(1)}, u32[]{:S(2)}, u32[]{:S(2)}) collective-permute-start(bf16[48,768]{1,0:T(8,128)(2,1)S(1)} %get-tuple-element.38), channel_id=1, source_target_pairs={{0,512},{512,0},{1,513},{513,1},{2,514},{514,2},{3,515},{515,3},{4... | collective-permute-start | bytes 221192 | tf_op jit(solution)/shard_map/ppermute | solution.py:347
  129.3 1.0 collective-permute-done.2
  130.3 1.2 update_0.1
  131.6 1.1 broadcast_in_dim.21
  132.6 6.5 %all-to-all-start.2 = ((bf16[16,48,768]{2,1,0:T(8,128)(2,1)}), bf16[16,48,768]{2,1,0:T(8,128)(2,1)S(1)}, u32[]{:S(2)}, u32[]{:S(2)}) async-start(bf16[16,48,768]{2,1,0:T(8,128)(2,1)} %broadcast_in_dim.21), calls=%async_computation.3 | async-start | bytes 2359296 | tf_op jit(solution)/shard_map/all_to_all | solution.py:351
  139.2 42.6 %all-gather.2.cloned.1.call-done = bf16[768,768]{1,0:T(8,128)(2,1)} async-done(((bf16[96,768]{1,0:T(8,128)(2,1)}), bf16[768,768]{1,0:T(8,128)(2,1)}) %all-gather.2.cloned.1.call-update) | async-done | bytes 1179664 | tf_op jit(solution)/shard_map/all_gather | solution.py:419
  181.8 1.3 copy-done.16
  183.0 1.3 place_1.1.refs_0_
  184.4 1.3 place_0.1
  (68 shorter events, 11.0 us)
Async XLA Ops:
  7.9 1.7 copy-start.6
  7.9 0.8 copy-start.9
  8.7 0.7 copy-start.14
  9.6 49.4 %copy-start.19 = (bf16[128,192]{0,1:T(8,128)(2,1)S(1)}, bf16[128,192]{0,1:T(8,128)(2,1)}, u32[]{:S(2)}) copy-start(bf16[128,192]{0,1:T(8,128)(2,1)} %param.12) | copy-start | bytes 147460
  9.7 49.7 %copy-start.20 = (s32[192,6]{0,1:T(8,128)S(1)}, s32[192,6]{0,1:T(8,128)}, u32[]{:S(2)}) copy-start(s32[192,6]{0,1:T(8,128)} %param.17) | copy-start | bytes 13828
  53.4 12.1 %collective-permute-start = (bf16[256,1536]{1,0:T(8,128)(2,1)S(1)}, bf16[256,1536]{1,0:T(8,128)(2,1)S(1)}, u32[]{:S(2)}, u32[]{:S(2)}) collective-permute-start(bf16[256,1536]{1,0:T(8,128)(2,1)S(1)} %bitcast.17), channel_id=1, source_target_pairs={{0,1},{1,0},{2,3},{3,2},{4,5},{5,4},{6,7},{7,6},{8,9},{9,8},{10,11... | collective-permute-start | bytes 2359304 | tf_op jit(solution)/shard_map/ppermute | solution.py:347
  59.5 1.1 copy-start.17
  61.8 1.1 copy-start.5
  62.9 1.0 copy-start.8
  63.9 0.9 copy-start.11
  66.9 1.0 copy-start.1
  67.9 37.2 %all-to-all-start.1 = ((bf16[16,48,768]{2,1,0:T(8,128)(2,1)}), bf16[16,48,768]{2,1,0:T(8,128)(2,1)S(1)}, u32[]{:S(2)}, u32[]{:S(2)}) async-start(bf16[16,48,768]{2,1,0:T(8,128)(2,1)} %bitcast.21), calls=%async_computation.1 | async-start | bytes 2359296 | tf_op jit(solution)/shard_map/all_to_all | solution.py:400
  76.3 47.9 %reduce-scatter.2.cloned.1.call-start = ((), (), s32[]{:S(2)}) async-start(), calls=%async_computation.4 | async-start | bytes 1327104 | tf_op jit(solution)/shard_map/reduce_scatter | solution.py:399
  82.5 1.3 copy-start.2
  85.1 1.0 copy-start
  86.1 0.9 copy-start.18
  86.1 0.9 copy-start.7
  86.1 0.9 copy-start.10
  86.1 95.6 %all-gather.2.cloned.1.call-start = ((), (), s32[]{:S(2)}) async-start(), calls=%async_computation.5 | async-start | bytes 1327104 | tf_op jit(solution)/shard_map/all_gather | solution.py:419
  87.1 1.7 copy-start.15
  88.7 3.5 %copy-start.12 = (bf16[128,512]{1,0:T(8,128)(2,1)S(1)}, bf16[128,512]{1,0:T(8,128)(2,1)}, u32[]{:S(2)}) copy-start(bf16[128,512]{1,0:T(8,128)(2,1)} %constant.48.clone.widen_ref.collect_ref) | copy-start | bytes 393220
  88.7 3.5 %copy-start.13 = (f32[128,192]{1,0:T(8,128)S(1)}, f32[128,192]{1,0:T(8,128)}, u32[]{:S(2)}) copy-start(f32[128,192]{1,0:T(8,128)} %get-tuple-element.42.slope_ref) | copy-start | bytes 294916
  92.3 12.9 %copy-start.3 = (f32[12,6144]{1,0:T(8,128)S(1)}, f32[12,6144]{1,0:T(8,128)}, u32[]{:S(2)}) copy-start(f32[12,6144]{1,0:T(8,128)} %first_ref.3) | copy-start | bytes 884740
  105.1 1.0 copy-start.4
  107.4 5.5 %collective-permute-start.1 = (bf16[48,768]{1,0:T(8,128)(2,1)S(1)}, bf16[48,768]{1,0:T(8,128)(2,1)S(1)}, u32[]{:S(2)}, u32[]{:S(2)}) collective-permute-start(bf16[48,768]{1,0:T(8,128)(2,1)S(1)} %get-tuple-element.16), channel_id=1, source_target_pairs={{0,512},{512,0},{1,513},{513,1},{2,514},{514,2},{3,515},{515,3},{4... | collective-permute-start | bytes 221192 | tf_op jit(solution)/shard_map/ppermute | solution.py:347
  125.2 5.1 %collective-permute-start.2 = (bf16[48,768]{1,0:T(8,128)(2,1)S(1)}, bf16[48,768]{1,0:T(8,128)(2,1)S(1)}, u32[]{:S(2)}, u32[]{:S(2)}) collective-permute-start(bf16[48,768]{1,0:T(8,128)(2,1)S(1)} %get-tuple-element.38), channel_id=1, source_target_pairs={{0,512},{512,0},{1,513},{513,1},{2,514},{514,2},{3,515},{515,3},{4... | collective-permute-start | bytes 221192 | tf_op jit(solution)/shard_map/ppermute | solution.py:347
  132.6 51.7 %all-to-all-start.2 = ((bf16[16,48,768]{2,1,0:T(8,128)(2,1)}), bf16[16,48,768]{2,1,0:T(8,128)(2,1)S(1)}, u32[]{:S(2)}, u32[]{:S(2)}) async-start(bf16[16,48,768]{2,1,0:T(8,128)(2,1)} %broadcast_in_dim.21), calls=%async_computation.3 | async-start | bytes 2359296 | tf_op jit(solution)/shard_map/all_to_all | solution.py:351
  181.8 1.3 copy-start.16
Sparse Core Ops, SparseCore 0:
  86.3 37.9 reduce-scatter.1
  126.9 54.8 all-gather.1

commit v4 on v3

--- a/solution.py
+++ b/solution.py
@@ -49,7 +49,12 @@
     col_segment = col % (SEGS * 2) // 2
     widen = np.arange(TOK)[:, None] == patch[None, :]
     same = segment[:, None] == col_segment[None, :]
-    return [jnp.asarray(table, bf16) for table in (spread, widen, same)]
+    tile = np.arange(COLS // 1024)[None, :]
+    block = tile // 3 * BLOCKS + (3 * segment[:, None] + tile % 3) // 4
+    choice = block[:, :, None] == np.arange(COLS // 1024)
+    gather = np.repeat(np.eye(COLS // 1024), COLS // 1024, axis=0)
+    shown = (spread, widen, same, choice.reshape(row.size, -1), gather)
+    return [jnp.asarray(table, bf16) for table in shown]
 
 
 def butterfly(parts):
@@ -73,7 +78,7 @@
 
 
 def rotate_upstream_kernel(u_ref, sign_ref, had_ref, out_ref, x_ref, z_ref):
-    turned = u_ref[...].astype(f32) * sign_ref[...]
+    turned = u_ref[...].astype(f32) * (1 - 2 * sign_ref[...]).astype(f32)
     for t in range(COLS // LANES):
         x_ref[2 * t : 2 * t + 2, :] = turned[:, LANES * t : LANES * (t + 1)]
     x_ref[...] = jnp.dot(
@@ -90,7 +95,7 @@
     out_ref[...] = z_ref[...].astype(bf16)
 
 
-def rotate_upstream(upstream, sign_row, had):
+def rotate_upstream(upstream, signs, had):
     return pl.pallas_call(
         rotate_upstream_kernel,
         out_shape=jax.ShapeDtypeStruct((2 * SEGS, 2 * SEG), bf16),
@@ -100,10 +105,13 @@
         ],
         compiler_params=params(),
         name="rotate_upstream",
-    )(upstream, sign_row, had)
-
-
-def expand_hidden_kernel(hidden_ref, spread_ref, widen_ref, same_ref, out_ref):
+    )(upstream, signs, had)
+
+
+def expand_hidden_kernel(
+    hidden_ref, shrink_ref, spread_ref, widen_ref, same_ref, choice_ref, gather_ref,
+    out_ref, scale_ref,
+):
     rows = lax.dot_general(
         spread_ref[...],
         hidden_ref[...],
@@ -112,25 +120,35 @@
     ).astype(bf16)
     wide = jnp.dot(rows, widen_ref[...], preferred_element_type=f32)
     out_ref[...] = (wide * same_ref[...].astype(f32)).astype(bf16)
-
-
-def expand_hidden(hidden, spread, widen, same):
+    every = jnp.dot(spread_ref[...], shrink_ref[...], preferred_element_type=f32)
+    chosen = (every * choice_ref[...].astype(f32)).astype(bf16)
+    scale_ref[...] = jnp.dot(chosen, gather_ref[...], preferred_element_type=f32)
+
+
+def expand_hidden(hidden, shrink, spread, widen, same, choice, gather):
     return pl.pallas_call(
         expand_hidden_kernel,
-        out_shape=jax.ShapeDtypeStruct(same.shape, bf16),
+        out_shape=(
+            jax.ShapeDtypeStruct(same.shape, bf16),
+            jax.ShapeDtypeStruct((same.shape[0], gather.shape[1]), f32),
+        ),
         compiler_params=params(),
         cost_estimate=pl.CostEstimate(
             flops=2 * 768 * 128 * 700, bytes_accessed=4 << 20, transcendentals=0
         ),
         name="expand_hidden",
-    )(hidden, spread, widen, same)
-
-
-def encode_kernel(by_line, left_ref, own_ref, other_ref, scale_ref, out_ref):
-    half = own_ref.shape[0]
-    total = jnp.dot(left_ref[:, :half], own_ref[...], preferred_element_type=f32)
-    total += jnp.dot(left_ref[:, half:], other_ref[...], preferred_element_type=f32)
-    total = jnp.clip(total * scale_ref[0], -clip_limit, clip_limit).astype(bf16)
+    )(hidden, shrink, spread, widen, same, choice, gather)
+
+
+def encode_kernel(half, by_line, left_ref, own_ref, other_ref, scale_ref, out_ref):
+    depth = own_ref.shape[0]
+    total = jnp.dot(left_ref[:, :depth], own_ref[...], preferred_element_type=f32)
+    total += jnp.dot(left_ref[:, depth:], other_ref[...], preferred_element_type=f32)
+    scales = scale_ref[...]
+    column = lax.broadcasted_iota(jnp.int32, scales.shape, 1)
+    here = column == half * (SEG // TILE) + pl.program_id(0)
+    scale = jnp.sum(jnp.where(here, scales, 0.0), axis=1, keepdims=True)
+    total = jnp.clip(total * scale, -clip_limit, clip_limit).astype(bf16)
     step = SEGS * OWN
     for d in range(REPLICAS):
         to = d % LINE * 2 + d // LINE if by_line else d
@@ -142,14 +160,14 @@
     depth = own.shape[0]
     tiles = SEG // TILE
     return pl.pallas_call(
-        functools.partial(encode_kernel, by_line),
-        out_shape=jax.ShapeDtypeStruct((rows, SEG), bf16),
+        functools.partial(encode_kernel, half, by_line),
+        out_shape=pltpu.HBM((rows, SEG), bf16),
         grid=(tiles,),
         in_specs=[
             whole(left.shape),
             pl.BlockSpec((depth, TILE), lambda n: (0, half * tiles + n)),
             pl.BlockSpec((depth, TILE), lambda n: (0, half * tiles + n)),
-            pl.BlockSpec((1, rows, 1), lambda n: (n, 0, 0)),
+            whole(scale.shape),
         ],
         out_specs=pl.BlockSpec((rows, TILE), lambda n: (0, n)),
         compiler_params=params(12),
@@ -354,15 +372,13 @@
 
 
 def body(upstream, pre_act, w_down, first_moment, second_moment, signs, exponents):
-    spread, widen, same = tables()
+    spread, widen, same, choice, gather = tables()
     had = jnp.asarray(hadamard(LANES), bf16)
-    sign_row = (1 - 2 * signs).astype(f32).reshape(1, COLS)
     core = lax.axis_index("core")
     plane = lax.axis_index("z_lo")
 
-    rotated = rotate_upstream(upstream, sign_row, had)
+    rotated = rotate_upstream(upstream, signs.reshape(1, COLS), had)
     own = to_all(rotated, ("z_hi", "y"), PEERS).reshape(-1, 2 * SEG)
-    other = swap(own, "core")
 
     pairs = pre_act.reshape(PEERS, 2, 2, ROWS)
     mine = jnp.where(core == 0, pairs[:, 0], pairs[:, 1]).reshape(TOK // 2, ROWS)
@@ -371,34 +387,24 @@
     normal_cdf = 0.5 * (1.0 + lax.erf(preact * root_half))
     hidden = (preact * normal_cdf).astype(bf16)
     slope = normal_cdf + preact * jnp.exp(-0.5 * preact * preact) * density_norm
-    left = expand_hidden(hidden, spread, widen, same)
-
     scale_power = exponents.astype(f32)
-    shrink = jnp.exp2(-scale_power)
+    shrink = jnp.tile(jnp.exp2(-scale_power).astype(bf16), (1, COLS // 1024))
+    left, scale = expand_hidden(hidden, shrink, spread, widen, same, choice, gather)
+
+    own, left, scale = lax.optimization_barrier((own, left, scale))
+    other = swap(own, "core")
+    encoded0 = encode(0, True, left, own, other, scale)
+    encoded0, left = lax.optimization_barrier((encoded0, left))
+    encoded1 = encode(1, False, left, own, other, scale)
+
+    sign_row = (1 - 2 * signs).astype(f32).reshape(1, COLS)
     offset = lax.axis_index(("z_lo", "x")) * OWN
     own_power = jnp.exp2(lax.dynamic_slice_in_dim(scale_power, offset, OWN, 0))
     own_weight = lax.dynamic_slice_in_dim(w_down, offset, OWN, 0)
 
-    encoded = []
-    for half in range(2):
-        picked = jnp.stack(
-            [
-                shrink[:, BLOCKS * half + (3 * s + n) // 4]
-                for n in range(SEG // TILE)
-                for s in range(SEGS)
-            ],
-            axis=0,
-        )
-        scale = (
-            picked.reshape(SEG // TILE, SEGS, REPLICAS, OWN)
-            .transpose(0, 2, 1, 3)
-            .reshape(SEG // TILE, REPLICAS * SEGS * OWN, 1)
-        )
-        encoded.append(encode(half, half == 0, left, own, other, scale))
-
-    along = lax.psum_scatter(encoded[0], "x", scatter_dimension=0, tiled=True)
+    along = lax.psum_scatter(encoded0, "x", scatter_dimension=0, tiled=True)
     terms = lax.all_to_all(
-        encoded[1].reshape(REPLICAS, SEGS * OWN, SEG), ("z_lo", "x"), 0, 0, tiled=True
+        encoded1.reshape(REPLICAS, SEGS * OWN, SEG), ("z_lo", "x"), 0, 0, tiled=True
     )
     states = (sign_row, had, first_moment, second_moment, own_weight)
     *earlier, sent1 = update(1, [terms], own_power, *states, ())

time: 194 us -> 191 us (0.985)
  the two profiles are of different devices: /device:TPU:1 before, /device:TPU:16 now
where the time goes in v4:
time: 191 us; the launch traced here: 190 us
  waiting for transfers between devices  102 us (53%)
  starting transfers between devices  44.9 us (24%)
  Pallas kernels  15.7 us (8%)
  between operations  14.3 us (7%)
  local copies, waits for them, and re-layouts  10.7 us (6%)
  other arithmetic  2.54 us (1%)
    all_gather x1, waiting for transfers between devices, body(): line = lax.all_gather(both, 'x', axis=0, tiled=True)  39.4 us
    all_to_all x2, starting transfers between devices, to_all(): lax.all_to_all(jnp.broadcast_to(values[None], (count,) + values.shape), a...  27.9 us
    all_to_all x1, waiting for transfers between devices, body(): lax.all_to_all(encoded1.reshape(REPLICAS, SEGS * OWN, SEG), ('z_lo', 'x')...  26.6 us
    all_to_all x2, waiting for transfers between devices, to_all(): lax.all_to_all(jnp.broadcast_to(values[None], (count,) + values.shape), a...  23.7 us
    all_to_all x1, starting transfers between devices, body(): lax.all_to_all(encoded1.reshape(REPLICAS, SEGS * OWN, SEG), ('z_lo', 'x')...  8.57 us
    ppermute x3, starting transfers between devices, swap(): return lax.ppermute(values, axis, [(0, 1), (1, 0)])  8.29 us
    ppermute x3, waiting for transfers between devices, swap(): return lax.ppermute(values, axis, [(0, 1), (1, 0)])  7.43 us
    unnamed x39, local copies, waits for them, and re-layouts  7.15 us
  transfers between devices with their start and end apart: 8, of which 7 were waited for; matrix products, arithmetic and copies ran while one was open for 3% of the time, Pallas kernels for 5%

profile of v4, /device:TPU:16, one launch (start us, length us, event | category | flops | bytes accessed | tf_op | source)
XLA Modules:
  0.0 190.0 jit_solution(10271162444795640119)
XLA Ops:
  7.2 0.7 copy-done.4
  7.9 0.7 copy-done.9
  8.7 0.7 copy-done.11
  9.6 0.9 broadcast_in_dim.8
  10.6 22.1 %all-to-all-start = ((bf16[32,8,1536]{2,1,0:T(8,128)(2,1)}), bf16[32,8,1536]{2,1,0:T(8,128)(2,1)S(1)}, u32[]{:S(2)}, u32[]{:S(2)}) async-start(bf16[32,8,1536]{2,1,0:T(8,128)(2,1)} %broadcast_in_dim.8), calls=%async_computation | async-start | bytes 1572864 | tf_op jit(solution)/shard_map/all_to_all | solution.py:369
  34.0 0.8 expand_hidden.1
  34.7 23.7 %all-to-all-done = bf16[32,8,1536]{2,1,0:T(8,128)(2,1)S(1)} async-done(((bf16[32,8,1536]{2,1,0:T(8,128)(2,1)}), bf16[32,8,1536]{2,1,0:T(8,128)(2,1)S(1)}, u32[]{:S(2)}, u32[]{:S(2)}) %all-to-all-start) | async-done | bytes 786464 | tf_op jit(solution)/shard_map/all_to_all | solution.py:369
  58.4 1.9 %collective-permute-start = (bf16[256,1536]{1,0:T(8,128)(2,1)S(1)}, bf16[256,1536]{1,0:T(8,128)(2,1)S(1)}, u32[]{:S(2)}, u32[]{:S(2)}) collective-permute-start(bf16[256,1536]{1,0:T(8,128)(2,1)S(1)} %bitcast.12), channel_id=1, source_target_pairs={{0,1},{1,0},{2,3},{3,2},{4,5},{5,4},{6,7},{7,6},{8,9},{9,8},{10,11... | collective-permute-start | bytes 2359304 | tf_op jit(solution)/shard_map/ppermute | solution.py:365
  60.3 2.3 %collective-permute-done.other_ref = bf16[256,1536]{1,0:T(8,128)(2,1)S(1)} collective-permute-done((bf16[256,1536]{1,0:T(8,128)(2,1)S(1)}, bf16[256,1536]{1,0:T(8,128)(2,1)S(1)}, u32[]{:S(2)}, u32[]{:S(2)}) %collective-permute-start) | collective-permute-done | bytes 786464 | tf_op jit(solution)/shard_map/ppermute | solution.py:365
  62.6 2.3 %encode_0.1 = bf16[768,768]{1,0:T(8,128)(2,1)} custom-call(bf16[768,512]{1,0:T(8,128)(2,1)S(1)} %get-tuple-element.28.left_ref, bf16[256,1536]{1,0:T(8,128)(2,1)S(1)} %bitcast.13, bf16[256,1536]{1,0:T(8,128)(2,1)S(1)} %collective-permute-done.other_ref, f32[768,6]{1,0:T(8,128)S(1)} %get-tuple-element.27.scale_ref), custom_call_target="tpu_custom_call" | custom-call | flops 603979776 | bytes 4194304 | tf_op jit(solution)/shard_map/encode_0/pallas_call | solution.py:162
  64.9 2.4 %encode_1.1 = bf16[768,768]{1,0:T(8,128)(2,1)} custom-call(bf16[768,512]{1,0:T(8,128)(2,1)S(1)} %get-tuple-element.28.left_ref, bf16[256,1536]{1,0:T(8,128)(2,1)S(1)} %bitcast.14, bf16[256,1536]{1,0:T(8,128)(2,1)S(1)} %collective-permute-done.other_ref, f32[768,6]{1,0:T(8,128)S(1)} %get-tuple-element.27.scale_ref), custom_call_target="tpu_custom_call" | custom-call | flops 603979776 | bytes 4194304 | tf_op jit(solution)/shard_map/encode_1/pallas_call | solution.py:162
  67.3 8.6 %all-to-all-start.1 = ((bf16[16,48,768]{2,1,0:T(8,128)(2,1)}), bf16[16,48,768]{2,1,0:T(8,128)(2,1)S(1)}, u32[]{:S(2)}, u32[]{:S(2)}) async-start(bf16[16,48,768]{2,1,0:T(8,128)(2,1)} %bitcast.22), calls=%async_computation.1 | async-start | bytes 2359296 | tf_op jit(solution)/shard_map/all_to_all | solution.py:406
  76.9 1.7 copy-done.12
  78.6 2.5 %rotate_weight.1.w_ref = bf16[192,6144]{1,0:T(8,128)(2,1)S(1)} custom-call(bf16[192,6144]{1,0:T(8,128)(2,1)S(1)} %copy-done.12, f32[1,6144]{1,0:T(1,128)S(1)} %bitcast.16, bf16[128,128]{1,0:T(8,128)(2,1)S(1)} %copy-done.5), custom_call_target="tpu_custom_call" | custom-call | flops 2415919104 | bytes 5242880 | tf_op jit(solution)/shard_map/rotate_weight/pallas_call | solution.py:305
  81.0 1.0 constant_dynamic-slice_fusion.weight_ref
  82.1 2.4 %pre_grad.1 = bf16[128,192]{1,0:T(8,128)(2,1)S(1)} custom-call(bf16[256,1536]{1,0:T(8,128)(2,1)S(1)} %bitcast.15, bf16[256,1536]{1,0:T(8,128)(2,1)S(1)} %collective-permute-done.other_ref, bf16[192,6144]{1,0:T(8,128)(2,1)S(1)} %rotate_weight.1.w_ref, f32[128,192]{1,0:T(8,128)S(1)} %copy-done.8, bf16[128,512]{1,0:T(8,128)(2,1)S(1)} %copy-done.7), custom_call_target="tpu_custom_call" | custom-call | flops 1207959552 | bytes 6291456 | tf_op jit(solution)/shard_map/pre_grad/pallas_call | solution.py:352
  84.6 26.6 %all-to-all-done.1.refs_0_ = bf16[16,48,768]{2,1,0:T(8,128)(2,1)S(1)} async-done(((bf16[16,48,768]{2,1,0:T(8,128)(2,1)}), bf16[16,48,768]{2,1,0:T(8,128)(2,1)S(1)}, u32[]{:S(2)}, u32[]{:S(2)}) %all-to-all-start.1) | async-done | bytes 1179680 | tf_op jit(solution)/shard_map/all_to_all | solution.py:406
  111.2 1.0 copy-done.1
  112.2 1.3 update_1.1
  113.5 2.7 %collective-permute-start.1 = (bf16[48,768]{1,0:T(8,128)(2,1)S(1)}, bf16[48,768]{1,0:T(8,128)(2,1)S(1)}, u32[]{:S(2)}, u32[]{:S(2)}) collective-permute-start(bf16[48,768]{1,0:T(8,128)(2,1)S(1)} %get-tuple-element.29), channel_id=1, source_target_pairs={{0,512},{512,0},{1,513},{513,1},{2,514},{514,2},{3,515},{515,3},{4... | collective-permute-start | bytes 221192 | tf_op jit(solution)/shard_map/ppermute | solution.py:365
  116.3 3.4 %collective-permute-done.1 = bf16[48,768]{1,0:T(8,128)(2,1)S(1)} collective-permute-done((bf16[48,768]{1,0:T(8,128)(2,1)S(1)}, bf16[48,768]{1,0:T(8,128)(2,1)S(1)}, u32[]{:S(2)}, u32[]{:S(2)}) %collective-permute-start.1) | collective-permute-done | bytes 73760 | tf_op jit(solution)/shard_map/ppermute | solution.py:365
  120.4 4.1 %reduce-scatter.2.cloned.1.call-done = bf16[96,768]{1,0:T(8,128)(2,1)} async-done(((bf16[768,768]{1,0:T(8,128)(2,1)}), bf16[96,768]{1,0:T(8,128)(2,1)}) %reduce-scatter.2.cloned.1.call-update) | async-done | bytes 147472 | tf_op jit(solution)/shard_map/reduce_scatter | solution.py:405
  124.5 0.9 broadcast_select_fusion
  125.5 3.7 %collective-permute-start.2 = (bf16[48,768]{1,0:T(8,128)(2,1)S(1)}, bf16[48,768]{1,0:T(8,128)(2,1)S(1)}, u32[]{:S(2)}, u32[]{:S(2)}) collective-permute-start(bf16[48,768]{1,0:T(8,128)(2,1)S(1)} %get-tuple-element.51), channel_id=1, source_target_pairs={{0,512},{512,0},{1,513},{513,1},{2,514},{514,2},{3,515},{515,3},{4... | collective-permute-start | bytes 221192 | tf_op jit(solution)/shard_map/ppermute | solution.py:365
  129.9 1.8 collective-permute-done.2
  131.7 1.2 update_0.1
  133.0 1.1 broadcast_in_dim.21
  134.0 5.8 %all-to-all-start.2 = ((bf16[16,48,768]{2,1,0:T(8,128)(2,1)}), bf16[16,48,768]{2,1,0:T(8,128)(2,1)S(1)}, u32[]{:S(2)}, u32[]{:S(2)}) async-start(bf16[16,48,768]{2,1,0:T(8,128)(2,1)} %broadcast_in_dim.21), calls=%async_computation.3 | async-start | bytes 2359296 | tf_op jit(solution)/shard_map/all_to_all | solution.py:369
  139.9 39.4 %all-gather.2.cloned.1.call-done = bf16[768,768]{1,0:T(8,128)(2,1)} async-done(((bf16[96,768]{1,0:T(8,128)(2,1)}), bf16[768,768]{1,0:T(8,128)(2,1)}) %all-gather.2.cloned.1.call-update) | async-done | bytes 1179664 | tf_op jit(solution)/shard_map/all_gather | solution.py:425
  179.2 1.3 copy-done.14
  180.5 1.3 place_1.1.refs_0_
  181.8 1.3 place_0.1
  (58 shorter events, 4.0 us)
Async XLA Ops:
  7.2 0.8 copy-start.4
  7.9 0.7 copy-start.9
  8.7 0.7 copy-start.11
  9.6 23.1 %copy-start.16 = (s32[192,6]{0,1:T(8,128)S(1)}, s32[192,6]{0,1:T(8,128)}, u32[]{:S(2)}) copy-start(s32[192,6]{0,1:T(8,128)} %param.19) | copy-start | bytes 13828
  9.6 23.3 %copy-start.15 = (bf16[128,192]{0,1:T(8,128)(2,1)S(1)}, bf16[128,192]{0,1:T(8,128)(2,1)}, u32[]{:S(2)}) copy-start(bf16[128,192]{0,1:T(8,128)(2,1)} %param.14) | copy-start | bytes 147460
  10.6 23.4 %copy-start.2 = (bf16[768,512]{1,0:T(8,128)(2,1)S(1)}, bf16[768,512]{1,0:T(8,128)(2,1)}, u32[]{:S(2)}) copy-start(bf16[768,512]{1,0:T(8,128)(2,1)} %constant.53.clone.same_ref) | copy-start | bytes 2359300
  10.6 23.4 %copy-start.3 = (bf16[768,192]{1,0:T(8,128)(2,1)S(1)}, bf16[768,192]{1,0:T(8,128)(2,1)}, u32[]{:S(2)}) copy-start(bf16[768,192]{1,0:T(8,128)(2,1)} %constant.51.clone.spread_ref) | copy-start | bytes 884740
  10.6 23.4 %copy-start.6 = (bf16[768,36]{1,0:T(8,128)(2,1)S(1)}, bf16[768,36]{1,0:T(8,128)(2,1)}, u32[]{:S(2)}) copy-start(bf16[768,36]{1,0:T(8,128)(2,1)} %constant.54.clone.choice_ref) | copy-start | bytes 165892
  10.6 23.4 %copy-start.7 = (bf16[128,512]{1,0:T(8,128)(2,1)S(1)}, bf16[128,512]{1,0:T(8,128)(2,1)}, u32[]{:S(2)}) copy-start(bf16[128,512]{1,0:T(8,128)(2,1)} %constant.52.clone.widen_ref.collect_ref) | copy-start | bytes 393220
  10.6 23.4 %copy-start.13 = (bf16[36,6]{1,0:T(8,128)(2,1)S(1)}, bf16[36,6]{1,0:T(8,128)(2,1)}, u32[]{:S(2)}) copy-start(bf16[36,6]{1,0:T(8,128)(2,1)} %constant.55.clone.gather_ref) | copy-start | bytes 1300
  10.6 47.9 %all-to-all-start = ((bf16[32,8,1536]{2,1,0:T(8,128)(2,1)}), bf16[32,8,1536]{2,1,0:T(8,128)(2,1)S(1)}, u32[]{:S(2)}, u32[]{:S(2)}) async-start(bf16[32,8,1536]{2,1,0:T(8,128)(2,1)} %broadcast_in_dim.8), calls=%async_computation | async-start | bytes 1572864 | tf_op jit(solution)/shard_map/all_to_all | solution.py:369
  58.4 4.2 %collective-permute-start = (bf16[256,1536]{1,0:T(8,128)(2,1)S(1)}, bf16[256,1536]{1,0:T(8,128)(2,1)S(1)}, u32[]{:S(2)}, u32[]{:S(2)}) collective-permute-start(bf16[256,1536]{1,0:T(8,128)(2,1)S(1)} %bitcast.12), channel_id=1, source_target_pairs={{0,1},{1,0},{2,3},{3,2},{4,5},{5,4},{6,7},{7,6},{8,9},{9,8},{10,11... | collective-permute-start | bytes 2359304 | tf_op jit(solution)/shard_map/ppermute | solution.py:365
  67.3 43.9 %all-to-all-start.1 = ((bf16[16,48,768]{2,1,0:T(8,128)(2,1)}), bf16[16,48,768]{2,1,0:T(8,128)(2,1)S(1)}, u32[]{:S(2)}, u32[]{:S(2)}) async-start(bf16[16,48,768]{2,1,0:T(8,128)(2,1)} %bitcast.22), calls=%async_computation.1 | async-start | bytes 2359296 | tf_op jit(solution)/shard_map/all_to_all | solution.py:406
  75.9 0.8 copy-start.17
  75.9 1.0 copy-start.10
  75.9 1.0 copy-start.5
  75.9 48.6 %reduce-scatter.2.cloned.1.call-start = ((), (), s32[]{:S(2)}) async-start(), calls=%async_computation.4 | async-start | bytes 1327104 | tf_op jit(solution)/shard_map/reduce_scatter | solution.py:405
  76.6 102.6 %all-gather.2.cloned.1.call-start = ((), (), s32[]{:S(2)}) async-start(), calls=%async_computation.5 | async-start | bytes 1327104 | tf_op jit(solution)/shard_map/all_gather | solution.py:425
  76.9 1.7 copy-start.12
  78.6 3.5 %copy-start.8 = (f32[128,192]{1,0:T(8,128)S(1)}, f32[128,192]{1,0:T(8,128)}, u32[]{:S(2)}) copy-start(f32[128,192]{1,0:T(8,128)} %get-tuple-element.55.slope_ref) | copy-start | bytes 294916
  82.1 29.1 %copy-start = (f32[12,6144]{1,0:T(8,128)S(1)}, f32[12,6144]{1,0:T(8,128)}, u32[]{:S(2)}) copy-start(f32[12,6144]{1,0:T(8,128)} %first_ref.3) | copy-start | bytes 884740
  111.2 1.0 copy-start.1
  113.5 6.2 %collective-permute-start.1 = (bf16[48,768]{1,0:T(8,128)(2,1)S(1)}, bf16[48,768]{1,0:T(8,128)(2,1)S(1)}, u32[]{:S(2)}, u32[]{:S(2)}) collective-permute-start(bf16[48,768]{1,0:T(8,128)(2,1)S(1)} %get-tuple-element.29), channel_id=1, source_target_pairs={{0,512},{512,0},{1,513},{513,1},{2,514},{514,2},{3,515},{515,3},{4... | collective-permute-start | bytes 221192 | tf_op jit(solution)/shard_map/ppermute | solution.py:365
  125.5 6.2 %collective-permute-start.2 = (bf16[48,768]{1,0:T(8,128)(2,1)S(1)}, bf16[48,768]{1,0:T(8,128)(2,1)S(1)}, u32[]{:S(2)}, u32[]{:S(2)}) collective-permute-start(bf16[48,768]{1,0:T(8,128)(2,1)S(1)} %get-tuple-element.51), channel_id=1, source_target_pairs={{0,512},{512,0},{1,513},{513,1},{2,514},{514,2},{3,515},{515,3},{4... | collective-permute-start | bytes 221192 | tf_op jit(solution)/shard_map/ppermute | solution.py:365
  134.0 47.8 %all-to-all-start.2 = ((bf16[16,48,768]{2,1,0:T(8,128)(2,1)}), bf16[16,48,768]{2,1,0:T(8,128)(2,1)S(1)}, u32[]{:S(2)}, u32[]{:S(2)}) async-start(bf16[16,48,768]{2,1,0:T(8,128)(2,1)} %broadcast_in_dim.21), calls=%async_computation.3 | async-start | bytes 2359296 | tf_op jit(solution)/shard_map/all_to_all | solution.py:369
  179.2 1.3 copy-start.14
Sparse Core Ops, SparseCore 0:
  80.7 43.7 reduce-scatter.1
  127.2 52.0 all-gather.1

commit v5 on v1

--- a/solution.py
+++ b/solution.py
@@ -19,10 +19,12 @@
 SEGS = 4
 SEG = 1536
 BLOCKS = 6
+KEPT = 47
+SPARE = 128
+TILE = 256
 TOK = 128
 PEERS = 32
 LANES = 128
-VMEM = 48 * 1024 * 1024
 bf16 = jnp.bfloat16
 f32 = jnp.float32
 
@@ -37,20 +39,21 @@
 
 
 def tables():
-    row = np.arange(REPLICAS * SEGS * OWN)
-    owner, segment, own = row // (SEGS * OWN), row % (SEGS * OWN) // OWN, row % OWN
+    owner = np.concatenate([np.repeat(np.arange(REPLICAS), KEPT), np.arange(REPLICAS)])
+    part = np.concatenate([np.tile(np.arange(KEPT), REPLICAS), np.full(REPLICAS, KEPT)])
+    segment, own = part // OWN, part % OWN
     spread = (owner * OWN + own)[:, None] == np.arange(ROWS)[None, :]
     col = np.arange(2 * PEERS * SEGS * 2)
     patch = col // (SEGS * 2) * 2 + col % 2
     col_segment = col % (SEGS * 2) // 2
     widen = np.arange(TOK)[:, None] == patch[None, :]
     same = segment[:, None] == col_segment[None, :]
-    return (
-        spread.astype(np.float32),
-        widen.astype(np.float32),
-        same.astype(np.float32),
-        col_segment,
-    )
+    tiles = SEG // TILE
+    block = (3 * segment[:, None] + np.arange(tiles)[None, :] // 2) // 2
+    choice = block[:, :, None] == np.arange(BLOCKS)
+    gather = np.repeat(np.eye(tiles), BLOCKS, axis=0)
+    shown = (spread, widen, same, choice.reshape(owner.size, -1), gather)
+    return [jnp.asarray(table, bf16) for table in shown]
 
 
 def butterfly(parts):
@@ -69,12 +72,12 @@
     return pl.BlockSpec(shape, lambda *_: (0,) * len(shape))
 
 
-def params():
-    return pltpu.CompilerParams(vmem_limit_bytes=VMEM)
+def params(mebibytes=8):
+    return pltpu.CompilerParams(vmem_limit_bytes=mebibytes << 20)
 
 
 def rotate_upstream_kernel(u_ref, sign_ref, had_ref, out_ref, x_ref, z_ref):
-    turned = u_ref[...].astype(f32) * sign_ref[...]
+    turned = u_ref[...].astype(f32) * (1 - 2 * sign_ref[...]).astype(f32)
     for t in range(COLS // LANES):
         x_ref[2 * t : 2 * t + 2, :] = turned[:, LANES * t : LANES * (t + 1)]
     x_ref[...] = jnp.dot(
@@ -90,7 +93,7 @@
     out_ref[...] = z_ref[...].astype(bf16)
 
 
-def rotate_upstream(upstream, sign_row, had):
+def rotate_upstream(upstream, signs, had):
     return pl.pallas_call(
         rotate_upstream_kernel,
         out_shape=jax.ShapeDtypeStruct((2 * SEGS, SEG), bf16),
@@ -100,10 +103,13 @@
         ],
         compiler_params=params(),
         name="rotate_upstream",
-    )(upstream, sign_row, had)
-
-
-def expand_hidden_kernel(hidden_ref, spread_ref, widen_ref, same_ref, out_ref):
+    )(upstream, signs, had)
+
+
+def expand_hidden_kernel(
+    hidden_ref, shrink_ref, spread_ref, widen_ref, same_ref, choice_ref, gather_ref,
+    out_ref, scale_ref,
+):
     rows = lax.dot_general(
         spread_ref[...],
         hidden_ref[...],
@@ -112,48 +118,61 @@
     ).astype(bf16)
     wide = jnp.dot(rows, widen_ref[...], preferred_element_type=f32)
     out_ref[...] = (wide * same_ref[...].astype(f32)).astype(bf16)
-
-
-def expand_hidden(hidden, spread, widen, same):
+    every = jnp.dot(spread_ref[...], shrink_ref[...], preferred_element_type=f32)
+    chosen = (every * choice_ref[...].astype(f32)).astype(bf16)
+    scale_ref[...] = jnp.dot(chosen, gather_ref[...], preferred_element_type=f32)
+
+
+def expand_hidden(hidden, shrink, spread, widen, same, choice, gather):
     return pl.pallas_call(
         expand_hidden_kernel,
-        out_shape=jax.ShapeDtypeStruct(same.shape, bf16),
+        out_shape=(
+            jax.ShapeDtypeStruct(same.shape, bf16),
+            jax.ShapeDtypeStruct((same.shape[0], gather.shape[1]), f32),
+        ),
         compiler_params=params(),
         cost_estimate=pl.CostEstimate(
             flops=2 * 768 * 128 * 700, bytes_accessed=4 << 20, transcendentals=0
         ),
         name="expand_hidden",
-    )(hidden, spread, widen, same)
-
-
-TILE = 256
-
-
-def encode_kernel(left_ref, own_ref, other_ref, scale_ref, out_ref):
-    half = own_ref.shape[0]
-    total = jnp.dot(left_ref[:, :half], own_ref[...], preferred_element_type=f32)
-    total += jnp.dot(left_ref[:, half:], other_ref[...], preferred_element_type=f32)
-    total = jnp.clip(total * scale_ref[0], -clip_limit, clip_limit)
-    out_ref[...] = total.astype(bf16)
+    )(hidden, shrink, spread, widen, same, choice, gather)
+
+
+def encode_kernel(left_ref, own_ref, other_ref, scale_ref, out_ref, spare_ref):
+    depth = own_ref.shape[0]
+    full = REPLICAS * KEPT
+    scales = scale_ref[...]
+    spare_ref[...] = jnp.zeros_like(spare_ref)
+    for n in range(SEG // TILE):
+        lanes = slice(TILE * n, TILE * (n + 1))
+        total = jnp.dot(
+            left_ref[:, :depth], own_ref[:, lanes], preferred_element_type=f32
+        )
+        total += jnp.dot(
+            left_ref[:, depth:], other_ref[:, lanes], preferred_element_type=f32
+        )
+        total = jnp.clip(total * scales[:, n : n + 1], -clip_limit, clip_limit)
+        out_ref[:, lanes] = total[:full].astype(bf16)
+        for k in range(TILE // SPARE):
+            rows = pl.ds(TILE // SPARE * n + k, REPLICAS, stride=KEPT)
+            spare_ref[rows, :] = total[full:, SPARE * k : SPARE * (k + 1)]
+    out_ref[:, SEG:] = spare_ref[...].astype(bf16)
 
 
 def encode(left, own, other, scale):
-    rows = left.shape[0]
-    half = own.shape[0]
+    full = REPLICAS * KEPT
+    depth = own.shape[0]
+    shape = (full, SEG + SPARE)
     return pl.pallas_call(
         encode_kernel,
-        out_shape=jax.ShapeDtypeStruct((rows, SEG), bf16),
-        grid=(SEG // TILE,),
-        in_specs=[
-            whole(left.shape),
-            pl.BlockSpec((half, TILE), lambda n: (0, n)),
-            pl.BlockSpec((half, TILE), lambda n: (0, n)),
-            pl.BlockSpec((1, rows, 1), lambda n: (n // 2, 0, 0)),
-        ],
-        out_specs=pl.BlockSpec((rows, TILE), lambda n: (0, n)),
-        compiler_params=params(),
+        out_shape=pltpu.HBM(shape, bf16),
+        grid=(1,),
+        in_specs=[whole(array.shape) for array in (left, own, other, scale)],
+        out_specs=whole(shape),
+        scratch_shapes=[pltpu.VMEM((full, SPARE), f32)],
+        compiler_params=params(24),
         cost_estimate=pl.CostEstimate(
-            flops=2 * rows * 2 * half * SEG, bytes_accessed=6 << 20, transcendentals=0
+            flops=4 * full * depth * SEG, bytes_accessed=6 << 20, transcendentals=0
         ),
         name="encode",
     )(left, own, other, scale)
@@ -163,10 +182,10 @@
     received_ref, power_ref, sign_ref, had_ref, first_ref, second_ref, weight_ref,
     mean_ref, first_out, second_out, sent_ref, sum_ref, x_ref, y_ref,
 ):
-    total = received_ref[0].astype(f32)
-    for source in range(1, received_ref.shape[0]):
-        total += received_ref[source].astype(f32)
-    sum_ref[...] = total
+    total = received_ref[...].astype(f32)
+    sum_ref[:KEPT, :] = total[:, :SEG]
+    for k in range(SEG // SPARE):
+        sum_ref[KEPT : KEPT + 1, SPARE * k : SPARE * (k + 1)] = total[k : k + 1, SEG:]
     x_ref[...] = jnp.zeros_like(x_ref)
     for t in range(COLS // LANES):
         s, lane = divmod(t, SEG // LANES)
@@ -231,7 +250,7 @@
         place_kernel,
         out_shape=jax.ShapeDtypeStruct((ROWS, COLS), bf16),
         scratch_shapes=[pltpu.VMEM((ROWS, COLS), f32)],
-        compiler_params=params(),
+        compiler_params=params(20),
         name="place",
     )(gathered)
 
@@ -298,7 +317,7 @@
         pre_grad_kernel,
         out_shape=jax.ShapeDtypeStruct((TOK, ROWS), bf16),
         scratch_shapes=[pltpu.VMEM((2 * own.shape[0], ROWS), f32)],
-        compiler_params=params(),
+        compiler_params=params(16),
         cost_estimate=pl.CostEstimate(
             flops=8 * 512 * SEG * ROWS, bytes_accessed=6 << 20, transcendentals=0
         ),
@@ -306,28 +325,19 @@
     )(own, other, weight, slope, collect)
 
 
-def swap_core(values):
-    return lax.ppermute(values, "core", [(0, 1), (1, 0)])
+def to_all(values, axes, count):
+    return lax.all_to_all(
+        jnp.broadcast_to(values[None], (count,) + values.shape), axes, 0, 0, tiled=True
+    )
 
 
 def body(upstream, pre_act, w_down, first_moment, second_moment, signs, exponents):
-    spread_np, widen_np, same_np, _ = tables()
+    spread, widen, same, choice, gather = tables()
     had = jnp.asarray(hadamard(LANES), bf16)
-    spread = jnp.asarray(spread_np, bf16)
-    widen = jnp.asarray(widen_np, bf16)
-    same = jnp.asarray(same_np, bf16)
-    sign_row = (1 - 2 * signs).astype(f32).reshape(1, COLS)
     core = lax.axis_index("core")
 
-    rotated = rotate_upstream(upstream, sign_row, had)
-    own = lax.all_to_all(
-        jnp.broadcast_to(rotated[None], (PEERS, 2 * SEGS, SEG)),
-        ("z_hi", "y"),
-        0,
-        0,
-        tiled=True,
-    ).reshape(PEERS * 2 * SEGS, SEG)
-    other = swap_core(own)
+    rotated = rotate_upstream(upstream, signs.reshape(1, COLS), had)
+    own = to_all(rotated, ("z_hi", "y"), PEERS).reshape(-1, SEG)
 
     pairs = pre_act.reshape(PEERS, 2, 2, ROWS)
     mine = jnp.where(core == 0, pairs[:, 0], pairs[:, 1]).reshape(TOK // 2, ROWS)
@@ -336,48 +346,31 @@
     normal_cdf = 0.5 * (1.0 + lax.erf(preact * root_half))
     hidden = (preact * normal_cdf).astype(bf16)
     slope = normal_cdf + preact * jnp.exp(-0.5 * preact * preact) * density_norm
-
     scale_power = exponents.astype(f32)
-    shrink = jnp.exp2(-scale_power)
-    picked = jnp.stack(
-        [
-            jnp.stack([shrink[:, (3 * s + u) // 2] for s in range(SEGS)], axis=0)
-            for u in range(3)
-        ],
-        axis=0,
-    )
-    scale = (
-        picked.reshape(3, SEGS, REPLICAS, OWN)
-        .transpose(0, 2, 1, 3)
-        .reshape(3, REPLICAS * SEGS * OWN, 1)
-    )
-    left = expand_hidden(hidden, spread, widen, same)
+    shrink = jnp.tile(jnp.exp2(-scale_power).astype(bf16), (1, SEG // TILE))
+    left, scale = expand_hidden(hidden, shrink, spread, widen, same, choice, gather)
+    sign_row = (1 - 2 * signs).astype(f32).reshape(1, COLS)
+    turned_weight = rotate_weight(w_down, sign_row, had)
+    offset = lax.axis_index(("z_lo", "x")) * OWN
+    own_power = jnp.exp2(lax.dynamic_slice_in_dim(scale_power, offset, OWN, 0))
+    own_weight = lax.dynamic_slice_in_dim(w_down, offset, OWN, 0)
+
+    own, left, scale, turned_weight, own_power, own_weight = lax.optimization_barrier(
+        (own, left, scale, turned_weight, own_power, own_weight)
+    )
+    other = lax.ppermute(own, "core", [(0, 1), (1, 0)])
     encoded = encode(left, own, other, scale)
-    received = lax.all_to_all(
-        encoded.reshape(REPLICAS, SEGS * OWN, SEG), ("z_lo", "x"), 0, 0, tiled=True
-    )
-
-    turned_weight = rotate_weight(w_down, sign_row, had)
+    summed = lax.psum_scatter(encoded, ("z_lo", "x"), scatter_dimension=0, tiled=True)
+    grad_mean, first_new, second_new, sent = update(
+        summed, own_power, sign_row, had, first_moment, second_moment, own_weight
+    )
+    weight_new = place(to_all(sent, ("z_lo", "x"), REPLICAS))
+
     mixed = pre_grad_product(own, other, turned_weight, slope, widen)
     halves = mixed.reshape(2, PEERS, 2, ROWS)
     zero = jnp.where(core == 0, halves[0], halves[1])
     one = jnp.where(core == 0, halves[1], halves[0])
     pre_grad = jnp.stack([zero, one], axis=1).reshape(TOK, ROWS)
-
-    offset = lax.axis_index(("z_lo", "x")) * OWN
-    own_power = jnp.exp2(lax.dynamic_slice_in_dim(scale_power, offset, OWN, 0))
-    own_weight = lax.dynamic_slice_in_dim(w_down, offset, OWN, 0)
-    grad_mean, first_new, second_new, sent = update(
-        received, own_power, sign_row, had, first_moment, second_moment, own_weight
-    )
-    gathered = lax.all_to_all(
-        jnp.broadcast_to(sent[None], (REPLICAS, SEGS * OWN, SEG)),
-        ("z_lo", "x"),
-        0,
-        0,
-        tiled=True,
-    )
-    weight_new = place(gathered)
     return (pre_grad, grad_mean, first_new, second_new, weight_new)
 
 

time: 199 us -> 172 us (0.86)
  waiting for transfers between devices: 125 us -> 58.8 us
  blocking collectives: 0 us -> 47.4 us
  starting transfers between devices: 41.6 us -> 31.8 us
  local copies, waits for them, and re-layouts: 13.8 us -> 17.2 us
  Pallas kernels: 15.2 us -> 12.4 us
    all_to_all x3 -> x2, waiting for transfers between devices: 125 us -> 56.6 us  [to_all(): lax.all_to_all(jnp.broadcast_to(values[None], (count,) + values.shape), a...]
    unnamed x0 -> x1, blocking collectives: none -> 47.4 us
    all_to_all x3 -> x2, starting transfers between devices: 39.7 us -> 28.2 us  [to_all(): lax.all_to_all(jnp.broadcast_to(values[None], (count,) + values.shape), a...]
    unnamed x29 -> x45, local copies, waits for them, and re-layouts: 8.65 us -> 13.1 us
    ppermute x1, waiting for transfers between devices: 0.01 us -> 2.25 us  [body(): other = lax.ppermute(own, 'core', [(0, 1), (1, 0)])]
  transfers between devices with their start and end apart: 4 -> 4, of which waited for: 3 -> 3; matrix products, arithmetic and copies ran while one was open for 2% -> 4% of each run, Pallas kernels for 3% -> 3%
where the time goes in v5:
time: 172 us
  waiting for transfers between devices  58.8 us (34%)
  blocking collectives  47.4 us (28%)
  starting transfers between devices  31.8 us (18%)
  local copies, waits for them, and re-layouts  17.2 us (10%)
  Pallas kernels  12.4 us (7%)
  other arithmetic  2.35 us (1%)
    all_to_all x2, waiting for transfers between devices, to_all(): lax.all_to_all(jnp.broadcast_to(values[None], (count,) + values.shape), a...  56.6 us
    unnamed x1, blocking collectives  47.4 us
    all_to_all x2, starting transfers between devices, to_all(): lax.all_to_all(jnp.broadcast_to(values[None], (count,) + values.shape), a...  28.2 us
    unnamed x45, local copies, waits for them, and re-layouts  13.1 us
  transfers between devices with their start and end apart: 4, of which 3 were waited for; matrix products, arithmetic and copies ran while one was open for 4% of the time, Pallas kernels for 3%

profile of v5, /device:TPU:16, one launch (start us, length us, event | category | flops | bytes accessed | tf_op | source)
XLA Modules:
  0.0 171.5 jit_solution(12508924220875787522)
XLA Ops:
  0.7 0.9 copy-done.8
  1.6 0.7 copy-done.11
  2.3 0.7 copy-done.12
  3.2 0.9 broadcast_in_dim.4
  4.2 22.0 %all-to-all-start = ((bf16[32,8,1536]{2,1,0:T(8,128)(2,1)}), bf16[32,8,1536]{2,1,0:T(8,128)(2,1)S(1)}, u32[]{:S(2)}, u32[]{:S(2)}) async-start(bf16[32,8,1536]{2,1,0:T(8,128)(2,1)} %broadcast_in_dim.4), calls=%async_computation | async-start | bytes 1572864 | tf_op jit(solution)/shard_map/all_to_all | solution.py:329
  26.5 0.7 copy.42
  27.5 0.7 fusion.7
  28.2 0.7 copy-done.14
  28.9 0.8 expand_hidden.1
  29.7 0.7 multiply_exponential_fusion.power_ref
  30.4 0.7 subtract_convert_fusion
  31.1 1.7 copy-done.13
  32.8 2.5 %rotate_weight.1.w_ref = bf16[192,6144]{1,0:T(8,128)(2,1)S(1)} custom-call(bf16[192,6144]{1,0:T(8,128)(2,1)S(1)} %copy-done.13, f32[1,6144]{1,0:T(1,128)S(1)} %bitcast.14, bf16[128,128]{1,0:T(8,128)(2,1)S(1)} %copy-done.9), custom_call_target="tpu_custom_call" | custom-call | flops 2415919104 | bytes 5242880 | tf_op jit(solution)/shard_map/rotate_weight/pallas_call | solution.py:273
  35.3 1.4 copy-done.15
  36.7 1.0 constant_dynamic-slice_fusion.1.weight_ref
  37.7 14.2 %all-to-all-done = bf16[32,8,1536]{2,1,0:T(8,128)(2,1)S(1)} async-done(((bf16[32,8,1536]{2,1,0:T(8,128)(2,1)}), bf16[32,8,1536]{2,1,0:T(8,128)(2,1)S(1)}, u32[]{:S(2)}, u32[]{:S(2)}) %all-to-all-start) | async-done | bytes 786464 | tf_op jit(solution)/shard_map/all_to_all | solution.py:329
  51.9 1.9 %collective-permute-start = (bf16[256,1536]{1,0:T(8,128)(2,1)S(1)}, bf16[256,1536]{1,0:T(8,128)(2,1)S(1)}, u32[]{:S(2)}, u32[]{:S(2)}) collective-permute-start(bf16[256,1536]{1,0:T(8,128)(2,1)S(1)} %bitcast.10), channel_id=1, source_target_pairs={{0,1},{1,0},{2,3},{3,2},{4,5},{5,4},{6,7},{7,6},{8,9},{9,8},{10,11... | collective-permute-start | bytes 2359304 | tf_op jit(solution)/shard_map/ppermute | solution.py:361
  53.8 2.3 %collective-permute-done.other_ref = bf16[256,1536]{1,0:T(8,128)(2,1)S(1)} collective-permute-done((bf16[256,1536]{1,0:T(8,128)(2,1)S(1)}, bf16[256,1536]{1,0:T(8,128)(2,1)S(1)}, u32[]{:S(2)}, u32[]{:S(2)}) %collective-permute-start) | collective-permute-done | bytes 786464 | tf_op jit(solution)/shard_map/ppermute | solution.py:361
  56.1 2.8 %encode.1 = bf16[752,1664]{1,0:T(8,128)(2,1)} custom-call(bf16[768,512]{1,0:T(8,128)(2,1)S(1)} %get-tuple-element.21.left_ref, bf16[256,1536]{1,0:T(8,128)(2,1)S(1)} %bitcast.11, bf16[256,1536]{1,0:T(8,128)(2,1)S(1)} %collective-permute-done.other_ref, f32[768,6]{1,0:T(8,128)S(1)} %get-tuple-element.22.scale_ref), custom_call_target="tpu_custom_call" | custom-call | flops 1182793728 | bytes 6291456 | tf_op jit(solution)/shard_map/encode/pallas_call | solution.py:166
  58.9 0.9 copy-done.1
  59.8 47.4 %fusion = bf16[48,1664]{1,0:T(8,128)(2,1)S(1)} fusion(bf16[752,1664]{1,0:T(8,128)(2,1)} %encode.1), kind=kCustom, calls=%all-reduce-scatter | all-reduce-scatter fusion | flops 1277953 | bytes 2666496
  107.2 1.7 collective-permute-start.1
  108.9 1.3 dynamic-slice.4
  111.3 1.7 update.1
  113.0 1.6 broadcast_in_dim.5
  114.7 6.3 %all-to-all-start.1 = ((bf16[16,48,1536]{2,1,0:T(8,128)(2,1)}), bf16[16,48,1536]{2,1,0:T(8,128)(2,1)S(1)}, u32[]{:S(2)}, u32[]{:S(2)}) async-start(bf16[16,48,1536]{2,1,0:T(8,128)(2,1)} %broadcast_in_dim.5), calls=%async_computation.1 | async-start | bytes 4718592 | tf_op jit(solution)/shard_map/all_to_all | solution.py:329
  121.0 1.1 copy-done.2
  122.1 1.7 copy-done.16
  123.7 2.4 %pre_grad.1 = bf16[128,192]{1,0:T(8,128)(2,1)S(1)} custom-call(bf16[256,1536]{1,0:T(8,128)(2,1)S(1)} %bitcast.12, bf16[256,1536]{1,0:T(8,128)(2,1)S(1)} %copy-done.2, bf16[192,6144]{1,0:T(8,128)(2,1)S(1)} %copy-done.16, f32[128,192]{1,0:T(8,128)S(1)} %copy-done.10, bf16[128,512]{1,0:T(8,128)(2,1)S(1)} %copy-done.7), custom_call_target="tpu_custom_call" | custom-call | flops 1207959552 | bytes 6291456 | tf_op jit(solution)/shard_map/pre_grad/pallas_call | solution.py:316
  126.4 0.7 copy.41
  127.1 42.3 %all-to-all-done.1.gathered_ref = bf16[16,48,1536]{2,1,0:T(8,128)(2,1)S(1)} async-done(((bf16[16,48,1536]{2,1,0:T(8,128)(2,1)}), bf16[16,48,1536]{2,1,0:T(8,128)(2,1)S(1)}, u32[]{:S(2)}, u32[]{:S(2)}) %all-to-all-start.1) | async-done | bytes 2359328 | tf_op jit(solution)/shard_map/all_to_all | solution.py:329
  169.5 2.0 %place.1 = bf16[192,6144]{1,0:T(8,128)(2,1)} custom-call(bf16[16,48,1536]{2,1,0:T(8,128)(2,1)S(1)} %all-to-all-done.1.gathered_ref), custom_call_target="tpu_custom_call" | custom-call | tf_op jit(solution)/shard_map/place/pallas_call | solution.py:249
  (50 shorter events, 1.5 us)
Async XLA Ops:
  0.6 27.5 %copy-start.7 = (bf16[128,512]{1,0:T(8,128)(2,1)S(1)}, bf16[128,512]{1,0:T(8,128)(2,1)}, u32[]{:S(2)}) copy-start(bf16[128,512]{1,0:T(8,128)(2,1)} %constant.52.clone.widen_ref.collect_ref) | copy-start | bytes 393220
  0.6 27.5 %copy-start.6 = (bf16[768,36]{1,0:T(8,128)(2,1)S(1)}, bf16[768,36]{1,0:T(8,128)(2,1)}, u32[]{:S(2)}) copy-start(bf16[768,36]{1,0:T(8,128)(2,1)} %constant.54.clone.choice_ref) | copy-start | bytes 165892
  0.7 27.5 %copy-start = (bf16[768,512]{1,0:T(8,128)(2,1)S(1)}, bf16[768,512]{1,0:T(8,128)(2,1)}, u32[]{:S(2)}) copy-start(bf16[768,512]{1,0:T(8,128)(2,1)} %constant.53.clone.same_ref) | copy-start | bytes 2359300
  0.7 27.5 %copy-start.5 = (bf16[768,192]{1,0:T(8,128)(2,1)S(1)}, bf16[768,192]{1,0:T(8,128)(2,1)}, u32[]{:S(2)}) copy-start(bf16[768,192]{1,0:T(8,128)(2,1)} %constant.51.clone.spread_ref) | copy-start | bytes 884740
  0.7 0.9 copy-start.8
  1.6 0.7 copy-start.11
  2.3 0.7 copy-start.12
  3.0 23.1 %copy-start.18 = (s32[192,6]{0,1:T(8,128)S(1)}, s32[192,6]{0,1:T(8,128)}, u32[]{:S(2)}) copy-start(s32[192,6]{0,1:T(8,128)} %param.19) | copy-start | bytes 13828
  3.0 23.2 %copy-start.17 = (bf16[128,192]{0,1:T(8,128)(2,1)S(1)}, bf16[128,192]{0,1:T(8,128)(2,1)}, u32[]{:S(2)}) copy-start(bf16[128,192]{0,1:T(8,128)(2,1)} %param.14) | copy-start | bytes 147460
  3.2 27.9 %copy-start.9 = (bf16[128,128]{1,0:T(8,128)(2,1)S(1)}, bf16[128,128]{1,0:T(8,128)(2,1)}, u32[]{:S(2)}) copy-start(bf16[128,128]{1,0:T(8,128)(2,1)} %constant.56.clone.had_ref) | copy-start | bytes 98308
  4.2 47.7 %all-to-all-start = ((bf16[32,8,1536]{2,1,0:T(8,128)(2,1)}), bf16[32,8,1536]{2,1,0:T(8,128)(2,1)S(1)}, u32[]{:S(2)}, u32[]{:S(2)}) async-start(bf16[32,8,1536]{2,1,0:T(8,128)(2,1)} %broadcast_in_dim.4), calls=%async_computation | async-start | bytes 1572864 | tf_op jit(solution)/shard_map/all_to_all | solution.py:329
  28.2 0.7 copy-start.14
  31.1 1.7 copy-start.13
  35.2 1.4 copy-start.15
  51.9 4.2 %collective-permute-start = (bf16[256,1536]{1,0:T(8,128)(2,1)S(1)}, bf16[256,1536]{1,0:T(8,128)(2,1)S(1)}, u32[]{:S(2)}, u32[]{:S(2)}) collective-permute-start(bf16[256,1536]{1,0:T(8,128)(2,1)S(1)} %bitcast.10), channel_id=1, source_target_pairs={{0,1},{1,0},{2,3},{3,2},{4,5},{5,4},{6,7},{7,6},{8,9},{9,8},{10,11... | collective-permute-start | bytes 2359304 | tf_op jit(solution)/shard_map/ppermute | solution.py:361
  58.9 0.9 copy-start.1
  59.8 51.5 %copy-start.3 = (f32[12,6144]{1,0:T(8,128)S(1)}, f32[12,6144]{1,0:T(8,128)}, u32[]{:S(2)}) copy-start(f32[12,6144]{1,0:T(8,128)} %first_ref.1) | copy-start | bytes 884740
  59.8 51.5 %copy-start.4 = (f32[12,6144]{1,0:T(8,128)S(1)}, f32[12,6144]{1,0:T(8,128)}, u32[]{:S(2)}) copy-start(f32[12,6144]{1,0:T(8,128)} %second_ref.1) | copy-start | bytes 884740
  107.2 3.6 %collective-permute-start.1 = (bf16[15,1664]{1,0:T(8,128)(2,1)S(1)}, bf16[15,1664]{1,0:T(8,128)(2,1)S(1)}, u32[]{:S(2)}, u32[]{:S(2)}) collective-permute-start(bf16[15,1664]{1,0:T(8,128)(2,1)S(1)} %slice.26), channel_id=1, source_target_pairs={{0,64},{64,128},{128,192},{192,256},{256,320},{320,384},{384,448},... | collective-permute-start | bytes 149768
  114.7 6.3 %copy-start.10 = (f32[128,192]{1,0:T(8,128)S(1)}, f32[128,192]{1,0:T(8,128)}, u32[]{:S(2)}) copy-start(f32[128,192]{1,0:T(8,128)} %get-tuple-element.46.slope_ref) | copy-start | bytes 294916
  114.7 54.8 %all-to-all-start.1 = ((bf16[16,48,1536]{2,1,0:T(8,128)(2,1)}), bf16[16,48,1536]{2,1,0:T(8,128)(2,1)S(1)}, u32[]{:S(2)}, u32[]{:S(2)}) async-start(bf16[16,48,1536]{2,1,0:T(8,128)(2,1)} %broadcast_in_dim.5), calls=%async_computation.1 | async-start | bytes 4718592 | tf_op jit(solution)/shard_map/all_to_all | solution.py:329
  120.9 1.1 copy-start.2
  122.1 1.7 copy-start.16

commit v6 on v5

--- a/solution.py
+++ b/solution.py
@@ -19,7 +19,8 @@
 SEGS = 4
 SEG = 1536
 BLOCKS = 6
-KEPT = 47
+LINE = 8
+KEPT = 95
 SPARE = 128
 TILE = 256
 TOK = 128
@@ -39,9 +40,10 @@
 
 
 def tables():
-    owner = np.concatenate([np.repeat(np.arange(REPLICAS), KEPT), np.arange(REPLICAS)])
-    part = np.concatenate([np.tile(np.arange(KEPT), REPLICAS), np.full(REPLICAS, KEPT)])
-    segment, own = part // OWN, part % OWN
+    line = np.concatenate([np.repeat(np.arange(LINE), KEPT), np.arange(LINE)])
+    part = np.concatenate([np.tile(np.arange(KEPT), LINE), np.full(LINE, KEPT)])
+    owner = part // (SEGS * OWN) * LINE + line
+    segment, own = part // OWN % SEGS, part % OWN
     spread = (owner * OWN + own)[:, None] == np.arange(ROWS)[None, :]
     col = np.arange(2 * PEERS * SEGS * 2)
     patch = col // (SEGS * 2) * 2 + col % 2
@@ -76,7 +78,18 @@
     return pltpu.CompilerParams(vmem_limit_bytes=mebibytes << 20)
 
 
-def rotate_upstream_kernel(u_ref, sign_ref, had_ref, out_ref, x_ref, z_ref):
+def rotate_upstream_kernel(
+    u_hbm, sign_hbm, had_hbm, out_ref, u_ref, sign_ref, had_ref, x_ref, z_ref, sems
+):
+    pairs = ((u_hbm, u_ref), (sign_hbm, sign_ref), (had_hbm, had_ref))
+    copies = [
+        pltpu.make_async_copy(source, target, sems.at[k])
+        for k, (source, target) in enumerate(pairs)
+    ]
+    for copy in copies:
+        copy.start()
+    for copy in copies:
+        copy.wait()
     turned = u_ref[...].astype(f32) * (1 - 2 * sign_ref[...]).astype(f32)
     for t in range(COLS // LANES):
         x_ref[2 * t : 2 * t + 2, :] = turned[:, LANES * t : LANES * (t + 1)]
@@ -94,16 +107,23 @@
 
 
 def rotate_upstream(upstream, signs, had):
+    arrays = [
+        pltpu.with_memory_space_constraint(array, pltpu.HBM)
+        for array in (upstream, signs, had)
+    ]
     return pl.pallas_call(
         rotate_upstream_kernel,
         out_shape=jax.ShapeDtypeStruct((2 * SEGS, SEG), bf16),
-        scratch_shapes=[
+        in_specs=[pl.BlockSpec(memory_space=pltpu.HBM)] * 3,
+        scratch_shapes=[pltpu.VMEM(array.shape, array.dtype) for array in arrays]
+        + [
             pltpu.VMEM((2 * COLS // LANES, LANES), f32),
             pltpu.VMEM((2 * SEGS, SEG), f32),
+            pltpu.SemaphoreType.DMA((3,)),
         ],
         compiler_params=params(),
         name="rotate_upstream",
-    )(upstream, signs, had)
+    )(*arrays)
 
 
 def expand_hidden_kernel(
@@ -140,7 +160,7 @@
 
 def encode_kernel(left_ref, own_ref, other_ref, scale_ref, out_ref, spare_ref):
     depth = own_ref.shape[0]
-    full = REPLICAS * KEPT
+    full = LINE * KEPT
     scales = scale_ref[...]
     spare_ref[...] = jnp.zeros_like(spare_ref)
     for n in range(SEG // TILE):
@@ -154,13 +174,13 @@
         total = jnp.clip(total * scales[:, n : n + 1], -clip_limit, clip_limit)
         out_ref[:, lanes] = total[:full].astype(bf16)
         for k in range(TILE // SPARE):
-            rows = pl.ds(TILE // SPARE * n + k, REPLICAS, stride=KEPT)
+            rows = pl.ds(TILE // SPARE * n + k, LINE, stride=KEPT)
             spare_ref[rows, :] = total[full:, SPARE * k : SPARE * (k + 1)]
     out_ref[:, SEG:] = spare_ref[...].astype(bf16)
 
 
 def encode(left, own, other, scale):
-    full = REPLICAS * KEPT
+    full = LINE * KEPT
     depth = own.shape[0]
     shape = (full, SEG + SPARE)
     return pl.pallas_call(
@@ -178,14 +198,38 @@
     )(left, own, other, scale)
 
 
+def split_kernel(plane_ref, summed_ref, kept_ref, given_ref, rows_ref):
+    total = summed_ref[...].astype(f32)
+    rows_ref[:KEPT, :] = total[:, :SEG]
+    for k in range(SEG // SPARE):
+        rows_ref[KEPT : KEPT + 1, SPARE * k : SPARE * (k + 1)] = total[k : k + 1, SEG:]
+    upper = rows_ref[: SEGS * OWN, :].astype(bf16)
+    lower = rows_ref[SEGS * OWN :, :].astype(bf16)
+    first = plane_ref[0] == 0
+    kept_ref[...] = jnp.where(first, upper, lower)
+    given_ref[...] = jnp.where(first, lower, upper)
+
+
+def split(plane, summed):
+    part = jax.ShapeDtypeStruct((SEGS * OWN, SEG), bf16)
+    return pl.pallas_call(
+        split_kernel,
+        out_shape=(part, part),
+        in_specs=[
+            pl.BlockSpec(memory_space=pltpu.SMEM),
+            pl.BlockSpec(memory_space=pltpu.VMEM),
+        ],
+        scratch_shapes=[pltpu.VMEM((2 * SEGS * OWN, SEG), f32)],
+        compiler_params=params(),
+        name="split",
+    )(plane, summed)
+
+
 def update_kernel(
-    received_ref, power_ref, sign_ref, had_ref, first_ref, second_ref, weight_ref,
+    kept_ref, taken_ref, power_ref, sign_ref, had_ref, first_ref, second_ref, weight_ref,
     mean_ref, first_out, second_out, sent_ref, sum_ref, x_ref, y_ref,
 ):
-    total = received_ref[...].astype(f32)
-    sum_ref[:KEPT, :] = total[:, :SEG]
-    for k in range(SEG // SPARE):
-        sum_ref[KEPT : KEPT + 1, SPARE * k : SPARE * (k + 1)] = total[k : k + 1, SEG:]
+    sum_ref[...] = kept_ref[...].astype(f32) + taken_ref[...].astype(f32)
     x_ref[...] = jnp.zeros_like(x_ref)
     for t in range(COLS // LANES):
         s, lane = divmod(t, SEG // LANES)
@@ -220,7 +264,7 @@
     sent_ref[...] = sum_ref[...].astype(bf16)
 
 
-def update(received, power, sign_row, had, first, second, weight):
+def update(kept, taken, power, sign_row, had, first, second, weight):
     own = jax.ShapeDtypeStruct((OWN, COLS), f32)
     return pl.pallas_call(
         update_kernel,
@@ -232,7 +276,7 @@
         ],
         compiler_params=params(),
         name="update",
-    )(received, power, sign_row, had, first, second, weight)
+    )(kept, taken, power, sign_row, had, first, second, weight)
 
 
 def place_kernel(gathered_ref, out_ref, rows_ref):
@@ -360,10 +404,12 @@
     )
     other = lax.ppermute(own, "core", [(0, 1), (1, 0)])
     encoded = encode(left, own, other, scale)
-    summed = lax.psum_scatter(encoded, ("z_lo", "x"), scatter_dimension=0, tiled=True)
-    grad_mean, first_new, second_new, sent = update(
-        summed, own_power, sign_row, had, first_moment, second_moment, own_weight
-    )
+    summed = lax.psum_scatter(encoded, "x", scatter_dimension=0, tiled=True)
+    plane = lax.axis_index("z_lo").astype(jnp.int32).reshape(1)
+    kept, given = split(plane, summed)
+    taken = lax.ppermute(given, "z_lo", [(0, 1), (1, 0)])
+    states = (own_power, sign_row, had, first_moment, second_moment, own_weight)
+    grad_mean, first_new, second_new, sent = update(kept, taken, *states)
     weight_new = place(to_all(sent, ("z_lo", "x"), REPLICAS))
 
     mixed = pre_grad_product(own, other, turned_weight, slope, widen)

time: 172 us -> 175 us (1.017)
  the two profiles are of different devices: /device:TPU:16 before, /device:TPU:18 now
where the time goes in v6:
time: 175 us
  waiting for transfers between devices  66.2 us (38%)
  starting transfers between devices  39.5 us (23%)
  blocking collectives  35.2 us (20%)
  local copies, waits for them, and re-layouts  16.4 us (9%)
  Pallas kernels  13.4 us (8%)
  other arithmetic  2.35 us (1%)
    all_to_all x2, waiting for transfers between devices, to_all(): lax.all_to_all(jnp.broadcast_to(values[None], (count,) + values.shape), a...  59.4 us
    unnamed x1, blocking collectives  35.2 us
    all_to_all x2, starting transfers between devices, to_all(): lax.all_to_all(jnp.broadcast_to(values[None], (count,) + values.shape), a...  31 us
    unnamed x39, local copies, waits for them, and re-layouts  12.3 us
    ppermute x1, starting transfers between devices, body(): taken = lax.ppermute(given, 'z_lo', [(0, 1), (1, 0)])  4.18 us
  transfers between devices with their start and end apart: 5, of which 5 were waited for; matrix products, arithmetic and copies ran while one was open for 4% of the time, Pallas kernels for 3%

profile of v6, /device:TPU:18, one launch (start us, length us, event | category | flops | bytes accessed | tf_op | source)
XLA Modules:
  0.0 174.6 jit_solution(6720763416555743076)
XLA Ops:
  0.7 1.1 rotate_upstream.1
  1.8 1.0 broadcast_in_dim.4
  2.8 22.0 %all-to-all-start = ((bf16[32,8,1536]{2,1,0:T(8,128)(2,1)}), bf16[32,8,1536]{2,1,0:T(8,128)(2,1)S(1)}, u32[]{:S(2)}, u32[]{:S(2)}) async-start(bf16[32,8,1536]{2,1,0:T(8,128)(2,1)} %broadcast_in_dim.4), calls=%async_computation | async-start | bytes 1572864 | tf_op jit(solution)/shard_map/all_to_all | solution.py:373
  26.1 0.7 fusion.7
  27.5 0.8 expand_hidden.1
  28.3 0.7 multiply_exponential_fusion.power_ref
  29.0 0.7 subtract_convert_fusion
  29.7 1.7 copy-done.10
  31.4 2.4 %rotate_weight.1.w_ref = bf16[192,6144]{1,0:T(8,128)(2,1)S(1)} custom-call(bf16[192,6144]{1,0:T(8,128)(2,1)S(1)} %copy-done.10, f32[1,6144]{1,0:T(1,128)S(1)} %bitcast.14, bf16[128,128]{1,0:T(8,128)(2,1)S(1)} %copy-done.9), custom_call_target="tpu_custom_call" | custom-call | flops 2415919104 | bytes 5242880 | tf_op jit(solution)/shard_map/rotate_weight/pallas_call | solution.py:317
  33.9 1.4 copy-done.12
  35.3 1.0 constant_dynamic-slice_fusion.1.weight_ref
  36.3 14.2 %all-to-all-done = bf16[32,8,1536]{2,1,0:T(8,128)(2,1)S(1)} async-done(((bf16[32,8,1536]{2,1,0:T(8,128)(2,1)}), bf16[32,8,1536]{2,1,0:T(8,128)(2,1)S(1)}, u32[]{:S(2)}, u32[]{:S(2)}) %all-to-all-start) | async-done | bytes 786464 | tf_op jit(solution)/shard_map/all_to_all | solution.py:373
  50.5 1.9 %collective-permute-start = (bf16[256,1536]{1,0:T(8,128)(2,1)S(1)}, bf16[256,1536]{1,0:T(8,128)(2,1)S(1)}, u32[]{:S(2)}, u32[]{:S(2)}) collective-permute-start(bf16[256,1536]{1,0:T(8,128)(2,1)S(1)} %bitcast.11), channel_id=1, source_target_pairs={{0,1},{1,0},{2,3},{3,2},{4,5},{5,4},{6,7},{7,6},{8,9},{9,8},{10,11... | collective-permute-start | bytes 2359304 | tf_op jit(solution)/shard_map/ppermute | solution.py:405
  52.4 2.3 %collective-permute-done.other_ref = bf16[256,1536]{1,0:T(8,128)(2,1)S(1)} collective-permute-done((bf16[256,1536]{1,0:T(8,128)(2,1)S(1)}, bf16[256,1536]{1,0:T(8,128)(2,1)S(1)}, u32[]{:S(2)}, u32[]{:S(2)}) %collective-permute-start) | collective-permute-done | bytes 786464 | tf_op jit(solution)/shard_map/ppermute | solution.py:405
  54.7 2.8 %encode.1 = bf16[760,1664]{1,0:T(8,128)(2,1)} custom-call(bf16[768,512]{1,0:T(8,128)(2,1)S(1)} %get-tuple-element.23.left_ref, bf16[256,1536]{1,0:T(8,128)(2,1)S(1)} %bitcast.12, bf16[256,1536]{1,0:T(8,128)(2,1)S(1)} %collective-permute-done.other_ref, f32[768,6]{1,0:T(8,128)S(1)} %get-tuple-element.24.scale_ref), custom_call_target="tpu_custom_call" | custom-call | flops 1195376640 | bytes 6291456 | tf_op jit(solution)/shard_map/encode/pallas_call | solution.py:186
  57.5 0.9 copy-done.1
  58.4 35.2 %fusion = bf16[96,1664]{1,0:T(8,128)(2,1)S(1)} fusion(bf16[760,1664]{1,0:T(8,128)(2,1)} %encode.1), kind=kCustom, calls=%all-reduce-scatter | all-reduce-scatter fusion | flops 1277953 | bytes 2852864
  93.7 2.3 %collective-permute-start.2 = (bf16[7,1664]{1,0:T(8,128)(2,1)S(1)}, bf16[7,1664]{1,0:T(8,128)(2,1)S(1)}, u32[]{:S(2)}, u32[]{:S(2)}) collective-permute-start(bf16[7,1664]{1,0:T(8,128)(2,1)S(1)} %slice.26), channel_id=1, source_target_pairs={{0,64},{64,128},{128,192},{192,256},{256,320},{320,384},{384,448},... | collective-permute-start | bytes 69896
  96.0 1.3 dynamic-slice.4
  97.9 1.5 collective-permute-done.2
  99.4 1.9 %concatenate.4 = bf16[103,1664]{1,0:T(8,128)(2,1)S(1)} concatenate(bf16[7,1664]{1,0:T(8,128)(2,1)S(1)} %collective-permute-done.2, bf16[96,1664]{1,0:T(8,128)(2,1)S(1)} %fusion), dimensions={0} | concatenate | bytes 685568
  101.5 4.2 %collective-permute-start.1 = (bf16[48,1536]{1,0:T(8,128)(2,1)S(1)}, bf16[48,1536]{1,0:T(8,128)(2,1)S(1)}, u32[]{:S(2)}, u32[]{:S(2)}) collective-permute-start(bf16[48,1536]{1,0:T(8,128)(2,1)S(1)} %get-tuple-element.26), channel_id=1, source_target_pairs={{0,512},{512,0},{1,513},{513,1},{2,514},{514,2},{3,515},{515,3},{4... | collective-permute-start | bytes 442376 | tf_op jit(solution)/shard_map/ppermute | solution.py:410
  105.7 3.1 %collective-permute-done.1.taken_ref = bf16[48,1536]{1,0:T(8,128)(2,1)S(1)} collective-permute-done((bf16[48,1536]{1,0:T(8,128)(2,1)S(1)}, bf16[48,1536]{1,0:T(8,128)(2,1)S(1)}, u32[]{:S(2)}, u32[]{:S(2)}) %collective-permute-start.1) | collective-permute-done | bytes 147488 | tf_op jit(solution)/shard_map/ppermute | solution.py:410
  108.8 1.7 update.1
  110.5 1.6 broadcast_in_dim.5
  112.1 9.1 %all-to-all-start.1 = ((bf16[16,48,1536]{2,1,0:T(8,128)(2,1)}), bf16[16,48,1536]{2,1,0:T(8,128)(2,1)S(1)}, u32[]{:S(2)}, u32[]{:S(2)}) async-start(bf16[16,48,1536]{2,1,0:T(8,128)(2,1)} %broadcast_in_dim.5), calls=%async_computation.1 | async-start | bytes 4718592 | tf_op jit(solution)/shard_map/all_to_all | solution.py:373
  121.2 1.1 copy-done.2
  122.3 1.7 copy-done.13
  124.0 2.4 %pre_grad.1 = bf16[128,192]{1,0:T(8,128)(2,1)S(1)} custom-call(bf16[256,1536]{1,0:T(8,128)(2,1)S(1)} %bitcast.13, bf16[256,1536]{1,0:T(8,128)(2,1)S(1)} %copy-done.2, bf16[192,6144]{1,0:T(8,128)(2,1)S(1)} %copy-done.13, f32[128,192]{1,0:T(8,128)S(1)} %copy-done.8, bf16[128,512]{1,0:T(8,128)(2,1)S(1)} %copy-done.7), custom_call_target="tpu_custom_call" | custom-call | flops 1207959552 | bytes 6291456 | tf_op jit(solution)/shard_map/pre_grad/pallas_call | solution.py:360
  126.7 0.7 copy.41
  127.4 45.2 %all-to-all-done.1.gathered_ref = bf16[16,48,1536]{2,1,0:T(8,128)(2,1)S(1)} async-done(((bf16[16,48,1536]{2,1,0:T(8,128)(2,1)}), bf16[16,48,1536]{2,1,0:T(8,128)(2,1)S(1)}, u32[]{:S(2)}, u32[]{:S(2)}) %all-to-all-start.1) | async-done | bytes 2359328 | tf_op jit(solution)/shard_map/all_to_all | solution.py:373
  172.6 2.0 %place.1 = bf16[192,6144]{1,0:T(8,128)(2,1)} custom-call(bf16[16,48,1536]{2,1,0:T(8,128)(2,1)S(1)} %all-to-all-done.1.gathered_ref), custom_call_target="tpu_custom_call" | custom-call | tf_op jit(solution)/shard_map/place/pallas_call | solution.py:293
  (47 shorter events, 2.4 us)
Async XLA Ops:
  0.6 26.2 %copy-start.7 = (bf16[128,512]{1,0:T(8,128)(2,1)S(1)}, bf16[128,512]{1,0:T(8,128)(2,1)}, u32[]{:S(2)}) copy-start(bf16[128,512]{1,0:T(8,128)(2,1)} %constant.52.clone.widen_ref.collect_ref) | copy-start | bytes 393220
  0.6 26.1 %copy-start.6 = (bf16[768,36]{1,0:T(8,128)(2,1)S(1)}, bf16[768,36]{1,0:T(8,128)(2,1)}, u32[]{:S(2)}) copy-start(bf16[768,36]{1,0:T(8,128)(2,1)} %constant.54.clone.choice_ref) | copy-start | bytes 165892
  0.7 26.1 %copy-start = (bf16[768,512]{1,0:T(8,128)(2,1)S(1)}, bf16[768,512]{1,0:T(8,128)(2,1)}, u32[]{:S(2)}) copy-start(bf16[768,512]{1,0:T(8,128)(2,1)} %constant.53.clone.same_ref) | copy-start | bytes 2359300
  0.7 26.1 %copy-start.5 = (bf16[768,192]{1,0:T(8,128)(2,1)S(1)}, bf16[768,192]{1,0:T(8,128)(2,1)}, u32[]{:S(2)}) copy-start(bf16[768,192]{1,0:T(8,128)(2,1)} %constant.51.clone.spread_ref) | copy-start | bytes 884740
  0.7 24.1 %copy-start.15 = (s32[192,6]{0,1:T(8,128)S(1)}, s32[192,6]{0,1:T(8,128)}, u32[]{:S(2)}) copy-start(s32[192,6]{0,1:T(8,128)} %param.19) | copy-start | bytes 13828
  0.7 24.1 %copy-start.14 = (bf16[128,192]{0,1:T(8,128)(2,1)S(1)}, bf16[128,192]{0,1:T(8,128)(2,1)}, u32[]{:S(2)}) copy-start(bf16[128,192]{0,1:T(8,128)(2,1)} %param.14) | copy-start | bytes 147460
  1.8 27.9 %copy-start.9 = (bf16[128,128]{1,0:T(8,128)(2,1)S(1)}, bf16[128,128]{1,0:T(8,128)(2,1)}, u32[]{:S(2)}) copy-start(bf16[128,128]{1,0:T(8,128)(2,1)} %constant.56.clone.had_hbm.had_ref) | copy-start | bytes 98308
  2.8 47.7 %all-to-all-start = ((bf16[32,8,1536]{2,1,0:T(8,128)(2,1)}), bf16[32,8,1536]{2,1,0:T(8,128)(2,1)S(1)}, u32[]{:S(2)}, u32[]{:S(2)}) async-start(bf16[32,8,1536]{2,1,0:T(8,128)(2,1)} %broadcast_in_dim.4), calls=%async_computation | async-start | bytes 1572864 | tf_op jit(solution)/shard_map/all_to_all | solution.py:373
  26.8 0.7 copy-start.11
  29.7 1.7 copy-start.10
  33.9 1.4 copy-start.12
  50.5 4.2 %collective-permute-start = (bf16[256,1536]{1,0:T(8,128)(2,1)S(1)}, bf16[256,1536]{1,0:T(8,128)(2,1)S(1)}, u32[]{:S(2)}, u32[]{:S(2)}) collective-permute-start(bf16[256,1536]{1,0:T(8,128)(2,1)S(1)} %bitcast.11), channel_id=1, source_target_pairs={{0,1},{1,0},{2,3},{3,2},{4,5},{5,4},{6,7},{7,6},{8,9},{9,8},{10,11... | collective-permute-start | bytes 2359304 | tf_op jit(solution)/shard_map/ppermute | solution.py:405
  57.5 0.9 copy-start.1
  58.4 50.4 %copy-start.3 = (f32[12,6144]{1,0:T(8,128)S(1)}, f32[12,6144]{1,0:T(8,128)}, u32[]{:S(2)}) copy-start(f32[12,6144]{1,0:T(8,128)} %first_ref.1) | copy-start | bytes 884740
  58.4 50.4 %copy-start.4 = (f32[12,6144]{1,0:T(8,128)S(1)}, f32[12,6144]{1,0:T(8,128)}, u32[]{:S(2)}) copy-start(f32[12,6144]{1,0:T(8,128)} %second_ref.1) | copy-start | bytes 884740
  93.7 5.7 %collective-permute-start.2 = (bf16[7,1664]{1,0:T(8,128)(2,1)S(1)}, bf16[7,1664]{1,0:T(8,128)(2,1)S(1)}, u32[]{:S(2)}, u32[]{:S(2)}) collective-permute-start(bf16[7,1664]{1,0:T(8,128)(2,1)S(1)} %slice.26), channel_id=1, source_target_pairs={{0,64},{64,128},{128,192},{192,256},{256,320},{320,384},{384,448},... | collective-permute-start | bytes 69896
  101.5 7.3 %collective-permute-start.1 = (bf16[48,1536]{1,0:T(8,128)(2,1)S(1)}, bf16[48,1536]{1,0:T(8,128)(2,1)S(1)}, u32[]{:S(2)}, u32[]{:S(2)}) collective-permute-start(bf16[48,1536]{1,0:T(8,128)(2,1)S(1)} %get-tuple-element.26), channel_id=1, source_target_pairs={{0,512},{512,0},{1,513},{513,1},{2,514},{514,2},{3,515},{515,3},{4... | collective-permute-start | bytes 442376 | tf_op jit(solution)/shard_map/ppermute | solution.py:410
  112.1 9.1 %copy-start.8 = (f32[128,192]{1,0:T(8,128)S(1)}, f32[128,192]{1,0:T(8,128)}, u32[]{:S(2)}) copy-start(f32[128,192]{1,0:T(8,128)} %get-tuple-element.50.slope_ref) | copy-start | bytes 294916
  112.1 60.4 %all-to-all-start.1 = ((bf16[16,48,1536]{2,1,0:T(8,128)(2,1)}), bf16[16,48,1536]{2,1,0:T(8,128)(2,1)S(1)}, u32[]{:S(2)}, u32[]{:S(2)}) async-start(bf16[16,48,1536]{2,1,0:T(8,128)(2,1)} %broadcast_in_dim.5), calls=%async_computation.1 | async-start | bytes 4718592 | tf_op jit(solution)/shard_map/all_to_all | solution.py:373
  121.2 1.1 copy-start.2
  122.3 1.7 copy-start.13

commit v7 on v5

--- a/solution.py
+++ b/solution.py
@@ -19,8 +19,10 @@
 SEGS = 4
 SEG = 1536
 BLOCKS = 6
+LINE = 8
 KEPT = 47
 SPARE = 128
+RING = 640
 TILE = 256
 TOK = 128
 PEERS = 32
@@ -76,7 +78,18 @@
     return pltpu.CompilerParams(vmem_limit_bytes=mebibytes << 20)
 
 
-def rotate_upstream_kernel(u_ref, sign_ref, had_ref, out_ref, x_ref, z_ref):
+def rotate_upstream_kernel(
+    u_hbm, sign_hbm, had_hbm, out_ref, u_ref, sign_ref, had_ref, x_ref, z_ref, sems
+):
+    pairs = ((u_hbm, u_ref), (sign_hbm, sign_ref), (had_hbm, had_ref))
+    copies = [
+        pltpu.make_async_copy(source, target, sems.at[k])
+        for k, (source, target) in enumerate(pairs)
+    ]
+    for copy in copies:
+        copy.start()
+    for copy in copies:
+        copy.wait()
     turned = u_ref[...].astype(f32) * (1 - 2 * sign_ref[...]).astype(f32)
     for t in range(COLS // LANES):
         x_ref[2 * t : 2 * t + 2, :] = turned[:, LANES * t : LANES * (t + 1)]
@@ -94,16 +107,23 @@
 
 
 def rotate_upstream(upstream, signs, had):
+    arrays = [
+        pltpu.with_memory_space_constraint(array, pltpu.HBM)
+        for array in (upstream, signs, had)
+    ]
     return pl.pallas_call(
         rotate_upstream_kernel,
         out_shape=jax.ShapeDtypeStruct((2 * SEGS, SEG), bf16),
-        scratch_shapes=[
+        in_specs=[pl.BlockSpec(memory_space=pltpu.HBM)] * 3,
+        scratch_shapes=[pltpu.VMEM(array.shape, array.dtype) for array in arrays]
+        + [
             pltpu.VMEM((2 * COLS // LANES, LANES), f32),
             pltpu.VMEM((2 * SEGS, SEG), f32),
+            pltpu.SemaphoreType.DMA((3,)),
         ],
         compiler_params=params(),
         name="rotate_upstream",
-    )(upstream, signs, had)
+    )(*arrays)
 
 
 def expand_hidden_kernel(
@@ -180,7 +200,7 @@
 
 def update_kernel(
     received_ref, power_ref, sign_ref, had_ref, first_ref, second_ref, weight_ref,
-    mean_ref, first_out, second_out, sent_ref, sum_ref, x_ref, y_ref,
+    mean_ref, first_out, second_out, ring_ref, direct_ref, sum_ref, x_ref, y_ref,
 ):
     total = received_ref[...].astype(f32)
     sum_ref[:KEPT, :] = total[:, :SEG]
@@ -217,14 +237,23 @@
             sum_ref[OWN * s : OWN * (s + 1), LANES * lane : LANES * (lane + 1)] = (
                 weight_ref[:, lanes].astype(f32) * (1.0 - 0.01 * 0.1) - 0.01 * adjusted
             )
-    sent_ref[...] = sum_ref[...].astype(bf16)
+    ring_ref[...] = sum_ref[:, :RING].astype(bf16)
+    direct_ref[...] = jnp.broadcast_to(
+        sum_ref[:, RING:].astype(bf16)[None], direct_ref.shape
+    )
 
 
 def update(received, power, sign_row, had, first, second, weight):
     own = jax.ShapeDtypeStruct((OWN, COLS), f32)
     return pl.pallas_call(
         update_kernel,
-        out_shape=(own, own, own, jax.ShapeDtypeStruct((SEGS * OWN, SEG), bf16)),
+        out_shape=(
+            own,
+            own,
+            own,
+            jax.ShapeDtypeStruct((SEGS * OWN, RING), bf16),
+            jax.ShapeDtypeStruct((REPLICAS, SEGS * OWN, SEG - RING), bf16),
+        ),
         scratch_shapes=[
             pltpu.VMEM((SEGS * OWN, SEG), f32),
             pltpu.VMEM((16 * COLS // LANES, LANES), f32),
@@ -235,24 +264,27 @@
     )(received, power, sign_row, had, first, second, weight)
 
 
-def place_kernel(gathered_ref, out_ref, rows_ref):
+def place_kernel(ring_ref, direct_ref, out_ref, rows_ref):
     for d in range(REPLICAS):
-        chunk = gathered_ref[d].astype(f32)
-        for s in range(SEGS):
-            rows_ref[OWN * d : OWN * (d + 1), SEG * s : SEG * (s + 1)] = chunk[
-                OWN * s : OWN * (s + 1), :
-            ]
+        here = d % LINE * 2 + d // LINE
+        parts = ((0, ring_ref[here].astype(f32)), (RING, direct_ref[d].astype(f32)))
+        for lane, chunk in parts:
+            for s in range(SEGS):
+                start = SEG * s + lane
+                rows_ref[OWN * d : OWN * (d + 1), start : start + chunk.shape[1]] = (
+                    chunk[OWN * s : OWN * (s + 1), :]
+                )
     out_ref[...] = rows_ref[...].astype(bf16)
 
 
-def place(gathered):
+def place(ring, direct):
     return pl.pallas_call(
         place_kernel,
         out_shape=jax.ShapeDtypeStruct((ROWS, COLS), bf16),
         scratch_shapes=[pltpu.VMEM((ROWS, COLS), f32)],
         compiler_params=params(20),
         name="place",
-    )(gathered)
+    )(ring, direct)
 
 
 def rotate_weight_kernel(w_ref, sign_ref, had_ref, out_ref):
@@ -361,10 +393,19 @@
     other = lax.ppermute(own, "core", [(0, 1), (1, 0)])
     encoded = encode(left, own, other, scale)
     summed = lax.psum_scatter(encoded, ("z_lo", "x"), scatter_dimension=0, tiled=True)
-    grad_mean, first_new, second_new, sent = update(
+    grad_mean, first_new, second_new, ring, direct = update(
         summed, own_power, sign_row, had, first_moment, second_moment, own_weight
     )
-    weight_new = place(to_all(sent, ("z_lo", "x"), REPLICAS))
+    across = lax.ppermute(ring, "z_lo", [(0, 1), (1, 0)])
+    both = jnp.where(
+        lax.axis_index("z_lo") == 0,
+        jnp.concatenate([ring, across], axis=0),
+        jnp.concatenate([across, ring], axis=0),
+    )
+    both, own, direct = lax.optimization_barrier((both, own, direct))
+    direct = lax.all_to_all(direct, ("z_lo", "x"), 0, 0, tiled=True)
+    ring = lax.all_gather(both, "x", axis=0, tiled=True)
+    weight_new = place(ring.reshape(REPLICAS, SEGS * OWN, RING), direct)
 
     mixed = pre_grad_product(own, other, turned_weight, slope, widen)
     halves = mixed.reshape(2, PEERS, 2, ROWS)

time: 172 us -> 174 us (1.012)
  blocking collectives: 47.4 us -> 89.1 us
  waiting for transfers between devices: 58.8 us -> 22 us
  local copies, waits for them, and re-layouts: 17.2 us -> 10.8 us
  starting transfers between devices: 31.8 us -> 36 us
  other arithmetic: 2.35 us -> 0.29 us
    all_gather x0 -> x1, blocking collectives: none -> 41.8 us  [body(): ring = lax.all_gather(both, 'x', axis=0, tiled=True)]
    all_to_all x2 -> x1, waiting for transfers between devices: 56.6 us -> 16.6 us  [to_all(): lax.all_to_all(jnp.broadcast_to(values[None], (count,) + values.shape), a...]
    ppermute x0 -> x1, starting transfers between devices: none -> 6.71 us  [body(): across = lax.ppermute(ring, 'z_lo', [(0, 1), (1, 0)])]
    all_to_all x2 -> x1, starting transfers between devices: 28.2 us -> 22 us  [to_all(): lax.all_to_all(jnp.broadcast_to(values[None], (count,) + values.shape), a...]
    unnamed x45 -> x39, local copies, waits for them, and re-layouts: 13.1 us -> 8.41 us
    all_to_all x0 -> x1, starting transfers between devices: none -> 3.71 us  [body(): direct = lax.all_to_all(direct, ('z_lo', 'x'), 0, 0, tiled=True)]
    ppermute x0 -> x1, waiting for transfers between devices: none -> 3.1 us  [body(): across = lax.ppermute(ring, 'z_lo', [(0, 1), (1, 0)])]
  transfers between devices with their start and end apart: 4 -> 5, of which waited for: 3 -> 3; matrix products, arithmetic and copies ran while one was open for 4% -> 2% of each run, Pallas kernels for 3% -> 3%
where the time goes in v7:
time: 174 us
  blocking collectives  89.1 us (51%)
  starting transfers between devices  36 us (21%)
  waiting for transfers between devices  22 us (13%)
  Pallas kernels  13.9 us (8%)
  local copies, waits for them, and re-layouts  10.8 us (6%)
    unnamed x1, blocking collectives  47.4 us
    all_gather x1, blocking collectives, body(): ring = lax.all_gather(both, 'x', axis=0, tiled=True)  41.8 us
    all_to_all x1, starting transfers between devices, to_all(): lax.all_to_all(jnp.broadcast_to(values[None], (count,) + values.shape), a...  22 us
    all_to_all x1, waiting for transfers between devices, to_all(): lax.all_to_all(jnp.broadcast_to(values[None], (count,) + values.shape), a...  16.6 us
    unnamed x39, local copies, waits for them, and re-layouts  8.41 us
    ppermute x1, starting transfers between devices, body(): across = lax.ppermute(ring, 'z_lo', [(0, 1), (1, 0)])  6.71 us
    all_to_all x1, starting transfers between devices, body(): direct = lax.all_to_all(direct, ('z_lo', 'x'), 0, 0, tiled=True)  3.71 us
  transfers between devices with their start and end apart: 5, of which 3 were waited for; matrix products, arithmetic and copies ran while one was open for 2% of the time, Pallas kernels for 3%

profile of v7, /device:TPU:16, one launch (start us, length us, event | category | flops | bytes accessed | tf_op | source)
XLA Modules:
  0.0 173.7 jit_solution(8179277763051552212)
XLA Ops:
  0.7 1.1 rotate_upstream.1
  1.8 0.9 broadcast_in_dim.2
  2.8 22.0 %all-to-all-start = ((bf16[32,8,1536]{2,1,0:T(8,128)(2,1)}), bf16[32,8,1536]{2,1,0:T(8,128)(2,1)S(1)}, u32[]{:S(2)}, u32[]{:S(2)}) async-start(bf16[32,8,1536]{2,1,0:T(8,128)(2,1)} %broadcast_in_dim.2), calls=%async_computation | async-start | bytes 1572864 | tf_op jit(solution)/shard_map/all_to_all | solution.py:361
  24.8 0.1 copy.36
  25.0 0.1 constant_dynamic-slice_fusion.2
  25.2 0.1 copy.37.shrink_ref
  25.4 0.1 copy.42
  25.5 0.1 fusion.7
  25.6 0.8 expand_hidden.1
  26.4 0.9 copy-done.1
  27.3 1.7 copy-done.9
  29.0 2.5 %rotate_weight.1.w_ref = bf16[192,6144]{1,0:T(8,128)(2,1)S(1)} custom-call(bf16[192,6144]{1,0:T(8,128)(2,1)S(1)} %copy-done.9, f32[1,6144]{1,0:T(1,128)S(1)} %bitcast.15, bf16[128,128]{1,0:T(8,128)(2,1)S(1)} %copy-done.8), custom_call_target="tpu_custom_call" | custom-call | flops 2415919104 | bytes 5242880 | tf_op jit(solution)/shard_map/rotate_weight/pallas_call | solution.py:305
  31.5 1.4 copy-done.11
  32.9 1.0 constant_dynamic-slice_fusion.1.weight_ref
  33.9 16.6 %all-to-all-done = bf16[32,8,1536]{2,1,0:T(8,128)(2,1)S(1)} async-done(((bf16[32,8,1536]{2,1,0:T(8,128)(2,1)}), bf16[32,8,1536]{2,1,0:T(8,128)(2,1)S(1)}, u32[]{:S(2)}, u32[]{:S(2)}) %all-to-all-start) | async-done | bytes 786464 | tf_op jit(solution)/shard_map/all_to_all | solution.py:361
  50.5 1.9 %collective-permute-start = (bf16[256,1536]{1,0:T(8,128)(2,1)S(1)}, bf16[256,1536]{1,0:T(8,128)(2,1)S(1)}, u32[]{:S(2)}, u32[]{:S(2)}) collective-permute-start(bf16[256,1536]{1,0:T(8,128)(2,1)S(1)} %bitcast.12), channel_id=1, source_target_pairs={{0,1},{1,0},{2,3},{3,2},{4,5},{5,4},{6,7},{7,6},{8,9},{9,8},{10,11... | collective-permute-start | bytes 2359304 | tf_op jit(solution)/shard_map/ppermute | solution.py:393
  52.4 2.3 %collective-permute-done.other_ref = bf16[256,1536]{1,0:T(8,128)(2,1)S(1)} collective-permute-done((bf16[256,1536]{1,0:T(8,128)(2,1)S(1)}, bf16[256,1536]{1,0:T(8,128)(2,1)S(1)}, u32[]{:S(2)}, u32[]{:S(2)}) %collective-permute-start) | collective-permute-done | bytes 786464 | tf_op jit(solution)/shard_map/ppermute | solution.py:393
  54.7 2.9 %encode.1 = bf16[752,1664]{1,0:T(8,128)(2,1)} custom-call(bf16[768,512]{1,0:T(8,128)(2,1)S(1)} %copy-done.2, bf16[256,1536]{1,0:T(8,128)(2,1)S(1)} %bitcast.13, bf16[256,1536]{1,0:T(8,128)(2,1)S(1)} %collective-permute-done.other_ref, f32[768,6]{1,0:T(8,128)S(1)} %get-tuple-element.25.scale_ref), custom_call_target="tpu_custom_call" | custom-call | flops 1182793728 | bytes 6291456 | tf_op jit(solution)/shard_map/encode/pallas_call | solution.py:186
  57.5 47.4 %fusion = bf16[48,1664]{1,0:T(8,128)(2,1)S(1)} fusion(bf16[752,1664]{1,0:T(8,128)(2,1)} %encode.1), kind=kCustom, calls=%all-reduce-scatter | all-reduce-scatter fusion | flops 1277953 | bytes 2666496
  104.9 1.7 collective-permute-start.2
  106.6 1.3 dynamic-slice.4
  108.6 0.4 concatenate.12
  109.1 2.2 %update.1 = (f32[12,6144]{1,0:T(8,128)}, f32[12,6144]{1,0:T(8,128)}, f32[12,6144]{1,0:T(8,128)}, bf16[48,640]{1,0:T(8,128)(2,1)S(1)}, bf16[16,48,896]{2,1,0:T(8,128)(2,1)}) custom-call(bf16[47,1664]{1,0:T(8,128)(2,1)S(1)} %constant_dynamic-slice_fusion.received_ref, f32[12,6]{1,0:T(8,128)S(1)} %multiply_exponential_fusion.power_ref, f32[1,6144]{1,0:T(1,128)S(1)} %bitcast.16, ...), custom_call_target="tpu_custom_call" | custom-call | tf_op jit(solution)/shard_map/update/pallas_call | solution.py:248
  111.3 6.7 %collective-permute-start.1 = (bf16[48,640]{1,0:T(8,128)(2,1)S(1)}, bf16[48,640]{1,0:T(8,128)(2,1)S(1)}, u32[]{:S(2)}, u32[]{:S(2)}) collective-permute-start(bf16[48,640]{1,0:T(8,128)(2,1)S(1)} %get-tuple-element.28), channel_id=1, source_target_pairs={{0,512},{512,0},{1,513},{513,1},{2,514},{514,2},{3,515},{515,3},{4... | collective-permute-start | bytes 184328 | tf_op jit(solution)/shard_map/ppermute | solution.py:399
  118.0 3.1 %collective-permute-done.1 = bf16[48,640]{1,0:T(8,128)(2,1)S(1)} collective-permute-done((bf16[48,640]{1,0:T(8,128)(2,1)S(1)}, bf16[48,640]{1,0:T(8,128)(2,1)S(1)}, u32[]{:S(2)}, u32[]{:S(2)}) %collective-permute-start.1) | collective-permute-done | bytes 61472 | tf_op jit(solution)/shard_map/ppermute | solution.py:399
  121.1 3.7 %all-to-all-start.1 = ((bf16[16,48,896]{2,1,0:T(8,128)(2,1)}), bf16[16,48,896]{2,1,0:T(8,128)(2,1)S(1)}, u32[]{:S(2)}, u32[]{:S(2)}) async-start(bf16[16,48,896]{2,1,0:T(8,128)(2,1)} %get-tuple-element.36), calls=%async_computation.1 | async-start | bytes 2752512 | tf_op jit(solution)/shard_map/all_to_all | solution.py:406
  124.9 1.7 copy-done.12
  126.5 2.4 %pre_grad.1 = bf16[128,192]{1,0:T(8,128)(2,1)S(1)} custom-call(bf16[256,1536]{1,0:T(8,128)(2,1)S(1)} %bitcast.14, bf16[256,1536]{1,0:T(8,128)(2,1)S(1)} %collective-permute-done.other_ref, bf16[192,6144]{1,0:T(8,128)(2,1)S(1)} %copy-done.12, f32[128,192]{1,0:T(8,128)S(1)} %get-tuple-element.54.slope_ref, bf16[128,512]{1,0:T(8,128)(2,1)S(1)} %copy-done.7), custom_call_target="tpu_custom_call" | custom-call | flops 1207959552 | bytes 6291456 | tf_op jit(solution)/shard_map/pre_grad/pallas_call | solution.py:348
  129.0 0.1 pad_maximum_fusion.1
  129.2 0.7 copy.41
  129.9 41.8 %all_gather.3 = bf16[768,640]{1,0:T(8,128)(2,1)S(1)} all-gather(bf16[96,640]{1,0:T(8,128)(2,1)S(1)} %maximum_select_fusion), channel_id=1, replica_groups=mesh['z_lo'=2,'x'=8,'z_hi'=4,'y'=8,'core'=2] {'x'}, dimensions={0}, use_global_device_ids=true | all-gather | bytes 1105920 | tf_op jit(solution)/shard_map/all_gather | solution.py:407
  171.7 2.0 %place.1 = bf16[192,6144]{1,0:T(8,128)(2,1)} custom-call(bf16[16,48,640]{2,1,0:T(8,128)(2,1)S(1)} %bitcast.11, bf16[16,48,896]{2,1,0:T(8,128)(2,1)S(1)} %all-to-all-done.1.direct_ref), custom_call_target="tpu_custom_call" | custom-call | tf_op jit(solution)/shard_map/place/pallas_call | solution.py:281
  (47 shorter events, 0.5 us)
Async XLA Ops:
  0.6 24.9 %copy-start.5 = (bf16[768,192]{1,0:T(8,128)(2,1)S(1)}, bf16[768,192]{1,0:T(8,128)(2,1)}, u32[]{:S(2)}) copy-start(bf16[768,192]{1,0:T(8,128)(2,1)} %constant.51.clone.spread_ref) | copy-start | bytes 884740
  0.6 24.9 %copy-start.7 = (bf16[128,512]{1,0:T(8,128)(2,1)S(1)}, bf16[128,512]{1,0:T(8,128)(2,1)}, u32[]{:S(2)}) copy-start(bf16[128,512]{1,0:T(8,128)(2,1)} %constant.52.clone.widen_ref.collect_ref) | copy-start | bytes 393220
  0.7 24.9 %copy-start = (bf16[768,512]{1,0:T(8,128)(2,1)S(1)}, bf16[768,512]{1,0:T(8,128)(2,1)}, u32[]{:S(2)}) copy-start(bf16[768,512]{1,0:T(8,128)(2,1)} %constant.53.clone.same_ref) | copy-start | bytes 2359300
  0.7 24.9 %copy-start.6 = (bf16[768,36]{1,0:T(8,128)(2,1)S(1)}, bf16[768,36]{1,0:T(8,128)(2,1)}, u32[]{:S(2)}) copy-start(bf16[768,36]{1,0:T(8,128)(2,1)} %constant.54.clone.choice_ref) | copy-start | bytes 165892
  0.7 24.9 %copy-start.10 = (bf16[36,6]{1,0:T(8,128)(2,1)S(1)}, bf16[36,6]{1,0:T(8,128)(2,1)}, u32[]{:S(2)}) copy-start(bf16[36,6]{1,0:T(8,128)(2,1)} %constant.55.clone.gather_ref) | copy-start | bytes 1300
  0.7 24.1 %copy-start.15 = (s32[192,6]{0,1:T(8,128)S(1)}, s32[192,6]{0,1:T(8,128)}, u32[]{:S(2)}) copy-start(s32[192,6]{0,1:T(8,128)} %param.19) | copy-start | bytes 13828
  0.7 24.1 %copy-start.14 = (bf16[128,192]{0,1:T(8,128)(2,1)S(1)}, bf16[128,192]{0,1:T(8,128)(2,1)}, u32[]{:S(2)}) copy-start(bf16[128,192]{0,1:T(8,128)(2,1)} %param.14) | copy-start | bytes 147460
  1.8 25.5 %copy-start.13 = (s32[6144]{0:T(1024)S(1)}, s32[6144]{0:T(1024)}, u32[]{:S(2)}) copy-start(s32[6144]{0:T(1024)} %param.18) | copy-start | bytes 73732
  1.8 25.5 %copy-start.8 = (bf16[128,128]{1,0:T(8,128)(2,1)S(1)}, bf16[128,128]{1,0:T(8,128)(2,1)}, u32[]{:S(2)}) copy-start(bf16[128,128]{1,0:T(8,128)(2,1)} %constant.56.clone.had_hbm.had_ref) | copy-start | bytes 98308
  2.8 47.7 %all-to-all-start = ((bf16[32,8,1536]{2,1,0:T(8,128)(2,1)}), bf16[32,8,1536]{2,1,0:T(8,128)(2,1)S(1)}, u32[]{:S(2)}, u32[]{:S(2)}) async-start(bf16[32,8,1536]{2,1,0:T(8,128)(2,1)} %broadcast_in_dim.2), calls=%async_computation | async-start | bytes 1572864 | tf_op jit(solution)/shard_map/all_to_all | solution.py:361
  26.4 0.9 copy-start.1
  27.3 1.7 copy-start.9
  29.0 25.7 %copy-start.2 = (bf16[768,512]{1,0:T(8,128)(2,1)S(1)}, bf16[768,512]{1,0:T(8,128)(2,1)}, u32[]{:S(2)}) copy-start(bf16[768,512]{1,0:T(8,128)(2,1)} %copy-done.1) | copy-start | bytes 2359300
  31.5 1.4 copy-start.11
  50.5 4.2 %collective-permute-start = (bf16[256,1536]{1,0:T(8,128)(2,1)S(1)}, bf16[256,1536]{1,0:T(8,128)(2,1)S(1)}, u32[]{:S(2)}, u32[]{:S(2)}) collective-permute-start(bf16[256,1536]{1,0:T(8,128)(2,1)S(1)} %bitcast.12), channel_id=1, source_target_pairs={{0,1},{1,0},{2,3},{3,2},{4,5},{5,4},{6,7},{7,6},{8,9},{9,8},{10,11... | collective-permute-start | bytes 2359304 | tf_op jit(solution)/shard_map/ppermute | solution.py:393
  57.5 51.5 %copy-start.3 = (f32[12,6144]{1,0:T(8,128)S(1)}, f32[12,6144]{1,0:T(8,128)}, u32[]{:S(2)}) copy-start(f32[12,6144]{1,0:T(8,128)} %first_ref.1) | copy-start | bytes 884740
  57.5 51.5 %copy-start.4 = (f32[12,6144]{1,0:T(8,128)S(1)}, f32[12,6144]{1,0:T(8,128)}, u32[]{:S(2)}) copy-start(f32[12,6144]{1,0:T(8,128)} %second_ref.1) | copy-start | bytes 884740
  104.9 3.6 %collective-permute-start.2 = (bf16[15,1664]{1,0:T(8,128)(2,1)S(1)}, bf16[15,1664]{1,0:T(8,128)(2,1)S(1)}, u32[]{:S(2)}, u32[]{:S(2)}) collective-permute-start(bf16[15,1664]{1,0:T(8,128)(2,1)S(1)} %slice.26), channel_id=1, source_target_pairs={{0,64},{64,128},{128,192},{192,256},{256,320},{320,384},{384,448},... | collective-permute-start | bytes 149768
  111.3 9.8 %collective-permute-start.1 = (bf16[48,640]{1,0:T(8,128)(2,1)S(1)}, bf16[48,640]{1,0:T(8,128)(2,1)S(1)}, u32[]{:S(2)}, u32[]{:S(2)}) collective-permute-start(bf16[48,640]{1,0:T(8,128)(2,1)S(1)} %get-tuple-element.28), channel_id=1, source_target_pairs={{0,512},{512,0},{1,513},{513,1},{2,514},{514,2},{3,515},{515,3},{4... | collective-permute-start | bytes 184328 | tf_op jit(solution)/shard_map/ppermute | solution.py:399
  121.1 50.5 %all-to-all-start.1 = ((bf16[16,48,896]{2,1,0:T(8,128)(2,1)}), bf16[16,48,896]{2,1,0:T(8,128)(2,1)S(1)}, u32[]{:S(2)}, u32[]{:S(2)}) async-start(bf16[16,48,896]{2,1,0:T(8,128)(2,1)} %get-tuple-element.36), calls=%async_computation.1 | async-start | bytes 2752512 | tf_op jit(solution)/shard_map/all_to_all | solution.py:406
  124.9 1.7 copy-start.12

commit v8 on v7

--- a/solution.py
+++ b/solution.py
@@ -19,10 +19,8 @@
 SEGS = 4
 SEG = 1536
 BLOCKS = 6
-LINE = 8
 KEPT = 47
 SPARE = 128
-RING = 640
 TILE = 256
 TOK = 128
 PEERS = 32
@@ -103,7 +101,7 @@
             z_ref[2 * s : 2 * s + 2, LANES * lane : LANES * (lane + 1)] = (
                 part * hadamard_norm
             )
-    out_ref[...] = z_ref[...].astype(bf16)
+    out_ref[...] = jnp.broadcast_to(z_ref[...].astype(bf16)[None], out_ref.shape)
 
 
 def rotate_upstream(upstream, signs, had):
@@ -113,7 +111,7 @@
     ]
     return pl.pallas_call(
         rotate_upstream_kernel,
-        out_shape=jax.ShapeDtypeStruct((2 * SEGS, SEG), bf16),
+        out_shape=pltpu.HBM((PEERS, 2 * SEGS, SEG), bf16),
         in_specs=[pl.BlockSpec(memory_space=pltpu.HBM)] * 3,
         scratch_shapes=[pltpu.VMEM(array.shape, array.dtype) for array in arrays]
         + [
@@ -158,13 +156,26 @@
     )(hidden, shrink, spread, widen, same, choice, gather)
 
 
-def encode_kernel(left_ref, own_ref, other_ref, scale_ref, out_ref, spare_ref):
+def encode_kernel(
+    left_ref, own_ref, other_ref, scale_ref, out_hbm, kept_hbm, done_ref, spare_ref, sems
+):
     depth = own_ref.shape[0]
     full = REPLICAS * KEPT
+    tiles = SEG // TILE
     scales = scale_ref[...]
+    copies = [pltpu.make_async_copy(other_ref, kept_hbm, sems.at[0])]
+    copies[0].start()
+
+    def leave(lanes):
+        copy = pltpu.make_async_copy(
+            done_ref.at[:, lanes], out_hbm.at[:, lanes], sems.at[len(copies)]
+        )
+        copy.start()
+        copies.append(copy)
+
     spare_ref[...] = jnp.zeros_like(spare_ref)
-    for n in range(SEG // TILE):
-        lanes = slice(TILE * n, TILE * (n + 1))
+    for n in range(tiles):
+        lanes = pl.ds(TILE * n, TILE)
         total = jnp.dot(
             left_ref[:, :depth], own_ref[:, lanes], preferred_element_type=f32
         )
@@ -172,11 +183,15 @@
             left_ref[:, depth:], other_ref[:, lanes], preferred_element_type=f32
         )
         total = jnp.clip(total * scales[:, n : n + 1], -clip_limit, clip_limit)
-        out_ref[:, lanes] = total[:full].astype(bf16)
+        done_ref[:, lanes] = total[:full].astype(bf16)
+        leave(lanes)
         for k in range(TILE // SPARE):
             rows = pl.ds(TILE // SPARE * n + k, REPLICAS, stride=KEPT)
             spare_ref[rows, :] = total[full:, SPARE * k : SPARE * (k + 1)]
-    out_ref[:, SEG:] = spare_ref[...].astype(bf16)
+    done_ref[:, SEG:] = spare_ref[...].astype(bf16)
+    leave(pl.ds(SEG, SPARE))
+    for copy in copies:
+        copy.wait()
 
 
 def encode(left, own, other, scale):
@@ -185,12 +200,14 @@
     shape = (full, SEG + SPARE)
     return pl.pallas_call(
         encode_kernel,
-        out_shape=pltpu.HBM(shape, bf16),
-        grid=(1,),
-        in_specs=[whole(array.shape) for array in (left, own, other, scale)],
-        out_specs=whole(shape),
-        scratch_shapes=[pltpu.VMEM((full, SPARE), f32)],
-        compiler_params=params(24),
+        out_shape=(pltpu.HBM(shape, bf16), pltpu.HBM(other.shape, bf16)),
+        out_specs=(pl.BlockSpec(memory_space=pltpu.HBM),) * 2,
+        scratch_shapes=[
+            pltpu.VMEM(shape, bf16),
+            pltpu.VMEM((full, SPARE), f32),
+            pltpu.SemaphoreType.DMA((SEG // TILE + 2,)),
+        ],
+        compiler_params=params(16),
         cost_estimate=pl.CostEstimate(
             flops=4 * full * depth * SEG, bytes_accessed=6 << 20, transcendentals=0
         ),
@@ -200,7 +217,7 @@
 
 def update_kernel(
     received_ref, power_ref, sign_ref, had_ref, first_ref, second_ref, weight_ref,
-    mean_ref, first_out, second_out, ring_ref, direct_ref, sum_ref, x_ref, y_ref,
+    mean_ref, first_out, second_out, sent_ref, sum_ref, x_ref, y_ref,
 ):
     total = received_ref[...].astype(f32)
     sum_ref[:KEPT, :] = total[:, :SEG]
@@ -237,10 +254,7 @@
             sum_ref[OWN * s : OWN * (s + 1), LANES * lane : LANES * (lane + 1)] = (
                 weight_ref[:, lanes].astype(f32) * (1.0 - 0.01 * 0.1) - 0.01 * adjusted
             )
-    ring_ref[...] = sum_ref[:, :RING].astype(bf16)
-    direct_ref[...] = jnp.broadcast_to(
-        sum_ref[:, RING:].astype(bf16)[None], direct_ref.shape
-    )
+    sent_ref[...] = jnp.broadcast_to(sum_ref[...].astype(bf16)[None], sent_ref.shape)
 
 
 def update(received, power, sign_row, had, first, second, weight):
@@ -251,8 +265,7 @@
             own,
             own,
             own,
-            jax.ShapeDtypeStruct((SEGS * OWN, RING), bf16),
-            jax.ShapeDtypeStruct((REPLICAS, SEGS * OWN, SEG - RING), bf16),
+            pltpu.HBM((REPLICAS, SEGS * OWN, SEG), bf16),
         ),
         scratch_shapes=[
             pltpu.VMEM((SEGS * OWN, SEG), f32),
@@ -264,27 +277,43 @@
     )(received, power, sign_row, had, first, second, weight)
 
 
-def place_kernel(ring_ref, direct_ref, out_ref, rows_ref):
-    for d in range(REPLICAS):
-        here = d % LINE * 2 + d // LINE
-        parts = ((0, ring_ref[here].astype(f32)), (RING, direct_ref[d].astype(f32)))
-        for lane, chunk in parts:
+GROUP = 4
+
+
+def place_kernel(gathered_ref, out_hbm, rows_ref, done_ref, sems):
+    step = GROUP * OWN
+    copies = []
+    for g in range(REPLICAS // GROUP):
+        for k in range(GROUP):
+            chunk = gathered_ref[GROUP * g + k].astype(f32)
             for s in range(SEGS):
-                start = SEG * s + lane
-                rows_ref[OWN * d : OWN * (d + 1), start : start + chunk.shape[1]] = (
-                    chunk[OWN * s : OWN * (s + 1), :]
-                )
-    out_ref[...] = rows_ref[...].astype(bf16)
-
-
-def place(ring, direct):
+                rows_ref[OWN * k : OWN * (k + 1), SEG * s : SEG * (s + 1)] = chunk[
+                    OWN * s : OWN * (s + 1), :
+                ]
+        rows = pl.ds(step * g, step)
+        done_ref[rows, :] = rows_ref[...].astype(bf16)
+        copy = pltpu.make_async_copy(
+            done_ref.at[rows, :], out_hbm.at[rows, :], sems.at[g]
+        )
+        copy.start()
+        copies.append(copy)
+    for copy in copies:
+        copy.wait()
+
+
+def place(gathered):
     return pl.pallas_call(
         place_kernel,
-        out_shape=jax.ShapeDtypeStruct((ROWS, COLS), bf16),
-        scratch_shapes=[pltpu.VMEM((ROWS, COLS), f32)],
-        compiler_params=params(20),
+        out_shape=pltpu.HBM((ROWS, COLS), bf16),
+        out_specs=pl.BlockSpec(memory_space=pltpu.HBM),
+        scratch_shapes=[
+            pltpu.VMEM((GROUP * OWN, COLS), f32),
+            pltpu.VMEM((ROWS, COLS), bf16),
+            pltpu.SemaphoreType.DMA((REPLICAS // GROUP,)),
+        ],
+        compiler_params=params(16),
         name="place",
-    )(ring, direct)
+    )(gathered)
 
 
 def rotate_weight_kernel(w_ref, sign_ref, had_ref, out_ref):
@@ -357,10 +386,8 @@
     )(own, other, weight, slope, collect)
 
 
-def to_all(values, axes, count):
-    return lax.all_to_all(
-        jnp.broadcast_to(values[None], (count,) + values.shape), axes, 0, 0, tiled=True
-    )
+def to_all(copies, axes):
+    return lax.all_to_all(copies, axes, 0, 0, tiled=True)
 
 
 def body(upstream, pre_act, w_down, first_moment, second_moment, signs, exponents):
@@ -369,7 +396,7 @@
     core = lax.axis_index("core")
 
     rotated = rotate_upstream(upstream, signs.reshape(1, COLS), had)
-    own = to_all(rotated, ("z_hi", "y"), PEERS).reshape(-1, SEG)
+    own = to_all(rotated, ("z_hi", "y")).reshape(-1, SEG)
 
     pairs = pre_act.reshape(PEERS, 2, 2, ROWS)
     mine = jnp.where(core == 0, pairs[:, 0], pairs[:, 1]).reshape(TOK // 2, ROWS)
@@ -391,21 +418,12 @@
         (own, left, scale, turned_weight, own_power, own_weight)
     )
     other = lax.ppermute(own, "core", [(0, 1), (1, 0)])
-    encoded = encode(left, own, other, scale)
+    encoded, other = encode(left, own, other, scale)
     summed = lax.psum_scatter(encoded, ("z_lo", "x"), scatter_dimension=0, tiled=True)
-    grad_mean, first_new, second_new, ring, direct = update(
+    grad_mean, first_new, second_new, sent = update(
         summed, own_power, sign_row, had, first_moment, second_moment, own_weight
     )
-    across = lax.ppermute(ring, "z_lo", [(0, 1), (1, 0)])
-    both = jnp.where(
-        lax.axis_index("z_lo") == 0,
-        jnp.concatenate([ring, across], axis=0),
-        jnp.concatenate([across, ring], axis=0),
-    )
-    both, own, direct = lax.optimization_barrier((both, own, direct))
-    direct = lax.all_to_all(direct, ("z_lo", "x"), 0, 0, tiled=True)
-    ring = lax.all_gather(both, "x", axis=0, tiled=True)
-    weight_new = place(ring.reshape(REPLICAS, SEGS * OWN, RING), direct)
+    weight_new = place(to_all(sent, ("z_lo", "x")))
 
     mixed = pre_grad_product(own, other, turned_weight, slope, widen)
     halves = mixed.reshape(2, PEERS, 2, ROWS)

time: 174 us -> 168 us (0.966)
  blocking collectives: 89.1 us -> 47.4 us
  waiting for transfers between devices: 22 us -> 61.4 us
  starting transfers between devices: 36 us -> 31.7 us
    all_to_all x2, waiting for transfers between devices: 16.6 us -> 59.1 us  [to_all(): return lax.all_to_all(copies, axes, 0, 0, tiled=True)]
    all_gather x1 -> x0, blocking collectives: 41.8 us -> none  [body(): ring = lax.all_gather(both, 'x', axis=0, tiled=True)]
    ppermute x1 -> x0, starting transfers between devices: 6.71 us -> none  [body(): across = lax.ppermute(ring, 'z_lo', [(0, 1), (1, 0)])]
    ppermute x1 -> x0, waiting for transfers between devices: 3.1 us -> none  [body(): across = lax.ppermute(ring, 'z_lo', [(0, 1), (1, 0)])]
    all_to_all x2, starting transfers between devices: 25.7 us -> 28.1 us  [to_all(): return lax.all_to_all(copies, axes, 0, 0, tiled=True)]
    unnamed x39 -> x41, local copies, waits for them, and re-layouts: 8.41 us -> 9.36 us
  transfers between devices with their start and end apart: 5 -> 4, of which waited for: 3 -> 3; matrix products, arithmetic and copies ran while one was open for 2% -> 2% of each run, Pallas kernels for 3% -> 3%
where the time goes in v8:
time: 168 us
  waiting for transfers between devices  61.4 us (37%)
  blocking collectives  47.4 us (28%)
  starting transfers between devices  31.7 us (19%)
  Pallas kernels  14.4 us (9%)
  local copies, waits for them, and re-layouts  10.8 us (6%)
  between operations  1.7 us (1%)
    all_to_all x2, waiting for transfers between devices, to_all(): return lax.all_to_all(copies, axes, 0, 0, tiled=True)  59.1 us
    unnamed x1, blocking collectives  47.4 us
    all_to_all x2, starting transfers between devices, to_all(): return lax.all_to_all(copies, axes, 0, 0, tiled=True)  28.1 us
    unnamed x41, local copies, waits for them, and re-layouts  9.36 us
  transfers between devices with their start and end apart: 4, of which 3 were waited for; matrix products, arithmetic and copies ran while one was open for 2% of the time, Pallas kernels for 3%

profile of v8, /device:TPU:16, one launch (start us, length us, event | category | flops | bytes accessed | tf_op | source)
XLA Modules:
  0.0 167.7 jit_solution(13873640232368905820)
XLA Ops:
  0.7 2.0 %rotate_upstream.1 = bf16[32,8,1536]{2,1,0:T(8,128)(2,1)} custom-call(bf16[2,6144]{1,0:T(2,128)(2,1)} %u_hbm.1, s32[1,6144]{1,0:T(1,128)} %bitcast.17, bf16[128,128]{1,0:T(8,128)(2,1)} %constant.56.clone.had_hbm.had_ref), custom_call_target="tpu_custom_call" | custom-call | tf_op jit(solution)/shard_map/rotate_upstream/pallas_call | solution.py:112
  2.8 22.0 %all-to-all-start = ((bf16[32,8,1536]{2,1,0:T(8,128)(2,1)}), bf16[32,8,1536]{2,1,0:T(8,128)(2,1)S(1)}, u32[]{:S(2)}, u32[]{:S(2)}) async-start(bf16[32,8,1536]{2,1,0:T(8,128)(2,1)} %rotate_upstream.1), calls=%async_computation | async-start | bytes 1572864 | tf_op jit(solution)/shard_map/all_to_all | solution.py:390
  24.8 0.1 copy.36
  25.0 0.1 broadcast_select_fusion.1
  25.0 0.1 constant_dynamic-slice_fusion.2
  25.2 0.1 copy.37.shrink_ref
  25.4 0.1 copy.42
  25.5 0.1 fusion.7
  25.6 0.8 expand_hidden.1
  26.4 0.7 copy-done.9
  27.2 1.7 copy-done.7
  28.8 2.4 %rotate_weight.1.w_ref = bf16[192,6144]{1,0:T(8,128)(2,1)S(1)} custom-call(bf16[192,6144]{1,0:T(8,128)(2,1)S(1)} %copy-done.7, f32[1,6144]{1,0:T(1,128)S(1)} %bitcast.13, bf16[128,128]{1,0:T(8,128)(2,1)S(1)} %copy-done.6), custom_call_target="tpu_custom_call" | custom-call | flops 2415919104 | bytes 5242880 | tf_op jit(solution)/shard_map/rotate_weight/pallas_call | solution.py:334
  31.3 1.4 copy-done.11
  32.7 1.0 constant_dynamic-slice_fusion.1.weight_ref
  33.7 16.8 %all-to-all-done = bf16[32,8,1536]{2,1,0:T(8,128)(2,1)S(1)} async-done(((bf16[32,8,1536]{2,1,0:T(8,128)(2,1)}), bf16[32,8,1536]{2,1,0:T(8,128)(2,1)S(1)}, u32[]{:S(2)}, u32[]{:S(2)}) %all-to-all-start) | async-done | bytes 786464 | tf_op jit(solution)/shard_map/all_to_all | solution.py:390
  50.5 1.9 %collective-permute-start = (bf16[256,1536]{1,0:T(8,128)(2,1)S(1)}, bf16[256,1536]{1,0:T(8,128)(2,1)S(1)}, u32[]{:S(2)}, u32[]{:S(2)}) collective-permute-start(bf16[256,1536]{1,0:T(8,128)(2,1)S(1)} %bitcast.10), channel_id=1, source_target_pairs={{0,1},{1,0},{2,3},{3,2},{4,5},{5,4},{6,7},{7,6},{8,9},{9,8},{10,11... | collective-permute-start | bytes 2359304 | tf_op jit(solution)/shard_map/ppermute | solution.py:420
  52.4 2.3 %collective-permute-done.other_ref = bf16[256,1536]{1,0:T(8,128)(2,1)S(1)} collective-permute-done((bf16[256,1536]{1,0:T(8,128)(2,1)S(1)}, bf16[256,1536]{1,0:T(8,128)(2,1)S(1)}, u32[]{:S(2)}, u32[]{:S(2)}) %collective-permute-start) | collective-permute-done | bytes 786464 | tf_op jit(solution)/shard_map/ppermute | solution.py:420
  54.7 2.5 %encode.1 = (bf16[752,1664]{1,0:T(8,128)(2,1)}, bf16[256,1536]{1,0:T(8,128)(2,1)}) custom-call(bf16[768,512]{1,0:T(8,128)(2,1)S(1)} %get-tuple-element.22.left_ref, bf16[256,1536]{1,0:T(8,128)(2,1)S(1)} %bitcast.11, bf16[256,1536]{1,0:T(8,128)(2,1)S(1)} %collective-permute-done.other_ref, f32[768,6]{1,0:T(8,128)S(1)} %copy-done.10), custom_call_target="tpu_custom_call" | custom-call | flops 1182793728 | bytes 6291456 | tf_op jit(solution)/shard_map/encode/pallas_call | solution.py:201
  57.2 47.4 %fusion = bf16[48,1664]{1,0:T(8,128)(2,1)S(1)} fusion(bf16[752,1664]{1,0:T(8,128)(2,1)} %get-tuple-element.26), kind=kCustom, calls=%all-reduce-scatter | all-reduce-scatter fusion | flops 1277953 | bytes 2666496
  104.6 1.7 %collective-permute-start.1 = (bf16[15,1664]{1,0:T(8,128)(2,1)S(1)}, bf16[15,1664]{1,0:T(8,128)(2,1)S(1)}, u32[]{:S(2)}, u32[]{:S(2)}) collective-permute-start(bf16[15,1664]{1,0:T(8,128)(2,1)S(1)} %slice.26), channel_id=1, source_target_pairs={{0,64},{64,128},{128,192},{192,256},{256,320},{320,384},{384,448},... | collective-permute-start | bytes 149768
  106.3 1.3 dynamic-slice.4
  108.3 0.4 concatenate.4
  108.8 2.6 %update.1 = (f32[12,6144]{1,0:T(8,128)}, f32[12,6144]{1,0:T(8,128)}, f32[12,6144]{1,0:T(8,128)}, bf16[16,48,1536]{2,1,0:T(8,128)(2,1)}) custom-call(bf16[47,1664]{1,0:T(8,128)(2,1)S(1)} %constant_dynamic-slice_fusion.received_ref, f32[12,6]{1,0:T(8,128)S(1)} %multiply_exponential_fusion.power_ref, f32[1,6144]{1,0:T(1,128)S(1)} %bitcast.14, ...), custom_call_target="tpu_custom_call" | custom-call | tf_op jit(solution)/shard_map/update/pallas_call | solution.py:262
  111.4 6.2 %all-to-all-start.1 = ((bf16[16,48,1536]{2,1,0:T(8,128)(2,1)}), bf16[16,48,1536]{2,1,0:T(8,128)(2,1)S(1)}, u32[]{:S(2)}, u32[]{:S(2)}) async-start(bf16[16,48,1536]{2,1,0:T(8,128)(2,1)} %get-tuple-element.32), calls=%async_computation.1 | async-start | bytes 4718592 | tf_op jit(solution)/shard_map/all_to_all | solution.py:390
  117.6 1.7 copy-done.12
  119.2 1.1 copy-done.13
  120.4 2.4 %pre_grad.1 = bf16[128,192]{1,0:T(8,128)(2,1)S(1)} custom-call(bf16[256,1536]{1,0:T(8,128)(2,1)S(1)} %bitcast.12, bf16[256,1536]{1,0:T(8,128)(2,1)S(1)} %copy-done.13, bf16[192,6144]{1,0:T(8,128)(2,1)S(1)} %copy-done.12, f32[128,192]{1,0:T(8,128)S(1)} %get-tuple-element.50.slope_ref, bf16[128,512]{1,0:T(8,128)(2,1)S(1)} %copy-done.5), custom_call_target="tpu_custom_call" | custom-call | flops 1207959552 | bytes 6291456 | tf_op jit(solution)/shard_map/pre_grad/pallas_call | solution.py:377
  122.9 0.1 pad_maximum_fusion.1
  123.0 0.1 reshape.86
  123.0 0.7 copy.41
  123.8 42.3 %all-to-all-done.1.gathered_ref = bf16[16,48,1536]{2,1,0:T(8,128)(2,1)S(1)} async-done(((bf16[16,48,1536]{2,1,0:T(8,128)(2,1)}), bf16[16,48,1536]{2,1,0:T(8,128)(2,1)S(1)}, u32[]{:S(2)}, u32[]{:S(2)}) %all-to-all-start.1) | async-done | bytes 2359328 | tf_op jit(solution)/shard_map/all_to_all | solution.py:390
  166.1 1.6 place.1
  (44 shorter events, 0.4 us)
Async XLA Ops:
  0.6 24.9 %copy-start.3 = (bf16[768,192]{1,0:T(8,128)(2,1)S(1)}, bf16[768,192]{1,0:T(8,128)(2,1)}, u32[]{:S(2)}) copy-start(bf16[768,192]{1,0:T(8,128)(2,1)} %constant.51.clone.spread_ref) | copy-start | bytes 884740
  0.6 24.9 %copy-start.5 = (bf16[128,512]{1,0:T(8,128)(2,1)S(1)}, bf16[128,512]{1,0:T(8,128)(2,1)}, u32[]{:S(2)}) copy-start(bf16[128,512]{1,0:T(8,128)(2,1)} %constant.52.clone.widen_ref.collect_ref) | copy-start | bytes 393220
  0.7 24.9 %copy-start = (bf16[768,512]{1,0:T(8,128)(2,1)S(1)}, bf16[768,512]{1,0:T(8,128)(2,1)}, u32[]{:S(2)}) copy-start(bf16[768,512]{1,0:T(8,128)(2,1)} %constant.53.clone.same_ref) | copy-start | bytes 2359300
  0.7 24.9 %copy-start.4 = (bf16[768,36]{1,0:T(8,128)(2,1)S(1)}, bf16[768,36]{1,0:T(8,128)(2,1)}, u32[]{:S(2)}) copy-start(bf16[768,36]{1,0:T(8,128)(2,1)} %constant.54.clone.choice_ref) | copy-start | bytes 165892
  0.7 24.9 %copy-start.8 = (bf16[36,6]{1,0:T(8,128)(2,1)S(1)}, bf16[36,6]{1,0:T(8,128)(2,1)}, u32[]{:S(2)}) copy-start(bf16[36,6]{1,0:T(8,128)(2,1)} %constant.55.clone.gather_ref) | copy-start | bytes 1300
  0.7 24.1 %copy-start.16 = (s32[192,6]{0,1:T(8,128)S(1)}, s32[192,6]{0,1:T(8,128)}, u32[]{:S(2)}) copy-start(s32[192,6]{0,1:T(8,128)} %param.19) | copy-start | bytes 13828
  0.7 24.1 %copy-start.15 = (bf16[128,192]{0,1:T(8,128)(2,1)S(1)}, bf16[128,192]{0,1:T(8,128)(2,1)}, u32[]{:S(2)}) copy-start(bf16[128,192]{0,1:T(8,128)(2,1)} %param.14) | copy-start | bytes 147460
  0.7 26.4 %copy-start.14 = (s32[6144]{0:T(1024)S(1)}, s32[6144]{0:T(1024)}, u32[]{:S(2)}) copy-start(s32[6144]{0:T(1024)} %param.18) | copy-start | bytes 73732
  0.7 26.4 %copy-start.6 = (bf16[128,128]{1,0:T(8,128)(2,1)S(1)}, bf16[128,128]{1,0:T(8,128)(2,1)}, u32[]{:S(2)}) copy-start(bf16[128,128]{1,0:T(8,128)(2,1)} %constant.56.clone.had_hbm.had_ref) | copy-start | bytes 98308
  2.8 47.7 %all-to-all-start = ((bf16[32,8,1536]{2,1,0:T(8,128)(2,1)}), bf16[32,8,1536]{2,1,0:T(8,128)(2,1)S(1)}, u32[]{:S(2)}, u32[]{:S(2)}) async-start(bf16[32,8,1536]{2,1,0:T(8,128)(2,1)} %rotate_upstream.1), calls=%async_computation | async-start | bytes 1572864 | tf_op jit(solution)/shard_map/all_to_all | solution.py:390
  26.4 0.7 copy-start.9
  27.1 1.7 copy-start.7
  28.8 25.8 %copy-start.10 = (f32[768,6]{1,0:T(8,128)S(1)}, f32[768,6]{1,0:T(8,128)}, u32[]{:S(2)}) copy-start(f32[768,6]{1,0:T(8,128)} %copy-done.9) | copy-start | bytes 55300
  31.3 1.4 copy-start.11
  50.5 4.2 %collective-permute-start = (bf16[256,1536]{1,0:T(8,128)(2,1)S(1)}, bf16[256,1536]{1,0:T(8,128)(2,1)S(1)}, u32[]{:S(2)}, u32[]{:S(2)}) collective-permute-start(bf16[256,1536]{1,0:T(8,128)(2,1)S(1)} %bitcast.10), channel_id=1, source_target_pairs={{0,1},{1,0},{2,3},{3,2},{4,5},{5,4},{6,7},{7,6},{8,9},{9,8},{10,11... | collective-permute-start | bytes 2359304 | tf_op jit(solution)/shard_map/ppermute | solution.py:420
  57.2 51.6 %copy-start.1 = (f32[12,6144]{1,0:T(8,128)S(1)}, f32[12,6144]{1,0:T(8,128)}, u32[]{:S(2)}) copy-start(f32[12,6144]{1,0:T(8,128)} %first_ref.1) | copy-start | bytes 884740
  57.2 51.6 %copy-start.2 = (f32[12,6144]{1,0:T(8,128)S(1)}, f32[12,6144]{1,0:T(8,128)}, u32[]{:S(2)}) copy-start(f32[12,6144]{1,0:T(8,128)} %second_ref.1) | copy-start | bytes 884740
  104.6 3.6 %collective-permute-start.1 = (bf16[15,1664]{1,0:T(8,128)(2,1)S(1)}, bf16[15,1664]{1,0:T(8,128)(2,1)S(1)}, u32[]{:S(2)}, u32[]{:S(2)}) collective-permute-start(bf16[15,1664]{1,0:T(8,128)(2,1)S(1)} %slice.26), channel_id=1, source_target_pairs={{0,64},{64,128},{128,192},{192,256},{256,320},{320,384},{384,448},... | collective-permute-start | bytes 149768
  111.4 54.7 %all-to-all-start.1 = ((bf16[16,48,1536]{2,1,0:T(8,128)(2,1)}), bf16[16,48,1536]{2,1,0:T(8,128)(2,1)S(1)}, u32[]{:S(2)}, u32[]{:S(2)}) async-start(bf16[16,48,1536]{2,1,0:T(8,128)(2,1)} %get-tuple-element.32), calls=%async_computation.1 | async-start | bytes 4718592 | tf_op jit(solution)/shard_map/all_to_all | solution.py:390
  117.6 1.7 copy-start.12
  119.2 1.1 copy-start.13

commit v9 on v8

--- a/solution.py
+++ b/solution.py
@@ -285,7 +285,8 @@
     copies = []
     for g in range(REPLICAS // GROUP):
         for k in range(GROUP):
-            chunk = gathered_ref[GROUP * g + k].astype(f32)
+            plane, line = divmod(GROUP * g + k, REPLICAS // 2)
+            chunk = gathered_ref[2 * line + plane].astype(f32)
             for s in range(SEGS):
                 rows_ref[OWN * k : OWN * (k + 1), SEG * s : SEG * (s + 1)] = chunk[
                     OWN * s : OWN * (s + 1), :
@@ -423,7 +424,7 @@
     grad_mean, first_new, second_new, sent = update(
         summed, own_power, sign_row, had, first_moment, second_moment, own_weight
     )
-    weight_new = place(to_all(sent, ("z_lo", "x")))
+    weight_new = place(to_all(sent, ("x", "z_lo")))
 
     mixed = pre_grad_product(own, other, turned_weight, slope, widen)
     halves = mixed.reshape(2, PEERS, 2, ROWS)

time: 168 us -> 168 us (level)
  no operation moved by 1% of the time
where the time goes in v9:
time: 168 us; the launch traced here: 167 us
  waiting for transfers between devices  61 us (36%)
  blocking collectives  47.4 us (28%)
  starting transfers between devices  31.7 us (19%)
  Pallas kernels  14.4 us (9%)
  local copies, waits for them, and re-layouts  10.8 us (6%)
  between operations  1.7 us (1%)
    all_to_all x2, waiting for transfers between devices, to_all(): return lax.all_to_all(copies, axes, 0, 0, tiled=True)  58.7 us
    unnamed x1, blocking collectives  47.4 us
    all_to_all x2, starting transfers between devices, to_all(): return lax.all_to_all(copies, axes, 0, 0, tiled=True)  28.1 us
    unnamed x41, local copies, waits for them, and re-layouts  9.36 us
  transfers between devices with their start and end apart: 4, of which 3 were waited for; matrix products, arithmetic and copies ran while one was open for 2% of the time, Pallas kernels for 3%

profile of v9, /device:TPU:16, one launch (start us, length us, event | category | flops | bytes accessed | tf_op | source)
XLA Modules:
  0.0 167.3 jit_solution(703217241752916489)
XLA Ops:
  0.7 2.0 %rotate_upstream.1 = bf16[32,8,1536]{2,1,0:T(8,128)(2,1)} custom-call(bf16[2,6144]{1,0:T(2,128)(2,1)} %u_hbm.1, s32[1,6144]{1,0:T(1,128)} %bitcast.17, bf16[128,128]{1,0:T(8,128)(2,1)} %constant.56.clone.had_hbm.had_ref), custom_call_target="tpu_custom_call" | custom-call | tf_op jit(solution)/shard_map/rotate_upstream/pallas_call | solution.py:112
  2.8 22.0 %all-to-all-start = ((bf16[32,8,1536]{2,1,0:T(8,128)(2,1)}), bf16[32,8,1536]{2,1,0:T(8,128)(2,1)S(1)}, u32[]{:S(2)}, u32[]{:S(2)}) async-start(bf16[32,8,1536]{2,1,0:T(8,128)(2,1)} %rotate_upstream.1), calls=%async_computation | async-start | bytes 1572864 | tf_op jit(solution)/shard_map/all_to_all | solution.py:391
  24.8 0.1 copy.36
  25.0 0.1 broadcast_select_fusion.1
  25.0 0.1 constant_dynamic-slice_fusion.2
  25.2 0.1 copy.37.shrink_ref
  25.4 0.1 copy.42
  25.5 0.1 fusion.7
  25.6 0.8 expand_hidden.1
  26.4 0.7 copy-done.9
  27.2 1.7 copy-done.7
  28.8 2.4 %rotate_weight.1.w_ref = bf16[192,6144]{1,0:T(8,128)(2,1)S(1)} custom-call(bf16[192,6144]{1,0:T(8,128)(2,1)S(1)} %copy-done.7, f32[1,6144]{1,0:T(1,128)S(1)} %bitcast.13, bf16[128,128]{1,0:T(8,128)(2,1)S(1)} %copy-done.6), custom_call_target="tpu_custom_call" | custom-call | flops 2415919104 | bytes 5242880 | tf_op jit(solution)/shard_map/rotate_weight/pallas_call | solution.py:335
  31.3 1.4 copy-done.11
  32.7 1.0 constant_dynamic-slice_fusion.1.weight_ref
  33.7 16.8 %all-to-all-done = bf16[32,8,1536]{2,1,0:T(8,128)(2,1)S(1)} async-done(((bf16[32,8,1536]{2,1,0:T(8,128)(2,1)}), bf16[32,8,1536]{2,1,0:T(8,128)(2,1)S(1)}, u32[]{:S(2)}, u32[]{:S(2)}) %all-to-all-start) | async-done | bytes 786464 | tf_op jit(solution)/shard_map/all_to_all | solution.py:391
  50.5 1.9 %collective-permute-start = (bf16[256,1536]{1,0:T(8,128)(2,1)S(1)}, bf16[256,1536]{1,0:T(8,128)(2,1)S(1)}, u32[]{:S(2)}, u32[]{:S(2)}) collective-permute-start(bf16[256,1536]{1,0:T(8,128)(2,1)S(1)} %bitcast.10), channel_id=1, source_target_pairs={{0,1},{1,0},{2,3},{3,2},{4,5},{5,4},{6,7},{7,6},{8,9},{9,8},{10,11... | collective-permute-start | bytes 2359304 | tf_op jit(solution)/shard_map/ppermute | solution.py:421
  52.4 2.3 %collective-permute-done.other_ref = bf16[256,1536]{1,0:T(8,128)(2,1)S(1)} collective-permute-done((bf16[256,1536]{1,0:T(8,128)(2,1)S(1)}, bf16[256,1536]{1,0:T(8,128)(2,1)S(1)}, u32[]{:S(2)}, u32[]{:S(2)}) %collective-permute-start) | collective-permute-done | bytes 786464 | tf_op jit(solution)/shard_map/ppermute | solution.py:421
  54.7 2.5 %encode.1 = (bf16[752,1664]{1,0:T(8,128)(2,1)}, bf16[256,1536]{1,0:T(8,128)(2,1)}) custom-call(bf16[768,512]{1,0:T(8,128)(2,1)S(1)} %get-tuple-element.22.left_ref, bf16[256,1536]{1,0:T(8,128)(2,1)S(1)} %bitcast.11, bf16[256,1536]{1,0:T(8,128)(2,1)S(1)} %collective-permute-done.other_ref, f32[768,6]{1,0:T(8,128)S(1)} %copy-done.10), custom_call_target="tpu_custom_call" | custom-call | flops 1182793728 | bytes 6291456 | tf_op jit(solution)/shard_map/encode/pallas_call | solution.py:201
  57.2 47.4 %fusion = bf16[48,1664]{1,0:T(8,128)(2,1)S(1)} fusion(bf16[752,1664]{1,0:T(8,128)(2,1)} %get-tuple-element.26), kind=kCustom, calls=%all-reduce-scatter | all-reduce-scatter fusion | flops 1277953 | bytes 2666496
  104.6 1.7 %collective-permute-start.1 = (bf16[15,1664]{1,0:T(8,128)(2,1)S(1)}, bf16[15,1664]{1,0:T(8,128)(2,1)S(1)}, u32[]{:S(2)}, u32[]{:S(2)}) collective-permute-start(bf16[15,1664]{1,0:T(8,128)(2,1)S(1)} %slice.26), channel_id=1, source_target_pairs={{0,64},{64,128},{128,192},{192,256},{256,320},{320,384},{384,448},... | collective-permute-start | bytes 149768
  106.3 1.3 dynamic-slice.4
  108.3 0.4 concatenate.4
  108.8 2.6 %update.1 = (f32[12,6144]{1,0:T(8,128)}, f32[12,6144]{1,0:T(8,128)}, f32[12,6144]{1,0:T(8,128)}, bf16[16,48,1536]{2,1,0:T(8,128)(2,1)}) custom-call(bf16[47,1664]{1,0:T(8,128)(2,1)S(1)} %constant_dynamic-slice_fusion.received_ref, f32[12,6]{1,0:T(8,128)S(1)} %multiply_exponential_fusion.power_ref, f32[1,6144]{1,0:T(1,128)S(1)} %bitcast.14, ...), custom_call_target="tpu_custom_call" | custom-call | tf_op jit(solution)/shard_map/update/pallas_call | solution.py:262
  111.4 6.2 %all-to-all-start.1 = ((bf16[16,48,1536]{2,1,0:T(8,128)(2,1)}), bf16[16,48,1536]{2,1,0:T(8,128)(2,1)S(1)}, u32[]{:S(2)}, u32[]{:S(2)}) async-start(bf16[16,48,1536]{2,1,0:T(8,128)(2,1)} %get-tuple-element.32), calls=%async_computation.1 | async-start | bytes 4718592 | tf_op jit(solution)/shard_map/all_to_all | solution.py:391
  117.6 1.7 copy-done.12
  119.2 1.1 copy-done.13
  120.4 2.4 %pre_grad.1 = bf16[128,192]{1,0:T(8,128)(2,1)S(1)} custom-call(bf16[256,1536]{1,0:T(8,128)(2,1)S(1)} %bitcast.12, bf16[256,1536]{1,0:T(8,128)(2,1)S(1)} %copy-done.13, bf16[192,6144]{1,0:T(8,128)(2,1)S(1)} %copy-done.12, f32[128,192]{1,0:T(8,128)S(1)} %get-tuple-element.50.slope_ref, bf16[128,512]{1,0:T(8,128)(2,1)S(1)} %copy-done.5), custom_call_target="tpu_custom_call" | custom-call | flops 1207959552 | bytes 6291456 | tf_op jit(solution)/shard_map/pre_grad/pallas_call | solution.py:378
  122.9 0.1 pad_maximum_fusion.1
  123.0 0.1 reshape.86
  123.0 0.7 copy.41
  123.8 42.0 %all-to-all-done.1.gathered_ref = bf16[16,48,1536]{2,1,0:T(8,128)(2,1)S(1)} async-done(((bf16[16,48,1536]{2,1,0:T(8,128)(2,1)}), bf16[16,48,1536]{2,1,0:T(8,128)(2,1)S(1)}, u32[]{:S(2)}, u32[]{:S(2)}) %all-to-all-start.1) | async-done | bytes 2359328 | tf_op jit(solution)/shard_map/all_to_all | solution.py:391
  165.7 1.6 place.1
  (44 shorter events, 0.4 us)
Async XLA Ops:
  0.6 24.9 %copy-start.3 = (bf16[768,192]{1,0:T(8,128)(2,1)S(1)}, bf16[768,192]{1,0:T(8,128)(2,1)}, u32[]{:S(2)}) copy-start(bf16[768,192]{1,0:T(8,128)(2,1)} %constant.51.clone.spread_ref) | copy-start | bytes 884740
  0.6 24.9 %copy-start.5 = (bf16[128,512]{1,0:T(8,128)(2,1)S(1)}, bf16[128,512]{1,0:T(8,128)(2,1)}, u32[]{:S(2)}) copy-start(bf16[128,512]{1,0:T(8,128)(2,1)} %constant.52.clone.widen_ref.collect_ref) | copy-start | bytes 393220
  0.7 24.9 %copy-start = (bf16[768,512]{1,0:T(8,128)(2,1)S(1)}, bf16[768,512]{1,0:T(8,128)(2,1)}, u32[]{:S(2)}) copy-start(bf16[768,512]{1,0:T(8,128)(2,1)} %constant.53.clone.same_ref) | copy-start | bytes 2359300
  0.7 24.9 %copy-start.4 = (bf16[768,36]{1,0:T(8,128)(2,1)S(1)}, bf16[768,36]{1,0:T(8,128)(2,1)}, u32[]{:S(2)}) copy-start(bf16[768,36]{1,0:T(8,128)(2,1)} %constant.54.clone.choice_ref) | copy-start | bytes 165892
  0.7 24.9 %copy-start.8 = (bf16[36,6]{1,0:T(8,128)(2,1)S(1)}, bf16[36,6]{1,0:T(8,128)(2,1)}, u32[]{:S(2)}) copy-start(bf16[36,6]{1,0:T(8,128)(2,1)} %constant.55.clone.gather_ref) | copy-start | bytes 1300
  0.7 24.1 %copy-start.16 = (s32[192,6]{0,1:T(8,128)S(1)}, s32[192,6]{0,1:T(8,128)}, u32[]{:S(2)}) copy-start(s32[192,6]{0,1:T(8,128)} %param.19) | copy-start | bytes 13828
  0.7 24.1 %copy-start.15 = (bf16[128,192]{0,1:T(8,128)(2,1)S(1)}, bf16[128,192]{0,1:T(8,128)(2,1)}, u32[]{:S(2)}) copy-start(bf16[128,192]{0,1:T(8,128)(2,1)} %param.14) | copy-start | bytes 147460
  0.7 26.4 %copy-start.14 = (s32[6144]{0:T(1024)S(1)}, s32[6144]{0:T(1024)}, u32[]{:S(2)}) copy-start(s32[6144]{0:T(1024)} %param.18) | copy-start | bytes 73732
  0.7 26.4 %copy-start.6 = (bf16[128,128]{1,0:T(8,128)(2,1)S(1)}, bf16[128,128]{1,0:T(8,128)(2,1)}, u32[]{:S(2)}) copy-start(bf16[128,128]{1,0:T(8,128)(2,1)} %constant.56.clone.had_hbm.had_ref) | copy-start | bytes 98308
  2.8 47.7 %all-to-all-start = ((bf16[32,8,1536]{2,1,0:T(8,128)(2,1)}), bf16[32,8,1536]{2,1,0:T(8,128)(2,1)S(1)}, u32[]{:S(2)}, u32[]{:S(2)}) async-start(bf16[32,8,1536]{2,1,0:T(8,128)(2,1)} %rotate_upstream.1), calls=%async_computation | async-start | bytes 1572864 | tf_op jit(solution)/shard_map/all_to_all | solution.py:391
  26.4 0.7 copy-start.9
  27.1 1.7 copy-start.7
  28.8 25.8 %copy-start.10 = (f32[768,6]{1,0:T(8,128)S(1)}, f32[768,6]{1,0:T(8,128)}, u32[]{:S(2)}) copy-start(f32[768,6]{1,0:T(8,128)} %copy-done.9) | copy-start | bytes 55300
  31.3 1.4 copy-start.11
  50.5 4.2 %collective-permute-start = (bf16[256,1536]{1,0:T(8,128)(2,1)S(1)}, bf16[256,1536]{1,0:T(8,128)(2,1)S(1)}, u32[]{:S(2)}, u32[]{:S(2)}) collective-permute-start(bf16[256,1536]{1,0:T(8,128)(2,1)S(1)} %bitcast.10), channel_id=1, source_target_pairs={{0,1},{1,0},{2,3},{3,2},{4,5},{5,4},{6,7},{7,6},{8,9},{9,8},{10,11... | collective-permute-start | bytes 2359304 | tf_op jit(solution)/shard_map/ppermute | solution.py:421
  57.2 51.6 %copy-start.1 = (f32[12,6144]{1,0:T(8,128)S(1)}, f32[12,6144]{1,0:T(8,128)}, u32[]{:S(2)}) copy-start(f32[12,6144]{1,0:T(8,128)} %first_ref.1) | copy-start | bytes 884740
  57.2 51.6 %copy-start.2 = (f32[12,6144]{1,0:T(8,128)S(1)}, f32[12,6144]{1,0:T(8,128)}, u32[]{:S(2)}) copy-start(f32[12,6144]{1,0:T(8,128)} %second_ref.1) | copy-start | bytes 884740
  104.6 3.6 %collective-permute-start.1 = (bf16[15,1664]{1,0:T(8,128)(2,1)S(1)}, bf16[15,1664]{1,0:T(8,128)(2,1)S(1)}, u32[]{:S(2)}, u32[]{:S(2)}) collective-permute-start(bf16[15,1664]{1,0:T(8,128)(2,1)S(1)} %slice.26), channel_id=1, source_target_pairs={{0,64},{64,128},{128,192},{192,256},{256,320},{320,384},{384,448},... | collective-permute-start | bytes 149768
  111.4 54.3 %all-to-all-start.1 = ((bf16[16,48,1536]{2,1,0:T(8,128)(2,1)}), bf16[16,48,1536]{2,1,0:T(8,128)(2,1)S(1)}, u32[]{:S(2)}, u32[]{:S(2)}) async-start(bf16[16,48,1536]{2,1,0:T(8,128)(2,1)} %get-tuple-element.32), calls=%async_computation.1 | async-start | bytes 4718592 | tf_op jit(solution)/shard_map/all_to_all | solution.py:391
  117.6 1.7 copy-start.12
  119.2 1.1 copy-start.13

commit v10 on v9

--- a/solution.py
+++ b/solution.py
@@ -41,6 +41,7 @@
 def tables():
     owner = np.concatenate([np.repeat(np.arange(REPLICAS), KEPT), np.arange(REPLICAS)])
     part = np.concatenate([np.tile(np.arange(KEPT), REPLICAS), np.full(REPLICAS, KEPT)])
+    owner = owner % 2 * (REPLICAS // 2) + owner // 2
     segment, own = part // OWN, part % OWN
     spread = (owner * OWN + own)[:, None] == np.arange(ROWS)[None, :]
     col = np.arange(2 * PEERS * SEGS * 2)
@@ -420,7 +421,7 @@
     )
     other = lax.ppermute(own, "core", [(0, 1), (1, 0)])
     encoded, other = encode(left, own, other, scale)
-    summed = lax.psum_scatter(encoded, ("z_lo", "x"), scatter_dimension=0, tiled=True)
+    summed = lax.psum_scatter(encoded, ("x", "z_lo"), scatter_dimension=0, tiled=True)
     grad_mean, first_new, second_new, sent = update(
         summed, own_power, sign_row, had, first_moment, second_moment, own_weight
     )

time: 168 us -> 192 us (1.14)
  blocking collectives: 47.4 us -> 61.4 us
  waiting for transfers between devices: 61 us -> 67.2 us
  starting transfers between devices: 31.7 us -> 35.6 us
    unnamed x1, blocking collectives: 47.4 us -> 61.4 us
    all_to_all x2, waiting for transfers between devices: 58.7 us -> 65 us  [to_all(): return lax.all_to_all(copies, axes, 0, 0, tiled=True)]
    all_to_all x2, starting transfers between devices: 28.1 us -> 31.4 us  [to_all(): return lax.all_to_all(copies, axes, 0, 0, tiled=True)]
where the time goes in v10:
time: 192 us; the launch traced here: 191 us
  waiting for transfers between devices  67.2 us (35%)
  blocking collectives  61.4 us (32%)
  starting transfers between devices  35.6 us (19%)
  Pallas kernels  14.4 us (8%)
  local copies, waits for them, and re-layouts  10.8 us (6%)
    all_to_all x2, waiting for transfers between devices, to_all(): return lax.all_to_all(copies, axes, 0, 0, tiled=True)  65 us
    unnamed x1, blocking collectives  61.4 us
    all_to_all x2, starting transfers between devices, to_all(): return lax.all_to_all(copies, axes, 0, 0, tiled=True)  31.4 us
    unnamed x41, local copies, waits for them, and re-layouts  9.36 us
  transfers between devices with their start and end apart: 4, of which 3 were waited for; matrix products, arithmetic and copies ran while one was open for 2% of the time, Pallas kernels for 3%

profile of v10, /device:TPU:16, one launch (start us, length us, event | category | flops | bytes accessed | tf_op | source)
XLA Modules:
  0.0 191.3 jit_solution(6215396188609761863)
XLA Ops:
  0.7 2.0 %rotate_upstream.1 = bf16[32,8,1536]{2,1,0:T(8,128)(2,1)} custom-call(bf16[2,6144]{1,0:T(2,128)(2,1)} %u_hbm.1, s32[1,6144]{1,0:T(1,128)} %bitcast.17, bf16[128,128]{1,0:T(8,128)(2,1)} %constant.56.clone.had_hbm.had_ref), custom_call_target="tpu_custom_call" | custom-call | tf_op jit(solution)/shard_map/rotate_upstream/pallas_call | solution.py:113
  2.8 22.0 %all-to-all-start = ((bf16[32,8,1536]{2,1,0:T(8,128)(2,1)}), bf16[32,8,1536]{2,1,0:T(8,128)(2,1)S(1)}, u32[]{:S(2)}, u32[]{:S(2)}) async-start(bf16[32,8,1536]{2,1,0:T(8,128)(2,1)} %rotate_upstream.1), calls=%async_computation | async-start | bytes 1572864 | tf_op jit(solution)/shard_map/all_to_all | solution.py:392
  24.8 0.1 copy.36
  25.0 0.1 broadcast_select_fusion.1
  25.0 0.1 constant_dynamic-slice_fusion.2
  25.2 0.1 copy.37.shrink_ref
  25.4 0.1 copy.42
  25.5 0.1 fusion.7
  25.6 0.8 expand_hidden.1
  26.4 0.7 copy-done.9
  27.2 1.7 copy-done.7
  28.8 2.4 %rotate_weight.1.w_ref = bf16[192,6144]{1,0:T(8,128)(2,1)S(1)} custom-call(bf16[192,6144]{1,0:T(8,128)(2,1)S(1)} %copy-done.7, f32[1,6144]{1,0:T(1,128)S(1)} %bitcast.13, bf16[128,128]{1,0:T(8,128)(2,1)S(1)} %copy-done.6), custom_call_target="tpu_custom_call" | custom-call | flops 2415919104 | bytes 5242880 | tf_op jit(solution)/shard_map/rotate_weight/pallas_call | solution.py:336
  31.3 1.4 copy-done.11
  32.7 1.0 constant_dynamic-slice_fusion.1.weight_ref
  33.7 16.8 %all-to-all-done = bf16[32,8,1536]{2,1,0:T(8,128)(2,1)S(1)} async-done(((bf16[32,8,1536]{2,1,0:T(8,128)(2,1)}), bf16[32,8,1536]{2,1,0:T(8,128)(2,1)S(1)}, u32[]{:S(2)}, u32[]{:S(2)}) %all-to-all-start) | async-done | bytes 786464 | tf_op jit(solution)/shard_map/all_to_all | solution.py:392
  50.5 1.9 collective-permute-start
  52.4 2.3 %collective-permute-done.other_ref = bf16[256,1536]{1,0:T(8,128)(2,1)S(1)} collective-permute-done((bf16[256,1536]{1,0:T(8,128)(2,1)S(1)}, bf16[256,1536]{1,0:T(8,128)(2,1)S(1)}, u32[]{:S(2)}, u32[]{:S(2)}) %collective-permute-start) | collective-permute-done | bytes 786464 | tf_op jit(solution)/shard_map/ppermute | solution.py:422
  54.7 2.5 %encode.1 = (bf16[752,1664]{1,0:T(8,128)(2,1)}, bf16[256,1536]{1,0:T(8,128)(2,1)}) custom-call(bf16[768,512]{1,0:T(8,128)(2,1)S(1)} %get-tuple-element.22.left_ref, bf16[256,1536]{1,0:T(8,128)(2,1)S(1)} %bitcast.11, bf16[256,1536]{1,0:T(8,128)(2,1)S(1)} %collective-permute-done.other_ref, f32[768,6]{1,0:T(8,128)S(1)} %copy-done.10), custom_call_target="tpu_custom_call" | custom-call | flops 1182793728 | bytes 6291456 | tf_op jit(solution)/shard_map/encode/pallas_call | solution.py:202
  57.2 61.4 %fusion = bf16[48,1664]{1,0:T(8,128)(2,1)S(1)} fusion(bf16[752,1664]{1,0:T(8,128)(2,1)} %get-tuple-element.26), kind=kCustom, calls=%all-reduce-scatter | all-reduce-scatter fusion | flops 1277953 | bytes 2666496
  118.6 2.3 %collective-permute-start.1 = (bf16[15,1664]{1,0:T(8,128)(2,1)S(1)}, bf16[15,1664]{1,0:T(8,128)(2,1)S(1)}, u32[]{:S(2)}, u32[]{:S(2)}) collective-permute-start(bf16[15,1664]{1,0:T(8,128)(2,1)S(1)} %slice.26), channel_id=1, source_target_pairs={{0,512},{512,64},{64,576},{576,128},{128,640},{640,192},{192,704},... | collective-permute-start | bytes 149768
  121.0 1.3 dynamic-slice.4
  122.9 0.4 concatenate.4
  123.4 2.6 %update.1 = (f32[12,6144]{1,0:T(8,128)}, f32[12,6144]{1,0:T(8,128)}, f32[12,6144]{1,0:T(8,128)}, bf16[16,48,1536]{2,1,0:T(8,128)(2,1)}) custom-call(bf16[47,1664]{1,0:T(8,128)(2,1)S(1)} %constant_dynamic-slice_fusion.received_ref, f32[12,6]{1,0:T(8,128)S(1)} %multiply_exponential_fusion.power_ref, f32[1,6144]{1,0:T(1,128)S(1)} %bitcast.14, ...), custom_call_target="tpu_custom_call" | custom-call | tf_op jit(solution)/shard_map/update/pallas_call | solution.py:263
  126.0 9.4 %all-to-all-start.1 = ((bf16[16,48,1536]{2,1,0:T(8,128)(2,1)}), bf16[16,48,1536]{2,1,0:T(8,128)(2,1)S(1)}, u32[]{:S(2)}, u32[]{:S(2)}) async-start(bf16[16,48,1536]{2,1,0:T(8,128)(2,1)} %get-tuple-element.32), calls=%async_computation.1 | async-start | bytes 4718592 | tf_op jit(solution)/shard_map/all_to_all | solution.py:392
  135.4 1.7 copy-done.12
  137.1 1.1 copy-done.13
  138.2 2.4 %pre_grad.1 = bf16[128,192]{1,0:T(8,128)(2,1)S(1)} custom-call(bf16[256,1536]{1,0:T(8,128)(2,1)S(1)} %bitcast.12, bf16[256,1536]{1,0:T(8,128)(2,1)S(1)} %copy-done.13, bf16[192,6144]{1,0:T(8,128)(2,1)S(1)} %copy-done.12, f32[128,192]{1,0:T(8,128)S(1)} %get-tuple-element.50.slope_ref, bf16[128,512]{1,0:T(8,128)(2,1)S(1)} %copy-done.5), custom_call_target="tpu_custom_call" | custom-call | flops 1207959552 | bytes 6291456 | tf_op jit(solution)/shard_map/pre_grad/pallas_call | solution.py:379
  140.7 0.1 pad_maximum_fusion.1
  140.8 0.1 reshape.86
  140.9 0.7 copy.41
  141.6 48.2 %all-to-all-done.1.gathered_ref = bf16[16,48,1536]{2,1,0:T(8,128)(2,1)S(1)} async-done(((bf16[16,48,1536]{2,1,0:T(8,128)(2,1)}), bf16[16,48,1536]{2,1,0:T(8,128)(2,1)S(1)}, u32[]{:S(2)}, u32[]{:S(2)}) %all-to-all-start.1) | async-done | bytes 2359328 | tf_op jit(solution)/shard_map/all_to_all | solution.py:392
  189.8 1.6 place.1
  (44 shorter events, 0.4 us)
Async XLA Ops:
  0.6 24.9 %copy-start.3 = (bf16[768,192]{1,0:T(8,128)(2,1)S(1)}, bf16[768,192]{1,0:T(8,128)(2,1)}, u32[]{:S(2)}) copy-start(bf16[768,192]{1,0:T(8,128)(2,1)} %constant.51.clone.spread_ref) | copy-start | bytes 884740
  0.6 24.9 %copy-start.5 = (bf16[128,512]{1,0:T(8,128)(2,1)S(1)}, bf16[128,512]{1,0:T(8,128)(2,1)}, u32[]{:S(2)}) copy-start(bf16[128,512]{1,0:T(8,128)(2,1)} %constant.52.clone.widen_ref.collect_ref) | copy-start | bytes 393220
  0.7 24.9 %copy-start = (bf16[768,512]{1,0:T(8,128)(2,1)S(1)}, bf16[768,512]{1,0:T(8,128)(2,1)}, u32[]{:S(2)}) copy-start(bf16[768,512]{1,0:T(8,128)(2,1)} %constant.53.clone.same_ref) | copy-start | bytes 2359300
  0.7 24.9 %copy-start.4 = (bf16[768,36]{1,0:T(8,128)(2,1)S(1)}, bf16[768,36]{1,0:T(8,128)(2,1)}, u32[]{:S(2)}) copy-start(bf16[768,36]{1,0:T(8,128)(2,1)} %constant.54.clone.choice_ref) | copy-start | bytes 165892
  0.7 24.9 %copy-start.8 = (bf16[36,6]{1,0:T(8,128)(2,1)S(1)}, bf16[36,6]{1,0:T(8,128)(2,1)}, u32[]{:S(2)}) copy-start(bf16[36,6]{1,0:T(8,128)(2,1)} %constant.55.clone.gather_ref) | copy-start | bytes 1300
  0.7 24.1 %copy-start.16 = (s32[192,6]{0,1:T(8,128)S(1)}, s32[192,6]{0,1:T(8,128)}, u32[]{:S(2)}) copy-start(s32[192,6]{0,1:T(8,128)} %param.19) | copy-start | bytes 13828
  0.7 24.1 %copy-start.15 = (bf16[128,192]{0,1:T(8,128)(2,1)S(1)}, bf16[128,192]{0,1:T(8,128)(2,1)}, u32[]{:S(2)}) copy-start(bf16[128,192]{0,1:T(8,128)(2,1)} %param.14) | copy-start | bytes 147460
  0.7 26.4 %copy-start.14 = (s32[6144]{0:T(1024)S(1)}, s32[6144]{0:T(1024)}, u32[]{:S(2)}) copy-start(s32[6144]{0:T(1024)} %param.18) | copy-start | bytes 73732
  0.7 26.4 %copy-start.6 = (bf16[128,128]{1,0:T(8,128)(2,1)S(1)}, bf16[128,128]{1,0:T(8,128)(2,1)}, u32[]{:S(2)}) copy-start(bf16[128,128]{1,0:T(8,128)(2,1)} %constant.56.clone.had_hbm.had_ref) | copy-start | bytes 98308
  2.8 47.7 %all-to-all-start = ((bf16[32,8,1536]{2,1,0:T(8,128)(2,1)}), bf16[32,8,1536]{2,1,0:T(8,128)(2,1)S(1)}, u32[]{:S(2)}, u32[]{:S(2)}) async-start(bf16[32,8,1536]{2,1,0:T(8,128)(2,1)} %rotate_upstream.1), calls=%async_computation | async-start | bytes 1572864 | tf_op jit(solution)/shard_map/all_to_all | solution.py:392
  26.4 0.7 copy-start.9
  27.1 1.7 copy-start.7
  28.8 25.8 %copy-start.10 = (f32[768,6]{1,0:T(8,128)S(1)}, f32[768,6]{1,0:T(8,128)}, u32[]{:S(2)}) copy-start(f32[768,6]{1,0:T(8,128)} %copy-done.9) | copy-start | bytes 55300
  31.3 1.4 copy-start.11
  50.5 4.2 %collective-permute-start = (bf16[256,1536]{1,0:T(8,128)(2,1)S(1)}, bf16[256,1536]{1,0:T(8,128)(2,1)S(1)}, u32[]{:S(2)}, u32[]{:S(2)}) collective-permute-start(bf16[256,1536]{1,0:T(8,128)(2,1)S(1)} %bitcast.10), channel_id=1, source_target_pairs={{0,1},{1,0},{2,3},{3,2},{4,5},{5,4},{6,7},{7,6},{8,9},{9,8},{10,11... | collective-permute-start | bytes 2359304 | tf_op jit(solution)/shard_map/ppermute | solution.py:422
  57.2 66.2 %copy-start.1 = (f32[12,6144]{1,0:T(8,128)S(1)}, f32[12,6144]{1,0:T(8,128)}, u32[]{:S(2)}) copy-start(f32[12,6144]{1,0:T(8,128)} %first_ref.1) | copy-start | bytes 884740
  57.2 66.2 %copy-start.2 = (f32[12,6144]{1,0:T(8,128)S(1)}, f32[12,6144]{1,0:T(8,128)}, u32[]{:S(2)}) copy-start(f32[12,6144]{1,0:T(8,128)} %second_ref.1) | copy-start | bytes 884740
  118.6 4.2 %collective-permute-start.1 = (bf16[15,1664]{1,0:T(8,128)(2,1)S(1)}, bf16[15,1664]{1,0:T(8,128)(2,1)S(1)}, u32[]{:S(2)}, u32[]{:S(2)}) collective-permute-start(bf16[15,1664]{1,0:T(8,128)(2,1)S(1)} %slice.26), channel_id=1, source_target_pairs={{0,512},{512,64},{64,576},{576,128},{128,640},{640,192},{192,704},... | collective-permute-start | bytes 149768
  126.0 63.8 %all-to-all-start.1 = ((bf16[16,48,1536]{2,1,0:T(8,128)(2,1)}), bf16[16,48,1536]{2,1,0:T(8,128)(2,1)S(1)}, u32[]{:S(2)}, u32[]{:S(2)}) async-start(bf16[16,48,1536]{2,1,0:T(8,128)(2,1)} %get-tuple-element.32), calls=%async_computation.1 | async-start | bytes 4718592 | tf_op jit(solution)/shard_map/all_to_all | solution.py:392
  135.4 1.7 copy-start.12
  137.1 1.1 copy-start.13

commit v11 on v9

--- a/solution.py
+++ b/solution.py
@@ -41,6 +41,7 @@
 def tables():
     owner = np.concatenate([np.repeat(np.arange(REPLICAS), KEPT), np.arange(REPLICAS)])
     part = np.concatenate([np.tile(np.arange(KEPT), REPLICAS), np.full(REPLICAS, KEPT)])
+    owner = np.where(owner < REPLICAS // 2, owner, 3 * REPLICAS // 2 - 1 - owner)
     segment, own = part // OWN, part % OWN
     spread = (owner * OWN + own)[:, None] == np.arange(ROWS)[None, :]
     col = np.arange(2 * PEERS * SEGS * 2)
@@ -420,7 +421,15 @@
     )
     other = lax.ppermute(own, "core", [(0, 1), (1, 0)])
     encoded, other = encode(left, own, other, scale)
-    summed = lax.psum_scatter(encoded, ("z_lo", "x"), scatter_dimension=0, tiled=True)
+    half = REPLICAS // 2
+    ring = [*range(half), *range(REPLICAS - 1, half - 1, -1)]
+    summed = lax.psum_scatter(
+        encoded,
+        ("z_lo", "x"),
+        scatter_dimension=0,
+        axis_index_groups=[ring],
+        tiled=True,
+    )
     grad_mean, first_new, second_new, sent = update(
         summed, own_power, sign_row, had, first_moment, second_moment, own_weight
     )

time: 168 us -> 166 us (0.988)
  blocking collectives: 47.4 us -> 41.3 us
  starting transfers between devices: 31.7 us -> 35.4 us
    unnamed x1, blocking collectives: 47.4 us -> 41.3 us
    all_to_all x2, starting transfers between devices: 28.1 us -> 30.5 us  [to_all(): return lax.all_to_all(copies, axes, 0, 0, tiled=True)]
where the time goes in v11:
time: 166 us; the launch traced here: 165 us
  waiting for transfers between devices  61.7 us (37%)
  blocking collectives  41.3 us (25%)
  starting transfers between devices  35.4 us (21%)
  Pallas kernels  14.4 us (9%)
  local copies, waits for them, and re-layouts  10.8 us (7%)
  between operations  1.7 us (1%)
    all_to_all x2, waiting for transfers between devices, to_all(): return lax.all_to_all(copies, axes, 0, 0, tiled=True)  59.4 us
    unnamed x1, blocking collectives  41.3 us
    all_to_all x2, starting transfers between devices, to_all(): return lax.all_to_all(copies, axes, 0, 0, tiled=True)  30.5 us
    unnamed x41, local copies, waits for them, and re-layouts  9.36 us
  transfers between devices with their start and end apart: 4, of which 3 were waited for; matrix products, arithmetic and copies ran while one was open for 2% of the time, Pallas kernels for 3%

profile of v11, /device:TPU:16, one launch (start us, length us, event | category | flops | bytes accessed | tf_op | source)
XLA Modules:
  0.0 165.5 jit_solution(12548851356747496729)
XLA Ops:
  0.7 2.0 %rotate_upstream.1 = bf16[32,8,1536]{2,1,0:T(8,128)(2,1)} custom-call(bf16[2,6144]{1,0:T(2,128)(2,1)} %u_hbm.1, s32[1,6144]{1,0:T(1,128)} %bitcast.17, bf16[128,128]{1,0:T(8,128)(2,1)} %constant.56.clone.had_hbm.had_ref), custom_call_target="tpu_custom_call" | custom-call | tf_op jit(solution)/shard_map/rotate_upstream/pallas_call | solution.py:113
  2.8 22.0 %all-to-all-start = ((bf16[32,8,1536]{2,1,0:T(8,128)(2,1)}), bf16[32,8,1536]{2,1,0:T(8,128)(2,1)S(1)}, u32[]{:S(2)}, u32[]{:S(2)}) async-start(bf16[32,8,1536]{2,1,0:T(8,128)(2,1)} %rotate_upstream.1), calls=%async_computation | async-start | bytes 1572864 | tf_op jit(solution)/shard_map/all_to_all | solution.py:392
  24.8 0.1 copy.36
  25.0 0.1 broadcast_select_fusion.1
  25.0 0.1 constant_dynamic-slice_fusion.2
  25.2 0.1 copy.37.shrink_ref
  25.4 0.1 copy.42
  25.5 0.1 fusion.7
  25.6 0.8 expand_hidden.1
  26.4 0.7 copy-done.9
  27.2 1.7 %copy-done.7 = bf16[192,6144]{1,0:T(8,128)(2,1)S(1)} copy-done((bf16[192,6144]{1,0:T(8,128)(2,1)S(1)}, bf16[192,6144]{1,0:T(8,128)(2,1)}, u32[]{:S(2)}) %copy-start.7) | copy-done | bytes 2359320
  28.8 2.4 %rotate_weight.1.w_ref = bf16[192,6144]{1,0:T(8,128)(2,1)S(1)} custom-call(bf16[192,6144]{1,0:T(8,128)(2,1)S(1)} %copy-done.7, f32[1,6144]{1,0:T(1,128)S(1)} %bitcast.13, bf16[128,128]{1,0:T(8,128)(2,1)S(1)} %copy-done.6), custom_call_target="tpu_custom_call" | custom-call | flops 2415919104 | bytes 5242880 | tf_op jit(solution)/shard_map/rotate_weight/pallas_call | solution.py:336
  31.3 1.4 copy-done.11
  32.7 1.0 constant_dynamic-slice_fusion.1.weight_ref
  33.7 16.8 %all-to-all-done = bf16[32,8,1536]{2,1,0:T(8,128)(2,1)S(1)} async-done(((bf16[32,8,1536]{2,1,0:T(8,128)(2,1)}), bf16[32,8,1536]{2,1,0:T(8,128)(2,1)S(1)}, u32[]{:S(2)}, u32[]{:S(2)}) %all-to-all-start) | async-done | bytes 786464 | tf_op jit(solution)/shard_map/all_to_all | solution.py:392
  50.5 1.9 %collective-permute-start = (bf16[256,1536]{1,0:T(8,128)(2,1)S(1)}, bf16[256,1536]{1,0:T(8,128)(2,1)S(1)}, u32[]{:S(2)}, u32[]{:S(2)}) collective-permute-start(bf16[256,1536]{1,0:T(8,128)(2,1)S(1)} %bitcast.10), channel_id=1, source_target_pairs={{0,1},{1,0},{2,3},{3,2},{4,5},{5,4},{6,7},{7,6},{8,9},{9,8},{10,11... | collective-permute-start | bytes 2359304 | tf_op jit(solution)/shard_map/ppermute | solution.py:422
  52.4 2.3 %collective-permute-done.other_ref = bf16[256,1536]{1,0:T(8,128)(2,1)S(1)} collective-permute-done((bf16[256,1536]{1,0:T(8,128)(2,1)S(1)}, bf16[256,1536]{1,0:T(8,128)(2,1)S(1)}, u32[]{:S(2)}, u32[]{:S(2)}) %collective-permute-start) | collective-permute-done | bytes 786464 | tf_op jit(solution)/shard_map/ppermute | solution.py:422
  54.7 2.5 %encode.1 = (bf16[752,1664]{1,0:T(8,128)(2,1)}, bf16[256,1536]{1,0:T(8,128)(2,1)}) custom-call(bf16[768,512]{1,0:T(8,128)(2,1)S(1)} %get-tuple-element.22.left_ref, bf16[256,1536]{1,0:T(8,128)(2,1)S(1)} %bitcast.11, bf16[256,1536]{1,0:T(8,128)(2,1)S(1)} %collective-permute-done.other_ref, f32[768,6]{1,0:T(8,128)S(1)} %copy-done.10), custom_call_target="tpu_custom_call" | custom-call | flops 1182793728 | bytes 6291456 | tf_op jit(solution)/shard_map/encode/pallas_call | solution.py:202
  57.2 41.3 %fusion = bf16[48,1664]{1,0:T(8,128)(2,1)S(1)} fusion(bf16[752,1664]{1,0:T(8,128)(2,1)} %get-tuple-element.26), kind=kCustom, calls=%all-reduce-scatter | all-reduce-scatter fusion | flops 1277953 | bytes 2666496
  98.5 3.0 %collective-permute-start.1 = (bf16[15,1664]{1,0:T(8,128)(2,1)S(1)}, bf16[15,1664]{1,0:T(8,128)(2,1)S(1)}, u32[]{:S(2)}, u32[]{:S(2)}) collective-permute-start(bf16[15,1664]{1,0:T(8,128)(2,1)S(1)} %slice.26), channel_id=1, source_target_pairs={{0,64},{64,128},{128,192},{192,256},{256,320},{320,384},{384,448},... | collective-permute-start | bytes 149768
  101.5 1.3 dynamic-slice.4
  103.5 0.4 concatenate.4
  104.0 2.6 %update.1 = (f32[12,6144]{1,0:T(8,128)}, f32[12,6144]{1,0:T(8,128)}, f32[12,6144]{1,0:T(8,128)}, bf16[16,48,1536]{2,1,0:T(8,128)(2,1)}) custom-call(bf16[47,1664]{1,0:T(8,128)(2,1)S(1)} %constant_dynamic-slice_fusion.received_ref, f32[12,6]{1,0:T(8,128)S(1)} %multiply_exponential_fusion.power_ref, f32[1,6144]{1,0:T(1,128)S(1)} %bitcast.14, ...), custom_call_target="tpu_custom_call" | custom-call | tf_op jit(solution)/shard_map/update/pallas_call | solution.py:263
  106.6 8.5 %all-to-all-start.1 = ((bf16[16,48,1536]{2,1,0:T(8,128)(2,1)}), bf16[16,48,1536]{2,1,0:T(8,128)(2,1)S(1)}, u32[]{:S(2)}, u32[]{:S(2)}) async-start(bf16[16,48,1536]{2,1,0:T(8,128)(2,1)} %get-tuple-element.32), calls=%async_computation.1 | async-start | bytes 4718592 | tf_op jit(solution)/shard_map/all_to_all | solution.py:392
  115.1 1.7 %copy-done.12 = bf16[192,6144]{1,0:T(8,128)(2,1)S(1)} copy-done((bf16[192,6144]{1,0:T(8,128)(2,1)S(1)}, bf16[192,6144]{1,0:T(8,128)(2,1)}, u32[]{:S(2)}) %copy-start.12) | copy-done | bytes 2359320
  116.7 1.1 copy-done.13
  117.9 2.4 %pre_grad.1 = bf16[128,192]{1,0:T(8,128)(2,1)S(1)} custom-call(bf16[256,1536]{1,0:T(8,128)(2,1)S(1)} %bitcast.12, bf16[256,1536]{1,0:T(8,128)(2,1)S(1)} %copy-done.13, bf16[192,6144]{1,0:T(8,128)(2,1)S(1)} %copy-done.12, f32[128,192]{1,0:T(8,128)S(1)} %get-tuple-element.50.slope_ref, bf16[128,512]{1,0:T(8,128)(2,1)S(1)} %copy-done.5), custom_call_target="tpu_custom_call" | custom-call | flops 1207959552 | bytes 6291456 | tf_op jit(solution)/shard_map/pre_grad/pallas_call | solution.py:379
  120.3 0.1 pad_maximum_fusion.1
  120.4 0.1 reshape.86
  120.5 0.7 copy.41
  121.2 42.6 %all-to-all-done.1.gathered_ref = bf16[16,48,1536]{2,1,0:T(8,128)(2,1)S(1)} async-done(((bf16[16,48,1536]{2,1,0:T(8,128)(2,1)}), bf16[16,48,1536]{2,1,0:T(8,128)(2,1)S(1)}, u32[]{:S(2)}, u32[]{:S(2)}) %all-to-all-start.1) | async-done | bytes 2359328 | tf_op jit(solution)/shard_map/all_to_all | solution.py:392
  163.9 1.6 place.1
  (44 shorter events, 0.4 us)
Async XLA Ops:
  0.6 24.9 %copy-start.3 = (bf16[768,192]{1,0:T(8,128)(2,1)S(1)}, bf16[768,192]{1,0:T(8,128)(2,1)}, u32[]{:S(2)}) copy-start(bf16[768,192]{1,0:T(8,128)(2,1)} %constant.51.clone.spread_ref) | copy-start | bytes 884740
  0.6 24.9 %copy-start.5 = (bf16[128,512]{1,0:T(8,128)(2,1)S(1)}, bf16[128,512]{1,0:T(8,128)(2,1)}, u32[]{:S(2)}) copy-start(bf16[128,512]{1,0:T(8,128)(2,1)} %constant.52.clone.widen_ref.collect_ref) | copy-start | bytes 393220
  0.7 24.9 %copy-start = (bf16[768,512]{1,0:T(8,128)(2,1)S(1)}, bf16[768,512]{1,0:T(8,128)(2,1)}, u32[]{:S(2)}) copy-start(bf16[768,512]{1,0:T(8,128)(2,1)} %constant.53.clone.same_ref) | copy-start | bytes 2359300
  0.7 24.9 %copy-start.4 = (bf16[768,36]{1,0:T(8,128)(2,1)S(1)}, bf16[768,36]{1,0:T(8,128)(2,1)}, u32[]{:S(2)}) copy-start(bf16[768,36]{1,0:T(8,128)(2,1)} %constant.54.clone.choice_ref) | copy-start | bytes 165892
  0.7 24.9 %copy-start.8 = (bf16[36,6]{1,0:T(8,128)(2,1)S(1)}, bf16[36,6]{1,0:T(8,128)(2,1)}, u32[]{:S(2)}) copy-start(bf16[36,6]{1,0:T(8,128)(2,1)} %constant.55.clone.gather_ref) | copy-start | bytes 1300
  0.7 24.1 %copy-start.16 = (s32[192,6]{0,1:T(8,128)S(1)}, s32[192,6]{0,1:T(8,128)}, u32[]{:S(2)}) copy-start(s32[192,6]{0,1:T(8,128)} %param.19) | copy-start | bytes 13828
  0.7 24.1 %copy-start.15 = (bf16[128,192]{0,1:T(8,128)(2,1)S(1)}, bf16[128,192]{0,1:T(8,128)(2,1)}, u32[]{:S(2)}) copy-start(bf16[128,192]{0,1:T(8,128)(2,1)} %param.14) | copy-start | bytes 147460
  0.7 26.4 %copy-start.14 = (s32[6144]{0:T(1024)S(1)}, s32[6144]{0:T(1024)}, u32[]{:S(2)}) copy-start(s32[6144]{0:T(1024)} %param.18) | copy-start | bytes 73732
  0.7 26.4 %copy-start.6 = (bf16[128,128]{1,0:T(8,128)(2,1)S(1)}, bf16[128,128]{1,0:T(8,128)(2,1)}, u32[]{:S(2)}) copy-start(bf16[128,128]{1,0:T(8,128)(2,1)} %constant.56.clone.had_hbm.had_ref) | copy-start | bytes 98308
  2.8 47.7 %all-to-all-start = ((bf16[32,8,1536]{2,1,0:T(8,128)(2,1)}), bf16[32,8,1536]{2,1,0:T(8,128)(2,1)S(1)}, u32[]{:S(2)}, u32[]{:S(2)}) async-start(bf16[32,8,1536]{2,1,0:T(8,128)(2,1)} %rotate_upstream.1), calls=%async_computation | async-start | bytes 1572864 | tf_op jit(solution)/shard_map/all_to_all | solution.py:392
  26.4 0.7 copy-start.9
  27.1 1.7 %copy-start.7 = (bf16[192,6144]{1,0:T(8,128)(2,1)S(1)}, bf16[192,6144]{1,0:T(8,128)(2,1)}, u32[]{:S(2)}) copy-start(bf16[192,6144]{1,0:T(8,128)(2,1)} %w_ref.1) | copy-start | bytes 7077892
  28.8 25.8 %copy-start.10 = (f32[768,6]{1,0:T(8,128)S(1)}, f32[768,6]{1,0:T(8,128)}, u32[]{:S(2)}) copy-start(f32[768,6]{1,0:T(8,128)} %copy-done.9) | copy-start | bytes 55300
  31.3 1.4 copy-start.11
  50.5 4.2 %collective-permute-start = (bf16[256,1536]{1,0:T(8,128)(2,1)S(1)}, bf16[256,1536]{1,0:T(8,128)(2,1)S(1)}, u32[]{:S(2)}, u32[]{:S(2)}) collective-permute-start(bf16[256,1536]{1,0:T(8,128)(2,1)S(1)} %bitcast.10), channel_id=1, source_target_pairs={{0,1},{1,0},{2,3},{3,2},{4,5},{5,4},{6,7},{7,6},{8,9},{9,8},{10,11... | collective-permute-start | bytes 2359304 | tf_op jit(solution)/shard_map/ppermute | solution.py:422
  57.2 46.7 %copy-start.1 = (f32[12,6144]{1,0:T(8,128)S(1)}, f32[12,6144]{1,0:T(8,128)}, u32[]{:S(2)}) copy-start(f32[12,6144]{1,0:T(8,128)} %first_ref.1) | copy-start | bytes 884740
  57.2 46.7 %copy-start.2 = (f32[12,6144]{1,0:T(8,128)S(1)}, f32[12,6144]{1,0:T(8,128)}, u32[]{:S(2)}) copy-start(f32[12,6144]{1,0:T(8,128)} %second_ref.1) | copy-start | bytes 884740
  98.5 4.9 %collective-permute-start.1 = (bf16[15,1664]{1,0:T(8,128)(2,1)S(1)}, bf16[15,1664]{1,0:T(8,128)(2,1)S(1)}, u32[]{:S(2)}, u32[]{:S(2)}) collective-permute-start(bf16[15,1664]{1,0:T(8,128)(2,1)S(1)} %slice.26), channel_id=1, source_target_pairs={{0,64},{64,128},{128,192},{192,256},{256,320},{320,384},{384,448},... | collective-permute-start | bytes 149768
  106.6 57.3 %all-to-all-start.1 = ((bf16[16,48,1536]{2,1,0:T(8,128)(2,1)}), bf16[16,48,1536]{2,1,0:T(8,128)(2,1)S(1)}, u32[]{:S(2)}, u32[]{:S(2)}) async-start(bf16[16,48,1536]{2,1,0:T(8,128)(2,1)} %get-tuple-element.32), calls=%async_computation.1 | async-start | bytes 4718592 | tf_op jit(solution)/shard_map/all_to_all | solution.py:392
  115.0 1.7 %copy-start.12 = (bf16[192,6144]{1,0:T(8,128)(2,1)S(1)}, bf16[192,6144]{1,0:T(8,128)(2,1)}, u32[]{:S(2)}) copy-start(bf16[192,6144]{1,0:T(8,128)(2,1)} %copy-done.11) | copy-start | bytes 7077892
  116.7 1.1 copy-start.13
